TPU v7x, 1024 devices: a whole 4x8x16 slice. The times are simulated.
1024 devices in a mesh: dp: 32 (over x_lo, z), mx: 4 (over x_hi, core), my: 8 (over y).
Axes of the slice: x: 4 (x_hi: 2, x_lo: 2; x = x_hi * 2 + x_lo), y: 8, z: 16, core: 2. Of those that a mesh axis runs over, the one named last changes fastest.
Arguments:
- tokens_in: bfloat16 [8192, 6144], P('dp', 'mx'), as said below
- norm_gain: float32 [6144], P('mx'), may hold values from 0.1 to 1.9
- in_weight: bfloat16 [6144, 12288], P('mx', 'my'), as said below
- cotangent: bfloat16 [8192, 12288], P('dp', 'my'), may hold values from -6 to 6
Outputs:
- grad_weight: bfloat16 [4, 32, 48, 12288], P('mx', 'dp', None, 'my')
- grad_tokens: bfloat16 [8192, 6144], P(('dp', 'my'), 'mx')
Inputs may be any that keep to these rules, and one draw needn't show every extreme that they name: `tokens_in`: Real-valued activations; no structure is promised. `in_weight`: Real-valued weights; no structure is promised.
All inputs are finite; a program needn't handle non-finite values.
Results may differ from a plain program's by a relative error of at most 0.034.
Values may be sent and summed in bfloat16 or wider, within the bound.
No kernel may reach another device: no remote copies, remote signals or barrier semaphores. Data moves between devices by JAX's collectives and lax.ppermute only.
A program may use at most 32 MiB of HBM per device.

v0:
```python
import math

import jax
import jax.numpy as jnp
from jax import lax
from jax.sharding import PartitionSpec as P

D = 6144


epsilon = 1e-06


def gelu_slope(pre):
    cdf = 0.5 * (1.0 + jax.scipy.special.erf(pre * (1.0 / math.sqrt(2.0))))
    return cdf + pre * jnp.exp(-0.5 * pre * pre) * (1.0 / math.sqrt(2.0 * math.pi))


def body(tokens_in, norm_gain, in_weight, cotangent):
    tok_rows = tokens_in.shape[0]
    local_width = tokens_in.shape[1]
    local_hidden = in_weight.shape[1]
    values = tokens_in.astype(jnp.float32)
    sum_one, sum_two = lax.psum((jnp.sum(values, axis=1), jnp.sum(values * values, axis=1)), "mx")
    row_mean = sum_one / D
    inv_std = lax.rsqrt(sum_two / D - row_mean * row_mean + epsilon)
    centred = (values - row_mean[:, None]) * inv_std[:, None]
    normed = (centred * norm_gain[None, :]).astype(jnp.bfloat16)
    partial_value = jnp.dot(normed, in_weight, preferred_element_type=jnp.float32)
    pre = lax.psum(partial_value.astype(jnp.bfloat16), "mx").astype(jnp.float32)
    dpre = (cotangent.astype(jnp.float32) * gelu_slope(pre)).astype(jnp.bfloat16)
    grad_scale = 1.0 / math.sqrt(lax.axis_size("dp") * tok_rows)
    block_rows = local_width // lax.axis_size("dp")
    term = lax.dot_general(
        normed, dpre, (((0,), (0,)), ((), ())), preferred_element_type=jnp.float32
    )
    summed = lax.psum_scatter(
        (term * grad_scale).astype(jnp.bfloat16), "dp", scatter_dimension=0, tiled=True
    )
    grad_weight = summed.reshape(1, 1, block_rows, local_hidden)
    back_partial = lax.dot_general(
        dpre, in_weight, (((1,), (1,)), ((), ())), preferred_element_type=jnp.float32
    )
    dnormed = lax.psum_scatter(
        back_partial.astype(jnp.bfloat16), "my", scatter_dimension=0, tiled=True
    ).astype(jnp.float32)
    own_rows = tok_rows // lax.axis_size("my")
    first_row = lax.axis_index("my") * own_rows
    centred_rows = lax.dynamic_slice_in_dim(centred, first_row, own_rows, 0)
    inv_rows = lax.dynamic_slice_in_dim(inv_std, first_row, own_rows, 0)
    dcentred = dnormed * norm_gain[None, :]
    total_a, total_b = lax.psum(
        (jnp.sum(dcentred, axis=1), jnp.sum(dcentred * centred_rows, axis=1)), "mx"
    )
    mean_a = total_a / D
    mean_b = total_b / D
    grad_tokens = inv_rows[:, None] * (dcentred - mean_a[:, None] - centred_rows * mean_b[:, None])
    return (grad_weight, grad_tokens.astype(jnp.bfloat16))


def solution(mesh):
    return jax.shard_map(
        body,
        mesh=mesh,
        in_specs=(P("dp", "mx"), P("mx"), P("mx", "my"), P("dp", "my")),
        out_specs=(P("mx", "dp", None, "my"), P(("dp", "my"), "mx")),
        check_vma=False,
    )
```

profile of v0, /device:TPU:40, one launch (start us, length us, event | category | flops | bytes accessed | tf_op | source)
XLA Modules:
  0.0 305.3 jit_solution(13487037562844803670)
XLA Ops:
  7.2 0.0 all-reduce.4.cloned.1.call-start
  7.2 1.5 convert_reduce_fusion
  8.7 9.9 %all-reduce.1 = (f32[256]{0:T(256)S(1)}, f32[256]{0:T(256)S(1)}) all-reduce(f32[256]{0:T(256)S(1)} %get-tuple-element.3, f32[256]{0:T(256)S(1)} %get-tuple-element.2), channel_id=1, replica_groups=mesh['dp'=32,'mx'=4,'my'=8] {'mx'}, use_global_device_ids=true, to_apply=%region_3.0 | all-reduce | flops 512 | bytes 4096 | tf_op jit(solution)/shard_map/psum | solution.py:24
  18.6 0.0 copy-start.2
  18.6 5.0 %convolution_convert_fusion.1 = bf16[256,1536]{1,0:T(8,128)(2,1)} fusion(bf16[1536,1536]{1,0:T(8,128)(2,1)} %param.6, f32[1536]{0:T(1024)} %param.5, bf16[256,1536]{1,0:T(8,128)(2,1)} %param.4, f32[256]{0:T(256)S(1)} %get-tuple-element.11, f32[256]{0:T(256)S(1)} %get-tuple-element.10), kind=kOutput, calls=%fused_computation.7 | convolution fusion | flops 1210318848 | bytes 6299648 | tf_op jit(solution)/shard_map/dot_general | solution.py:29
  23.7 0.0 all-reduce.4.cloned.1.call-update
  23.7 0.0 copy-start
  23.7 0.0 copy-start.1
  23.7 0.0 reduce-scatter.5.cloned.1.call-start
  23.8 70.9 %all-reduce.4.cloned.1.call-done = bf16[256,1536]{1,0:T(8,128)(2,1)} async-done(((bf16[256,1536]{1,0:T(8,128)(2,1)}), bf16[256,1536]{1,0:T(8,128)(2,1)}) %all-reduce.4.cloned.1.call-update) | async-done | bytes 786448 | tf_op jit(solution)/shard_map/psum | solution.py:30
  94.6 0.0 copy-done.2
  94.6 0.0 copy-start.3
  94.6 5.3 %convolution_convert_fusion = bf16[256,1536]{1,0:T(8,128)(2,1)} fusion(bf16[1536,1536]{1,0:T(8,128)(2,1)} %param.6, bf16[256,1536]{1,0:T(8,128)(2,1)} %all-reduce.4.cloned.1.call-done, bf16[256,1536]{1,0:T(8,128)(2,1)S(1)} %copy-done.2), kind=kOutput, calls=%fused_computation.6 | convolution fusion | flops 1213071360 | bytes 7077888 | tf_op jit(solution)/shard_map/dot_general | solution.py:41
  99.9 0.0 reduce-scatter.5.cloned.1.call-update
  99.9 0.0 reduce-scatter.3.cloned.1.call-start
  100.0 0.0 copy-done
  100.0 0.0 copy-done.1
  100.0 0.0 copy-done.3
  100.0 4.3 %fusion = bf16[1536,1536]{1,0:T(8,128)(2,1)} fusion(f32[1536]{0:T(1024)S(1)} %copy-done.1, bf16[256,1536]{1,0:T(8,128)(2,1)S(1)} %copy-done, f32[256]{0:T(256)S(1)} %get-tuple-element.11, f32[256]{0:T(256)S(1)} %get-tuple-element.10, bf16[256,1536]{1,0:T(8,128)(2,1)S(1)} %copy-done.3, bf16[256,1536]{1,0:T(8,128)(2,1)S(1)} %copy-done.2), kind=kOutput, calls=%fused_computation.1 | convolution fusion | flops 1219362816 | bytes 7086080 | tf_op jit(solution)/shard_map/dot_general | solution.py:34
  104.3 0.0 reduce-scatter.3.cloned.1.call-update
  104.3 0.1 dynamic_slice.6
  104.4 0.3 fusion.1
  104.8 39.1 %reduce-scatter.5.cloned.1.call-done = bf16[32,1536]{1,0:T(8,128)(2,1)} async-done(((bf16[256,1536]{1,0:T(8,128)(2,1)}), bf16[32,1536]{1,0:T(8,128)(2,1)}) %reduce-scatter.5.cloned.1.call-update) | async-done | bytes 98320 | tf_op jit(solution)/shard_map/reduce_scatter | solution.py:44
  143.9 1.0 fusion.11
  144.9 7.2 %all-reduce = (f32[32]{0:T(128)S(1)}, f32[32]{0:T(128)S(1)}) all-reduce(f32[32]{0:T(128)S(1)} %get-tuple-element.5, f32[32]{0:T(128)S(1)} %get-tuple-element.4), channel_id=1, replica_groups=mesh['dp'=32,'mx'=4,'my'=8] {'mx'}, use_global_device_ids=true, to_apply=%region_10.0 | all-reduce | flops 64 | bytes 512 | tf_op jit(solution)/shard_map/psum | solution.py:52
  152.1 1.6 multiply_convert_fusion.3
  153.7 145.1 %reduce-scatter.3.cloned.1.call-done = bf16[48,1536]{1,0:T(8,128)(2,1)} async-done(((bf16[1536,1536]{1,0:T(8,128)(2,1)}), bf16[48,1536]{1,0:T(8,128)(2,1)}) %reduce-scatter.3.cloned.1.call-update) | async-done | bytes 147472 | tf_op jit(solution)/shard_map/reduce_scatter | solution.py:37
  (2 shorter events, 0.0 us)
Async XLA Ops:
  7.2 87.5 %all-reduce.4.cloned.1.call-start = ((), (), s32[]{:S(2)}) async-start(), calls=%async_computation.2 | async-start | bytes 1572864 | tf_op jit(solution)/shard_map/psum | solution.py:30
  18.6 76.0 %copy-start.2 = (bf16[256,1536]{1,0:T(8,128)(2,1)S(1)}, bf16[256,1536]{1,0:T(8,128)(2,1)}, u32[]{:S(2)}) copy-start(bf16[256,1536]{1,0:T(8,128)(2,1)} %param.7) | copy-start | bytes 2359300
  23.7 76.3 %copy-start = (bf16[256,1536]{1,0:T(8,128)(2,1)S(1)}, bf16[256,1536]{1,0:T(8,128)(2,1)}, u32[]{:S(2)}) copy-start(bf16[256,1536]{1,0:T(8,128)(2,1)} %param.4) | copy-start | bytes 2359300
  23.7 76.3 %copy-start.1 = (f32[1536]{0:T(1024)S(1)}, f32[1536]{0:T(1024)}, u32[]{:S(2)}) copy-start(f32[1536]{0:T(1024)} %param.5) | copy-start | bytes 18436
  23.7 120.2 %reduce-scatter.5.cloned.1.call-start = ((), (), s32[]{:S(2)}) async-start(), calls=%async_computation.4 | async-start | bytes 884736 | tf_op jit(solution)/shard_map/reduce_scatter | solution.py:44
  94.6 5.4 %copy-start.3 = (bf16[256,1536]{1,0:T(8,128)(2,1)S(1)}, bf16[256,1536]{1,0:T(8,128)(2,1)}, u32[]{:S(2)}) copy-start(bf16[256,1536]{1,0:T(8,128)(2,1)} %all-reduce.4.cloned.1.call-done) | copy-start | bytes 2359300
  99.9 198.8 %reduce-scatter.3.cloned.1.call-start = ((), (), s32[]{:S(2)}) async-start(), calls=%async_computation.3 | async-start | bytes 4866048 | tf_op jit(solution)/shard_map/reduce_scatter | solution.py:37
Sparse Core Ops, SparseCore 0:
  23.8 70.7 all-reduce.3
  100.1 43.7 reduce-scatter.4
  148.3 150.4 reduce-scatter.2
where the time goes:
time: 306 us; the launch traced here: 305 us
  waiting for transfers between devices  255 us (83%)
  blocking collectives  17.1 us (6%)
  matrix products  14.6 us (5%)
  between operations  13.8 us (5%)
  other arithmetic  4.5 us (1%)
    reduce_scatter x1, waiting for transfers between devices, body(): lax.psum_scatter((term * grad_scale).astype(jnp.bfloat16), 'dp', scatter_...  145 us
    psum x1, waiting for transfers between devices, body(): pre = lax.psum(partial_value.astype(jnp.bfloat16), 'mx').astype(jnp.float32)  70.9 us
    reduce_scatter x1, waiting for transfers between devices, body(): lax.psum_scatter(back_partial.astype(jnp.bfloat16), 'my', scatter_dimensi...  39.1 us
    psum x1, blocking collectives, body(): lax.psum((jnp.sum(values, axis=1), jnp.sum(values * values, axis=1)), 'mx')  9.93 us
    psum x1, blocking collectives, body(): lax.psum((jnp.sum(dcentred, axis=1), jnp.sum(dcentred * centred_rows, axi...  7.17 us
  transfers between devices with their start and end apart: 3, of which 3 were waited for; matrix products, arithmetic and copies ran while one was open for 2% of the time, Pallas kernels for 0%

commit v1 on v0

v1 whole, which is shorter than its diff:
```python
import math

import jax
import jax.numpy as jnp
from jax import lax
from jax.sharding import PartitionSpec as P

epsilon = 1e-06
BF = jnp.bfloat16
F32 = jnp.float32


def gelu_slope(pre):
    cdf = 0.5 * (1.0 + jax.scipy.special.erf(pre * (1.0 / math.sqrt(2.0))))
    return cdf + pre * jnp.exp(-0.5 * pre * pre) * (1.0 / math.sqrt(2.0 * math.pi))


def swap(value, axis, size, bits):
    return lax.ppermute(value, axis, [(i, i ^ bits) for i in range(size)])


def rows_at(value, start, count):
    return lax.dynamic_slice_in_dim(value, start, count, 0)


def dot(a, b, dims=((1,), (0,))):
    return lax.dot_general(a, b, (dims, ((), ())), preferred_element_type=F32)


Z = 16
ZH = Z // 2
GROUP = (16, 1, 17)


def body(tokens_in, norm_gain, in_weight, cotangent):
    tok_rows, width = tokens_in.shape
    hidden = in_weight.shape[1]
    n_dp, n_mx, n_my = lax.axis_size("dp"), lax.axis_size("mx"), lax.axis_size("my")
    d_all = width * n_mx
    half = tok_rows // 2
    dp, my = lax.axis_index("dp"), lax.axis_index("my")
    core = lax.axis_index("mx") % 2
    zh, x_lo, zl = (dp % Z) // 2, dp // Z, dp % 2
    block = width // n_dp

    values = tokens_in.astype(F32)
    sum_one, sum_two = lax.psum((jnp.sum(values, axis=1), jnp.sum(values * values, axis=1)), "mx")
    row_mean = sum_one / d_all
    inv_std = lax.rsqrt(sum_two / d_all - row_mean * row_mean + epsilon)
    centred = (values - row_mean[:, None]) * inv_std[:, None]
    normed = (centred * norm_gain[None, :]).astype(BF)

    mine = rows_at(normed, core * half, half)
    other = rows_at(normed, (1 - core) * half, half)
    sent = dot(other, in_weight).astype(BF)
    from_core = swap(sent, "mx", n_mx, 1)
    kept = dot(mine, in_weight) + from_core.astype(F32)
    from_x = swap(kept.astype(BF), "mx", n_mx, 2)
    pre = kept + from_x.astype(F32)
    cot = rows_at(cotangent, core * half, half)
    dpre = (cot.astype(F32) * gelu_slope(pre)).astype(BF)

    turned = jnp.concatenate([mine.T, other.T], axis=1).reshape(2, ZH, 2, block, tok_rows)
    turned = jnp.concatenate([turned, turned], axis=1)

    def columns(xb, zb):
        piece = lax.dynamic_slice(
            turned, (x_lo ^ xb, zh, zl ^ zb, 0, 0), (1, ZH, 1, block, tok_rows)
        )
        return piece.reshape(ZH * block, tok_rows)

    left = [columns(0, 0)]
    for bits in GROUP:
        left.append(swap(columns(bits // 16, bits % 2), "dp", n_dp, bits))

    own_pair = swap(dpre, "mx", n_mx, 1)
    arrived = [swap(dpre, "dp", n_dp, bits) for bits in GROUP]

    dpre_own = jnp.concatenate([dpre, own_pair], axis=0)
    back = dot(dpre_own, in_weight, ((1,), (1,))).astype(BF)
    own_rows = tok_rows // n_my
    parts = []
    for step in range(n_my):
        owner = (my + step) % n_my
        part = rows_at(back, (owner * own_rows + core * half) % tok_rows, own_rows)
        if step:
            part = lax.ppermute(part, "my", [(i, (i + step) % n_my) for i in range(n_my)])
        parts.append(part.astype(F32))
    dnormed = sum(parts)

    arrived = jnp.concatenate(arrived, axis=0)
    paired = swap(arrived, "mx", n_mx, 1)
    right = [dpre_own]
    for i in range(len(GROUP)):
        right.append(arrived[i * half : (i + 1) * half])
        right.append(paired[i * half : (i + 1) * half])
    grad_scale = 1.0 / math.sqrt(n_dp * tok_rows)
    term = (dot(jnp.concatenate(left, axis=1), jnp.concatenate(right, axis=0)) * grad_scale).astype(BF)
    total = term[:block].astype(F32)
    for step in range(1, ZH):
        perm = [
            (i, i // Z * Z + (i % Z + 2 * step) % Z) for i in range(n_dp)
        ]
        total += lax.ppermute(term[step * block : (step + 1) * block], "dp", perm).astype(F32)
    grad_weight = total.astype(BF).reshape(1, 1, block, hidden)

    first_row = my * own_rows
    centred_rows = rows_at(centred, first_row, own_rows)
    inv_rows = rows_at(inv_std, first_row, own_rows)
    dcentred = dnormed * norm_gain[None, :]
    total_a, total_b = lax.psum(
        (jnp.sum(dcentred, axis=1), jnp.sum(dcentred * centred_rows, axis=1)), "mx"
    )
    grad_tokens = inv_rows[:, None] * (
        dcentred - total_a[:, None] / d_all - centred_rows * (total_b[:, None] / d_all)
    )
    return (grad_weight, grad_tokens.astype(BF))


def solution(mesh):
    return jax.shard_map(
        body,
        mesh=mesh,
        in_specs=(P("dp", "mx"), P("mx"), P("mx", "my"), P("dp", "my")),
        out_specs=(P("mx", "dp", None, "my"), P(("dp", "my"), "mx")),
        check_vma=False,
    )
```

time: 306 us -> 220 us (0.72)
  the two profiles are of different devices: /device:TPU:40 before, /device:TPU:1 now
where the time goes in v1:
time: 220 us; the launch traced here: 219 us
  starting transfers between devices  93.7 us (43%)
  waiting for transfers between devices  59.7 us (27%)
  blocking collectives  29.7 us (14%)
  matrix products  14.5 us (7%)
  other arithmetic  10.6 us (5%)
  local copies, waits for them, and re-layouts  9.1 us (4%)
    ppermute x7, starting transfers between devices, body(): lax.ppermute(term[step * block:(step + 1) * block], 'dp', perm).astype(F32)  42.9 us
    ppermute x7, waiting for transfers between devices, body(): lax.ppermute(term[step * block:(step + 1) * block], 'dp', perm).astype(F32)  37.2 us
    ppermute x10, starting transfers between devices, swap(): return lax.ppermute(value, axis, [(i, i ^ bits) for i in range(size)])  28 us
    ppermute x7, starting transfers between devices, body(): lax.ppermute(part, 'my', [(i, (i + step) % n_my) for i in range(n_my)])  22.9 us
    ppermute x10, waiting for transfers between devices, swap(): return lax.ppermute(value, axis, [(i, i ^ bits) for i in range(size)])  20.9 us
    psum x1, blocking collectives, body(): lax.psum((jnp.sum(values, axis=1), jnp.sum(values * values, axis=1)), 'mx')  20.7 us
    dot_general x4, matrix products, dot(): return lax.dot_general(a, b, (dims, ((), ())), preferred_element_type=F32)  14.5 us
    psum x1, blocking collectives, body(): lax.psum((jnp.sum(dcentred, axis=1), jnp.sum(dcentred * centred_rows, axi...  9.05 us
  transfers between devices with their start and end apart: 24, of which 9 were waited for; matrix products, arithmetic and copies ran while one was open for 8% of the time, Pallas kernels for 0%

profile of v1, /device:TPU:1, one launch (start us, length us, event | category | flops | bytes accessed | tf_op | source)
XLA Modules:
  0.0 218.7 jit_solution(14973099859157648633)
XLA Ops:
  0.6 1.5 convert_reduce_fusion
  2.1 20.7 %all-reduce.1 = (f32[256]{0:T(256)S(1)}, f32[256]{0:T(256)S(1)}) all-reduce(f32[256]{0:T(256)S(1)} %get-tuple-element.3, f32[256]{0:T(256)S(1)} %get-tuple-element.2), channel_id=1, replica_groups=mesh['dp'=32,'mx'=4,'my'=8] {'mx'}, use_global_device_ids=true, to_apply=%region_3.4 | all-reduce | flops 512 | bytes 4096 | tf_op jit(solution)/shard_map/psum | solution.py:47
  22.8 1.5 fusion.1
  24.3 3.1 %convolution_convert_fusion.1 = bf16[128,1536]{1,0:T(8,128)(2,1)S(1)} fusion(bf16[1536,1536]{1,0:T(8,128)(2,1)} %param.6, bf16[256,1536]{1,0:T(8,128)(2,1)S(1)} %get-tuple-element.21, s32[]{:T(128)S(6)} %select_n.145), kind=kOutput, calls=%fused_computation.3 | convolution fusion | flops 604176384 | bytes 5505028 | tf_op jit(solution)/shard_map/dot_general | solution.py:27
  27.4 2.7 %collective-permute-start.3 = (bf16[128,1536]{1,0:T(8,128)(2,1)S(1)}, bf16[128,1536]{1,0:T(8,128)(2,1)S(1)}, u32[]{:S(2)}, u32[]{:S(2)}) collective-permute-start(bf16[128,1536]{1,0:T(8,128)(2,1)S(1)} %convolution_convert_fusion.1), channel_id=1, source_target_pairs={{0,8},{8,0},{16,24},{24,16},{1,9},{9,1},{17,25},{25,17},{2,10},{10... | collective-permute-start | bytes 1179656 | tf_op jit(solution)/shard_map/ppermute | solution.py:19
  30.1 1.3 collective-permute-done.3
  31.4 3.9 %fusion.19 = (bf16[128,1536]{1,0:T(8,128)(2,1)}, f32[128,1536]{1,0:T(8,128)S(1)}) fusion(bf16[128,1536]{1,0:T(8,128)(2,1)S(1)} %collective-permute-done.3, bf16[1536,1536]{1,0:T(8,128)(2,1)} %param.6, bf16[256,1536]{1,0:T(8,128)(2,1)S(1)} %get-tuple-element.21, s32[]{:T(128)S(6)} %select_n.144), kind=kOutput, calls=%fused_computation.38 | convolution fusion | flops 604569600 | bytes 6684676 | tf_op jit(solution)/shard_map/dot_general | solution.py:27
  35.3 1.9 collective-permute-start.4
  37.3 0.0 copy-start.2
  37.3 0.9 dynamic-slice_bitcast_fusion.1
  38.3 11.1 %collective-permute-done.4 = bf16[128,1536]{1,0:T(8,128)(2,1)} collective-permute-done((bf16[128,1536]{1,0:T(8,128)(2,1)}, bf16[128,1536]{1,0:T(8,128)(2,1)}, u32[]{:S(2)}, u32[]{:S(2)}) %collective-permute-start.4) | collective-permute-done | bytes 393248 | tf_op jit(solution)/shard_map/ppermute | solution.py:19
  49.3 2.4 %constant_dynamic-update-slice_fusion.4 = (bf16[1024,1536]{1,0:T(8,128)(2,1)}, bf16[128,1536]{1,0:T(8,128)(2,1)}) fusion(bf16[128,1536]{1,0:T(8,128)(2,1)} %collective-permute-done.4, f32[128,1536]{1,0:T(8,128)S(1)} %get-tuple-element.38, bf16[128,1536]{1,0:T(8,128)(2,1)S(1)} %collective-permute-done.3, bf16[256,1536]{1,0:T(8,128)(2,1)S(1)} %copy-done.2, ...), kind=kLoop, calls=%fused_computation.60 | loop fusion | flops 2949119 | bytes 2752516
  51.7 1.9 collective-permute-start.6
  53.6 1.9 collective-permute-start.7
  55.5 4.5 %collective-permute-start.8 = (bf16[128,1536]{1,0:T(8,128)(2,1)}, bf16[128,1536]{1,0:T(8,128)(2,1)S(1)}, u32[]{:S(2)}, u32[]{:S(2)}) collective-permute-start(bf16[128,1536]{1,0:T(8,128)(2,1)} %get-tuple-element.12), channel_id=1, source_target_pairs={{0,544},{32,512},{64,608},{96,576},{128,672},{160,640},{192,736},{... | collective-permute-start | bytes 1179656 | tf_op jit(solution)/shard_map/ppermute | solution.py:19
  60.3 0.1 dynamic_slice.58
  60.4 0.1 pad_maximum_fusion.1
  60.4 0.3 copy.6
  60.8 3.9 %collective-permute-start.5 = (bf16[128,1536]{1,0:T(8,128)(2,1)}, bf16[128,1536]{1,0:T(8,128)(2,1)S(1)}, u32[]{:S(2)}, u32[]{:S(2)}) collective-permute-start(bf16[128,1536]{1,0:T(8,128)(2,1)} %get-tuple-element.12), channel_id=1, source_target_pairs={{0,8},{8,0},{16,24},{24,16},{1,9},{9,1},{17,25},{25,17},{2,10},{10... | collective-permute-start | bytes 1179656 | tf_op jit(solution)/shard_map/ppermute | solution.py:19
  64.7 1.2 fusion.24
  65.9 0.0 collective-permute-done.7
  65.9 8.5 %collective-permute-done.8 = bf16[128,1536]{1,0:T(8,128)(2,1)S(1)} collective-permute-done((bf16[128,1536]{1,0:T(8,128)(2,1)}, bf16[128,1536]{1,0:T(8,128)(2,1)S(1)}, u32[]{:S(2)}, u32[]{:S(2)}) %collective-permute-start.8) | collective-permute-done | bytes 393248 | tf_op jit(solution)/shard_map/ppermute | solution.py:19
  74.4 2.2 %pad_maximum_fusion = bf16[384,1536]{1,0:T(8,128)(2,1)} fusion(bf16[128,1536]{1,0:T(8,128)(2,1)S(1)} %collective-permute-done.8, bf16[128,1536]{1,0:T(8,128)(2,1)} %collective-permute-done.7, bf16[128,1536]{1,0:T(8,128)(2,1)} %collective-permute-done.6), kind=kLoop, calls=%fused_computation.19 | loop fusion | flops 3538944 | bytes 2359296 | tf_op jit(solution)/shard_map/concatenate | solution.py:91
  76.6 4.3 %collective-permute-start.9 = (bf16[384,1536]{1,0:T(8,128)(2,1)}, bf16[384,1536]{1,0:T(8,128)(2,1)S(1)}, u32[]{:S(2)}, u32[]{:S(2)}) collective-permute-start(bf16[384,1536]{1,0:T(8,128)(2,1)} %pad_maximum_fusion), channel_id=1, source_target_pairs={{0,8},{8,0},{16,24},{24,16},{1,9},{9,1},{17,25},{25,17},{2,10},{10... | collective-permute-start | bytes 3538952 | tf_op jit(solution)/shard_map/ppermute | solution.py:19
  81.0 0.0 collective-permute-done.5
  81.0 3.9 %convolution_convert_fusion = bf16[256,1536]{1,0:T(8,128)(2,1)S(1)} fusion(bf16[1536,1536]{1,0:T(8,128)(2,1)} %param.6, bf16[128,1536]{1,0:T(8,128)(2,1)S(1)} %collective-permute-done.5, bf16[128,1536]{1,0:T(8,128)(2,1)} %get-tuple-element.12), kind=kOutput, calls=%fused_computation.2 | convolution fusion | flops 1209925632 | bytes 6291456 | tf_op jit(solution)/shard_map/dot_general | solution.py:27
  84.8 0.0 copy-start.4
  84.9 0.2 constant_dynamic-slice_fusion.6
  85.1 1.9 collective-permute-start.17
  87.0 1.9 collective-permute-start.18
  88.9 1.9 collective-permute-start.19
  90.8 7.5 %collective-permute-start.20 = (bf16[32,1536]{1,0:T(8,128)(2,1)S(1)}, bf16[32,1536]{1,0:T(8,128)(2,1)S(1)}, u32[]{:S(2)}, u32[]{:S(2)}) collective-permute-start(bf16[32,1536]{1,0:T(8,128)(2,1)S(1)} %get-tuple-element.26), channel_id=1, source_target_pairs={{0,4},{1,5},{2,6},{3,7},{4,0},{5,1},{6,2},{7,3},{8,12},{9,13},{10,... | collective-permute-start | bytes 294920 | tf_op jit(solution)/shard_map/ppermute | solution.py:87
  98.4 0.8 constant_dynamic-update-slice_fusion.3
  99.2 1.9 collective-permute-start.21
  101.1 5.5 %collective-permute-start.22 = (bf16[32,1536]{1,0:T(8,128)(2,1)S(1)}, bf16[32,1536]{1,0:T(8,128)(2,1)S(1)}, u32[]{:S(2)}, u32[]{:S(2)}) collective-permute-start(bf16[32,1536]{1,0:T(8,128)(2,1)S(1)} %get-tuple-element.24), channel_id=1, source_target_pairs={{0,6},{1,7},{2,0},{3,1},{4,2},{5,3},{6,4},{7,5},{8,14},{9,15},{10,... | collective-permute-start | bytes 294920 | tf_op jit(solution)/shard_map/ppermute | solution.py:87
  106.6 2.2 %collective-permute-start.23 = (bf16[32,1536]{1,0:T(8,128)(2,1)S(1)}, bf16[32,1536]{1,0:T(8,128)(2,1)S(1)}, u32[]{:S(2)}, u32[]{:S(2)}) collective-permute-start(bf16[32,1536]{1,0:T(8,128)(2,1)S(1)} %get-tuple-element.23), channel_id=1, source_target_pairs={{0,7},{1,0},{2,1},{3,2},{4,3},{5,4},{6,5},{7,6},{8,15},{9,8},{10,9... | collective-permute-start | bytes 294920 | tf_op jit(solution)/shard_map/ppermute | solution.py:87
  108.8 1.8 constant_dynamic-update-slice_fusion.2
  110.6 1.9 collective-permute-start
  112.5 1.9 collective-permute-start.1
  114.4 1.6 collective-permute-done.22
  116.0 3.0 %collective-permute-start.2 = (bf16[384,256]{1,0:T(8,128)(2,1)}, bf16[384,256]{1,0:T(8,128)(2,1)}, u32[]{:S(2)}, u32[]{:S(2)}) collective-permute-start(bf16[384,256]{1,0:T(8,128)(2,1)} %bitcast.6), channel_id=1, source_target_pairs={{0,544},{32,512},{64,608},{96,576},{128,672},{160,640},{192,736},{... | collective-permute-start | bytes 589832 | tf_op jit(solution)/shard_map/ppermute | solution.py:19
  119.0 0.3 fusion.32
  119.3 9.1 %all-reduce = (f32[32]{0:T(128)S(1)}, f32[32]{0:T(128)S(1)}) all-reduce(f32[32]{0:T(128)S(1)} %get-tuple-element.5, f32[32]{0:T(128)S(1)} %get-tuple-element.4), channel_id=1, replica_groups=mesh['dp'=32,'mx'=4,'my'=8] {'mx'}, use_global_device_ids=true, to_apply=%region_7.8 | all-reduce | flops 64 | bytes 512 | tf_op jit(solution)/shard_map/psum | solution.py:111
  128.3 0.8 slice_dynamic-update-slice_fusion.2
  129.1 1.8 constant_dynamic-update-slice_fusion.1
  130.9 0.8 slice_dynamic-update-slice_fusion.1
  131.7 0.8 constant_dynamic-update-slice_fusion
  132.5 0.8 slice_dynamic-update-slice_fusion
  133.3 3.6 %fusion = bf16[384,1536]{1,0:T(8,128)(2,1)S(1)} fusion(bf16[1024,1536]{1,0:T(8,128)(2,1)} %slice_dynamic-update-slice_fusion, bf16[384,256]{1,0:T(8,128)(2,1)} %collective-permute-done.2, bf16[384,256]{1,0:T(8,128)(2,1)} %collective-permute-done.1, bf16[384,256]{1,0:T(8,128)(2,1)} %collective-permute-done, bf16[384,256]{1,0:T(8,128)(2,1)S(1)} %bitcast.16), kind=kOutput, calls=%fused_computation.1 | convolution fusion | flops 1212284928 | bytes 5111808 | tf_op jit(solution)/shard_map/dot_general | solution.py:27
  136.9 0.1 fusion.34
  137.0 2.7 %collective-permute-start.10 = (bf16[48,1536]{1,0:T(8,128)(2,1)S(1)}, bf16[48,1536]{1,0:T(8,128)(2,1)S(1)}, u32[]{:S(2)}, u32[]{:S(2)}) collective-permute-start(bf16[48,1536]{1,0:T(8,128)(2,1)S(1)} %get-tuple-element.13), channel_id=1, source_target_pairs={{0,64},{32,96},{64,128},{96,160},{128,192},{160,224},{192,256},{22... | collective-permute-start | bytes 442376 | tf_op jit(solution)/shard_map/ppermute | solution.py:104
  139.7 10.6 %collective-permute-start.11 = (bf16[48,1536]{1,0:T(8,128)(2,1)S(1)}, bf16[48,1536]{1,0:T(8,128)(2,1)S(1)}, u32[]{:S(2)}, u32[]{:S(2)}) collective-permute-start(bf16[48,1536]{1,0:T(8,128)(2,1)S(1)} %get-tuple-element.19), channel_id=1, source_target_pairs={{0,128},{32,160},{64,192},{96,224},{128,256},{160,288},{192,320},{... | collective-permute-start | bytes 442376 | tf_op jit(solution)/shard_map/ppermute | solution.py:104
  150.3 10.0 %collective-permute-start.12 = (bf16[48,1536]{1,0:T(8,128)(2,1)S(1)}, bf16[48,1536]{1,0:T(8,128)(2,1)S(1)}, u32[]{:S(2)}, u32[]{:S(2)}) collective-permute-start(bf16[48,1536]{1,0:T(8,128)(2,1)S(1)} %get-tuple-element.18), channel_id=1, source_target_pairs={{0,192},{32,224},{64,256},{96,288},{128,320},{160,352},{192,384},{... | collective-permute-start | bytes 442376 | tf_op jit(solution)/shard_map/ppermute | solution.py:104
  160.4 3.7 %collective-permute-start.13 = (bf16[48,1536]{1,0:T(8,128)(2,1)S(1)}, bf16[48,1536]{1,0:T(8,128)(2,1)S(1)}, u32[]{:S(2)}, u32[]{:S(2)}) collective-permute-start(bf16[48,1536]{1,0:T(8,128)(2,1)S(1)} %get-tuple-element.17), channel_id=1, source_target_pairs={{0,256},{32,288},{64,320},{96,352},{128,384},{160,416},{192,448},{... | collective-permute-start | bytes 442376 | tf_op jit(solution)/shard_map/ppermute | solution.py:104
  164.1 10.3 %collective-permute-start.14 = (bf16[48,1536]{1,0:T(8,128)(2,1)S(1)}, bf16[48,1536]{1,0:T(8,128)(2,1)S(1)}, u32[]{:S(2)}, u32[]{:S(2)}) collective-permute-start(bf16[48,1536]{1,0:T(8,128)(2,1)S(1)} %get-tuple-element.16), channel_id=1, source_target_pairs={{0,320},{32,352},{64,384},{96,416},{128,448},{160,480},{192,0},{22... | collective-permute-start | bytes 442376 | tf_op jit(solution)/shard_map/ppermute | solution.py:104
  174.4 3.4 %collective-permute-start.15 = (bf16[48,1536]{1,0:T(8,128)(2,1)S(1)}, bf16[48,1536]{1,0:T(8,128)(2,1)S(1)}, u32[]{:S(2)}, u32[]{:S(2)}) collective-permute-start(bf16[48,1536]{1,0:T(8,128)(2,1)S(1)} %get-tuple-element.15), channel_id=1, source_target_pairs={{0,384},{32,416},{64,448},{96,480},{128,0},{160,32},{192,64},{224,... | collective-permute-start | bytes 442376 | tf_op jit(solution)/shard_map/ppermute | solution.py:104
  177.8 2.2 collective-permute-start.16
  179.9 0.7 multiply_convert_fusion.1
  180.7 8.8 %collective-permute-done.12 = bf16[48,1536]{1,0:T(8,128)(2,1)S(1)} collective-permute-done((bf16[48,1536]{1,0:T(8,128)(2,1)S(1)}, bf16[48,1536]{1,0:T(8,128)(2,1)S(1)}, u32[]{:S(2)}, u32[]{:S(2)}) %collective-permute-start.12) | collective-permute-done | bytes 147488 | tf_op jit(solution)/shard_map/ppermute | solution.py:104
  189.5 11.2 %collective-permute-done.13 = bf16[48,1536]{1,0:T(8,128)(2,1)S(1)} collective-permute-done((bf16[48,1536]{1,0:T(8,128)(2,1)S(1)}, bf16[48,1536]{1,0:T(8,128)(2,1)S(1)}, u32[]{:S(2)}, u32[]{:S(2)}) %collective-permute-start.13) | collective-permute-done | bytes 147488 | tf_op jit(solution)/shard_map/ppermute | solution.py:104
  200.7 11.4 %collective-permute-done.14 = bf16[48,1536]{1,0:T(8,128)(2,1)S(1)} collective-permute-done((bf16[48,1536]{1,0:T(8,128)(2,1)S(1)}, bf16[48,1536]{1,0:T(8,128)(2,1)S(1)}, u32[]{:S(2)}, u32[]{:S(2)}) %collective-permute-start.14) | collective-permute-done | bytes 147488 | tf_op jit(solution)/shard_map/ppermute | solution.py:104
  212.0 4.5 %collective-permute-done.15 = bf16[48,1536]{1,0:T(8,128)(2,1)S(1)} collective-permute-done((bf16[48,1536]{1,0:T(8,128)(2,1)S(1)}, bf16[48,1536]{1,0:T(8,128)(2,1)S(1)}, u32[]{:S(2)}, u32[]{:S(2)}) %collective-permute-start.15) | collective-permute-done | bytes 147488 | tf_op jit(solution)/shard_map/ppermute | solution.py:104
  216.5 1.4 collective-permute-done.16
  217.9 0.8 fusion.27
  (23 shorter events, 0.1 us)
Async XLA Ops:
  27.4 4.0 %collective-permute-start.3 = (bf16[128,1536]{1,0:T(8,128)(2,1)S(1)}, bf16[128,1536]{1,0:T(8,128)(2,1)S(1)}, u32[]{:S(2)}, u32[]{:S(2)}) collective-permute-start(bf16[128,1536]{1,0:T(8,128)(2,1)S(1)} %convolution_convert_fusion.1), channel_id=1, source_target_pairs={{0,8},{8,0},{16,24},{24,16},{1,9},{9,1},{17,25},{25,17},{2,10},{10... | collective-permute-start | bytes 1179656 | tf_op jit(solution)/shard_map/ppermute | solution.py:19
  35.3 14.0 %collective-permute-start.4 = (bf16[128,1536]{1,0:T(8,128)(2,1)}, bf16[128,1536]{1,0:T(8,128)(2,1)}, u32[]{:S(2)}, u32[]{:S(2)}) collective-permute-start(bf16[128,1536]{1,0:T(8,128)(2,1)} %get-tuple-element.37), channel_id=1, source_target_pairs={{0,16},{8,24},{16,0},{24,8},{1,17},{9,25},{17,1},{25,9},{2,18},{10... | collective-permute-start | bytes 1179656 | tf_op jit(solution)/shard_map/ppermute | solution.py:19
  37.3 12.0 %copy-start.2 = (bf16[256,1536]{1,0:T(8,128)(2,1)S(1)}, bf16[256,1536]{1,0:T(8,128)(2,1)}, u32[]{:S(2)}) copy-start(bf16[256,1536]{1,0:T(8,128)(2,1)} %param.7) | copy-start | bytes 2359300
  38.3 22.1 %copy-start = (bf16[1536,128]{0,1:T(8,128)(2,1)S(1)}, bf16[1536,128]{0,1:T(8,128)(2,1)}, u32[]{:S(2)}) copy-start(bf16[1536,128]{0,1:T(8,128)(2,1)} %get-tuple-element.33) | copy-start | bytes 1179652
  38.3 22.1 %copy-start.1 = (bf16[1536,128]{0,1:T(8,128)(2,1)S(1)}, bf16[1536,128]{0,1:T(8,128)(2,1)}, u32[]{:S(2)}) copy-start(bf16[1536,128]{0,1:T(8,128)(2,1)} %get-tuple-element.34) | copy-start | bytes 1179652
  51.7 14.2 %collective-permute-start.6 = (bf16[128,1536]{1,0:T(8,128)(2,1)}, bf16[128,1536]{1,0:T(8,128)(2,1)}, u32[]{:S(2)}, u32[]{:S(2)}) collective-permute-start(bf16[128,1536]{1,0:T(8,128)(2,1)} %get-tuple-element.12), channel_id=1, source_target_pairs={{0,512},{32,544},{64,576},{96,608},{128,640},{160,672},{192,704},{... | collective-permute-start | bytes 1179656 | tf_op jit(solution)/shard_map/ppermute | solution.py:19
  53.6 12.3 %collective-permute-start.7 = (bf16[128,1536]{1,0:T(8,128)(2,1)}, bf16[128,1536]{1,0:T(8,128)(2,1)}, u32[]{:S(2)}, u32[]{:S(2)}) collective-permute-start(bf16[128,1536]{1,0:T(8,128)(2,1)} %get-tuple-element.12), channel_id=1, source_target_pairs={{0,32},{32,0},{64,96},{96,64},{128,160},{160,128},{192,224},{224,1... | collective-permute-start | bytes 1179656 | tf_op jit(solution)/shard_map/ppermute | solution.py:19
  55.5 18.9 %collective-permute-start.8 = (bf16[128,1536]{1,0:T(8,128)(2,1)}, bf16[128,1536]{1,0:T(8,128)(2,1)S(1)}, u32[]{:S(2)}, u32[]{:S(2)}) collective-permute-start(bf16[128,1536]{1,0:T(8,128)(2,1)} %get-tuple-element.12), channel_id=1, source_target_pairs={{0,544},{32,512},{64,608},{96,576},{128,672},{160,640},{192,736},{... | collective-permute-start | bytes 1179656 | tf_op jit(solution)/shard_map/ppermute | solution.py:19
  60.8 20.2 %collective-permute-start.5 = (bf16[128,1536]{1,0:T(8,128)(2,1)}, bf16[128,1536]{1,0:T(8,128)(2,1)S(1)}, u32[]{:S(2)}, u32[]{:S(2)}) collective-permute-start(bf16[128,1536]{1,0:T(8,128)(2,1)} %get-tuple-element.12), channel_id=1, source_target_pairs={{0,8},{8,0},{16,24},{24,16},{1,9},{9,1},{17,25},{25,17},{2,10},{10... | collective-permute-start | bytes 1179656 | tf_op jit(solution)/shard_map/ppermute | solution.py:19
  76.6 51.7 %collective-permute-start.9 = (bf16[384,1536]{1,0:T(8,128)(2,1)}, bf16[384,1536]{1,0:T(8,128)(2,1)S(1)}, u32[]{:S(2)}, u32[]{:S(2)}) collective-permute-start(bf16[384,1536]{1,0:T(8,128)(2,1)} %pad_maximum_fusion), channel_id=1, source_target_pairs={{0,8},{8,0},{16,24},{24,16},{1,9},{9,1},{17,25},{25,17},{2,10},{10... | collective-permute-start | bytes 3538952 | tf_op jit(solution)/shard_map/ppermute | solution.py:19
  84.8 34.1 %copy-start.4 = (f32[1536]{0:T(1024)S(1)}, f32[1536]{0:T(1024)}, u32[]{:S(2)}) copy-start(f32[1536]{0:T(1024)} %param.5) | copy-start | bytes 18436
  85.1 14.1 %collective-permute-start.17 = (bf16[32,1536]{1,0:T(8,128)(2,1)S(1)}, bf16[32,1536]{1,0:T(8,128)(2,1)S(1)}, u32[]{:S(2)}, u32[]{:S(2)}) collective-permute-start(bf16[32,1536]{1,0:T(8,128)(2,1)S(1)} %get-tuple-element.22), channel_id=1, source_target_pairs={{0,1},{1,2},{2,3},{3,4},{4,5},{5,6},{6,7},{7,0},{8,9},{9,10},{10,1... | collective-permute-start | bytes 294920 | tf_op jit(solution)/shard_map/ppermute | solution.py:87
  87.0 14.1 %collective-permute-start.18 = (bf16[32,1536]{1,0:T(8,128)(2,1)S(1)}, bf16[32,1536]{1,0:T(8,128)(2,1)S(1)}, u32[]{:S(2)}, u32[]{:S(2)}) collective-permute-start(bf16[32,1536]{1,0:T(8,128)(2,1)S(1)} %get-tuple-element.28), channel_id=1, source_target_pairs={{0,2},{1,3},{2,4},{3,5},{4,6},{5,7},{6,0},{7,1},{8,10},{9,11},{10,... | collective-permute-start | bytes 294920 | tf_op jit(solution)/shard_map/ppermute | solution.py:87
  88.9 17.7 %collective-permute-start.19 = (bf16[32,1536]{1,0:T(8,128)(2,1)S(1)}, bf16[32,1536]{1,0:T(8,128)(2,1)S(1)}, u32[]{:S(2)}, u32[]{:S(2)}) collective-permute-start(bf16[32,1536]{1,0:T(8,128)(2,1)S(1)} %get-tuple-element.27), channel_id=1, source_target_pairs={{0,3},{1,4},{2,5},{3,6},{4,7},{5,0},{6,1},{7,2},{8,11},{9,12},{10,... | collective-permute-start | bytes 294920 | tf_op jit(solution)/shard_map/ppermute | solution.py:87
  90.8 19.7 %collective-permute-start.20 = (bf16[32,1536]{1,0:T(8,128)(2,1)S(1)}, bf16[32,1536]{1,0:T(8,128)(2,1)S(1)}, u32[]{:S(2)}, u32[]{:S(2)}) collective-permute-start(bf16[32,1536]{1,0:T(8,128)(2,1)S(1)} %get-tuple-element.26), channel_id=1, source_target_pairs={{0,4},{1,5},{2,6},{3,7},{4,0},{5,1},{6,2},{7,3},{8,12},{9,13},{10,... | collective-permute-start | bytes 294920 | tf_op jit(solution)/shard_map/ppermute | solution.py:87
  99.2 13.3 %collective-permute-start.21 = (bf16[32,1536]{1,0:T(8,128)(2,1)S(1)}, bf16[32,1536]{1,0:T(8,128)(2,1)S(1)}, u32[]{:S(2)}, u32[]{:S(2)}) collective-permute-start(bf16[32,1536]{1,0:T(8,128)(2,1)S(1)} %get-tuple-element.25), channel_id=1, source_target_pairs={{0,5},{1,6},{2,7},{3,0},{4,1},{5,2},{6,3},{7,4},{8,13},{9,14},{10,... | collective-permute-start | bytes 294920 | tf_op jit(solution)/shard_map/ppermute | solution.py:87
  101.1 14.9 %collective-permute-start.22 = (bf16[32,1536]{1,0:T(8,128)(2,1)S(1)}, bf16[32,1536]{1,0:T(8,128)(2,1)S(1)}, u32[]{:S(2)}, u32[]{:S(2)}) collective-permute-start(bf16[32,1536]{1,0:T(8,128)(2,1)S(1)} %get-tuple-element.24), channel_id=1, source_target_pairs={{0,6},{1,7},{2,0},{3,1},{4,2},{5,3},{6,4},{7,5},{8,14},{9,15},{10,... | collective-permute-start | bytes 294920 | tf_op jit(solution)/shard_map/ppermute | solution.py:87
  106.6 12.4 %collective-permute-start.23 = (bf16[32,1536]{1,0:T(8,128)(2,1)S(1)}, bf16[32,1536]{1,0:T(8,128)(2,1)S(1)}, u32[]{:S(2)}, u32[]{:S(2)}) collective-permute-start(bf16[32,1536]{1,0:T(8,128)(2,1)S(1)} %get-tuple-element.23), channel_id=1, source_target_pairs={{0,7},{1,0},{2,1},{3,2},{4,3},{5,4},{6,5},{7,6},{8,15},{9,8},{10,9... | collective-permute-start | bytes 294920 | tf_op jit(solution)/shard_map/ppermute | solution.py:87
  110.6 22.7 %collective-permute-start = (bf16[384,256]{1,0:T(8,128)(2,1)}, bf16[384,256]{1,0:T(8,128)(2,1)}, u32[]{:S(2)}, u32[]{:S(2)}) collective-permute-start(bf16[384,256]{1,0:T(8,128)(2,1)} %bitcast.4), channel_id=1, source_target_pairs={{0,512},{32,544},{64,576},{96,608},{128,640},{160,672},{192,704},{... | collective-permute-start | bytes 589832 | tf_op jit(solution)/shard_map/ppermute | solution.py:19
  112.5 20.8 %collective-permute-start.1 = (bf16[384,256]{1,0:T(8,128)(2,1)}, bf16[384,256]{1,0:T(8,128)(2,1)}, u32[]{:S(2)}, u32[]{:S(2)}) collective-permute-start(bf16[384,256]{1,0:T(8,128)(2,1)} %bitcast.5), channel_id=1, source_target_pairs={{0,32},{32,0},{64,96},{96,64},{128,160},{160,128},{192,224},{224,1... | collective-permute-start | bytes 589832 | tf_op jit(solution)/shard_map/ppermute | solution.py:19
  116.0 17.3 %collective-permute-start.2 = (bf16[384,256]{1,0:T(8,128)(2,1)}, bf16[384,256]{1,0:T(8,128)(2,1)}, u32[]{:S(2)}, u32[]{:S(2)}) collective-permute-start(bf16[384,256]{1,0:T(8,128)(2,1)} %bitcast.6), channel_id=1, source_target_pairs={{0,544},{32,512},{64,608},{96,576},{128,672},{160,640},{192,736},{... | collective-permute-start | bytes 589832 | tf_op jit(solution)/shard_map/ppermute | solution.py:19
  129.1 4.2 %copy-start.3 = (bf16[1,8,1,48,256]{4,3,2,1,0:T(8,128)(2,1)S(1)}, bf16[1,8,1,48,256]{4,3,2,1,0:T(8,128)(2,1)}, u32[]{:S(2)}) copy-start(bf16[1,8,1,48,256]{4,3,2,1,0:T(8,128)(2,1)} %get-tuple-element.29) | copy-start | bytes 589828
  137.0 37.4 %collective-permute-start.10 = (bf16[48,1536]{1,0:T(8,128)(2,1)S(1)}, bf16[48,1536]{1,0:T(8,128)(2,1)S(1)}, u32[]{:S(2)}, u32[]{:S(2)}) collective-permute-start(bf16[48,1536]{1,0:T(8,128)(2,1)S(1)} %get-tuple-element.13), channel_id=1, source_target_pairs={{0,64},{32,96},{64,128},{96,160},{128,192},{160,224},{192,256},{22... | collective-permute-start | bytes 442376 | tf_op jit(solution)/shard_map/ppermute | solution.py:104
  139.7 38.1 %collective-permute-start.11 = (bf16[48,1536]{1,0:T(8,128)(2,1)S(1)}, bf16[48,1536]{1,0:T(8,128)(2,1)S(1)}, u32[]{:S(2)}, u32[]{:S(2)}) collective-permute-start(bf16[48,1536]{1,0:T(8,128)(2,1)S(1)} %get-tuple-element.19), channel_id=1, source_target_pairs={{0,128},{32,160},{64,192},{96,224},{128,256},{160,288},{192,320},{... | collective-permute-start | bytes 442376 | tf_op jit(solution)/shard_map/ppermute | solution.py:104
  150.3 39.1 %collective-permute-start.12 = (bf16[48,1536]{1,0:T(8,128)(2,1)S(1)}, bf16[48,1536]{1,0:T(8,128)(2,1)S(1)}, u32[]{:S(2)}, u32[]{:S(2)}) collective-permute-start(bf16[48,1536]{1,0:T(8,128)(2,1)S(1)} %get-tuple-element.18), channel_id=1, source_target_pairs={{0,192},{32,224},{64,256},{96,288},{128,320},{160,352},{192,384},{... | collective-permute-start | bytes 442376 | tf_op jit(solution)/shard_map/ppermute | solution.py:104
  160.4 40.3 %collective-permute-start.13 = (bf16[48,1536]{1,0:T(8,128)(2,1)S(1)}, bf16[48,1536]{1,0:T(8,128)(2,1)S(1)}, u32[]{:S(2)}, u32[]{:S(2)}) collective-permute-start(bf16[48,1536]{1,0:T(8,128)(2,1)S(1)} %get-tuple-element.17), channel_id=1, source_target_pairs={{0,256},{32,288},{64,320},{96,352},{128,384},{160,416},{192,448},{... | collective-permute-start | bytes 442376 | tf_op jit(solution)/shard_map/ppermute | solution.py:104
  164.1 48.0 %collective-permute-start.14 = (bf16[48,1536]{1,0:T(8,128)(2,1)S(1)}, bf16[48,1536]{1,0:T(8,128)(2,1)S(1)}, u32[]{:S(2)}, u32[]{:S(2)}) collective-permute-start(bf16[48,1536]{1,0:T(8,128)(2,1)S(1)} %get-tuple-element.16), channel_id=1, source_target_pairs={{0,320},{32,352},{64,384},{96,416},{128,448},{160,480},{192,0},{22... | collective-permute-start | bytes 442376 | tf_op jit(solution)/shard_map/ppermute | solution.py:104
  174.4 42.1 %collective-permute-start.15 = (bf16[48,1536]{1,0:T(8,128)(2,1)S(1)}, bf16[48,1536]{1,0:T(8,128)(2,1)S(1)}, u32[]{:S(2)}, u32[]{:S(2)}) collective-permute-start(bf16[48,1536]{1,0:T(8,128)(2,1)S(1)} %get-tuple-element.15), channel_id=1, source_target_pairs={{0,384},{32,416},{64,448},{96,480},{128,0},{160,32},{192,64},{224,... | collective-permute-start | bytes 442376 | tf_op jit(solution)/shard_map/ppermute | solution.py:104
  177.8 40.1 %collective-permute-start.16 = (bf16[48,1536]{1,0:T(8,128)(2,1)S(1)}, bf16[48,1536]{1,0:T(8,128)(2,1)S(1)}, u32[]{:S(2)}, u32[]{:S(2)}) collective-permute-start(bf16[48,1536]{1,0:T(8,128)(2,1)S(1)} %get-tuple-element.14), channel_id=1, source_target_pairs={{0,448},{32,480},{64,0},{96,32},{128,64},{160,96},{192,128},{224,1... | collective-permute-start | bytes 442376 | tf_op jit(solution)/shard_map/ppermute | solution.py:104

commit v2 on v1

--- a/solution.py
+++ b/solution.py
@@ -3,6 +3,8 @@
 import jax
 import jax.numpy as jnp
 from jax import lax
+from jax.experimental import pallas as pl
+from jax.experimental.pallas import tpu as pltpu
 from jax.sharding import PartitionSpec as P
 
 epsilon = 1e-06
@@ -25,6 +27,43 @@
 
 def dot(a, b, dims=((1,), (0,))):
     return lax.dot_general(a, b, (dims, ((), ())), preferred_element_type=F32)
+
+
+def weight_kernel(scale, rows, *refs):
+    left, right, out = refs[:4], refs[4:12], refs[12:]
+    hidden = right[0].shape[1]
+    tile = 256
+
+    @pl.loop(0, hidden // tile)
+    def _(step):
+        cols = pl.ds(pl.multiple_of(step * tile, tile), tile)
+        total = None
+        for i in range(4):
+            tokens = jnp.concatenate([right[2 * i][:, cols], right[2 * i + 1][:, cols]], axis=0)
+            term = dot(left[i][...], tokens)
+            total = term if total is None else total + term
+        total = (total * scale).astype(BF)
+        for i, ref in enumerate(out):
+            ref[:, cols] = total[i * rows : (i + 1) * rows]
+
+
+def weight_blocks(left, right, scale, rows):
+    count = left[0].shape[0] // rows
+    hidden = right[0].shape[1]
+    tokens = sum(r.shape[0] for r in right)
+    whole = pl.BlockSpec(memory_space=pltpu.VMEM)
+    return pl.pallas_call(
+        lambda *refs: weight_kernel(scale, rows, *refs),
+        out_shape=[jax.ShapeDtypeStruct((rows, hidden), BF)] * count,
+        in_specs=[whole] * (len(left) + len(right)),
+        out_specs=[whole] * count,
+        compiler_params=pltpu.CompilerParams(vmem_limit_bytes=8 * 1024 * 1024),
+        cost_estimate=pl.CostEstimate(
+            flops=2 * rows * count * tokens * hidden,
+            bytes_accessed=2 * (rows * count * (tokens + hidden) + tokens * hidden),
+            transcendentals=0,
+        ),
+    )(*left, *right)
 
 
 Z = 16
@@ -54,11 +93,8 @@
     other = rows_at(normed, (1 - core) * half, half)
     sent = dot(other, in_weight).astype(BF)
     from_core = swap(sent, "mx", n_mx, 1)
-    kept = dot(mine, in_weight) + from_core.astype(F32)
+    kept = lax.optimization_barrier(dot(mine, in_weight)) + from_core.astype(F32)
     from_x = swap(kept.astype(BF), "mx", n_mx, 2)
-    pre = kept + from_x.astype(F32)
-    cot = rows_at(cotangent, core * half, half)
-    dpre = (cot.astype(F32) * gelu_slope(pre)).astype(BF)
 
     turned = jnp.concatenate([mine.T, other.T], axis=1).reshape(2, ZH, 2, block, tok_rows)
     turned = jnp.concatenate([turned, turned], axis=1)
@@ -72,37 +108,36 @@
     left = [columns(0, 0)]
     for bits in GROUP:
         left.append(swap(columns(bits // 16, bits % 2), "dp", n_dp, bits))
+    from_x, *left = lax.optimization_barrier((from_x, *left))
+
+    pre = kept + from_x.astype(F32)
+    cot = rows_at(cotangent, core * half, half)
+    dpre = (cot.astype(F32) * gelu_slope(pre)).astype(BF)
 
     own_pair = swap(dpre, "mx", n_mx, 1)
+    right = [dpre, own_pair]
     arrived = [swap(dpre, "dp", n_dp, bits) for bits in GROUP]
 
-    dpre_own = jnp.concatenate([dpre, own_pair], axis=0)
-    back = dot(dpre_own, in_weight, ((1,), (1,))).astype(BF)
+    in_order = jnp.where(core == 0, jnp.concatenate(right, axis=0), jnp.concatenate(right[::-1], axis=0))
+    back = dot(in_order, in_weight, ((1,), (1,)))
+    back, *arrived = lax.optimization_barrier((back, *arrived))
+    dnormed = lax.psum_scatter(back, "my", scatter_dimension=0, tiled=True)
     own_rows = tok_rows // n_my
-    parts = []
-    for step in range(n_my):
-        owner = (my + step) % n_my
-        part = rows_at(back, (owner * own_rows + core * half) % tok_rows, own_rows)
-        if step:
-            part = lax.ppermute(part, "my", [(i, (i + step) % n_my) for i in range(n_my)])
-        parts.append(part.astype(F32))
-    dnormed = sum(parts)
 
-    arrived = jnp.concatenate(arrived, axis=0)
-    paired = swap(arrived, "mx", n_mx, 1)
-    right = [dpre_own]
-    for i in range(len(GROUP)):
-        right.append(arrived[i * half : (i + 1) * half])
-        right.append(paired[i * half : (i + 1) * half])
-    grad_scale = 1.0 / math.sqrt(n_dp * tok_rows)
-    term = (dot(jnp.concatenate(left, axis=1), jnp.concatenate(right, axis=0)) * grad_scale).astype(BF)
-    total = term[:block].astype(F32)
-    for step in range(1, ZH):
-        perm = [
-            (i, i // Z * Z + (i % Z + 2 * step) % Z) for i in range(n_dp)
-        ]
-        total += lax.ppermute(term[step * block : (step + 1) * block], "dp", perm).astype(F32)
-    grad_weight = total.astype(BF).reshape(1, 1, block, hidden)
+    for piece in arrived:
+        right += [piece, swap(piece, "mx", n_mx, 1)]
+    terms = weight_blocks(left, right, 1.0 / math.sqrt(n_dp * tok_rows), block)
+
+    def hop(value, way):
+        perm = [(i, i // Z * Z + (i + 2 * way) % Z) for i in range(n_dp)]
+        return lax.ppermute(value.astype(BF), "dp", perm).astype(F32)
+
+    ahead, behind = terms[ZH // 2], terms[ZH // 2 + 1]
+    for step in range(1, ZH // 2):
+        ahead = hop(ahead, 1) + terms[ZH // 2 - step].astype(F32)
+        behind = hop(behind, -1) + terms[(ZH // 2 + 1 + step) % ZH].astype(F32)
+    ahead, dnormed = lax.optimization_barrier((ahead, dnormed))
+    grad_weight = (behind + hop(ahead, 1)).astype(BF).reshape(1, 1, block, hidden)
 
     first_row = my * own_rows
     centred_rows = rows_at(centred, first_row, own_rows)

time: 220 us -> 158 us (0.72)
  waiting for transfers between devices: 59.7 us -> 19.8 us
  starting transfers between devices: 93.7 us -> 64.3 us
  between operations: 1.4 us -> 14.5 us
  local copies, waits for them, and re-layouts: 9.1 us -> 1.99 us
  matrix products: 14.5 us -> 11.1 us
  Pallas kernels: 0 us -> 2.86 us
  blocking collectives: 29.7 us -> 32.2 us
    ppermute x14 -> x7, waiting for transfers between devices: 38.8 us -> 4.3 us  [hop(): return lax.ppermute(value.astype(BF), 'dp', perm).astype(F32)]
    ppermute x14 -> x7, starting transfers between devices: 65.7 us -> 33.4 us  [hop(): return lax.ppermute(value.astype(BF), 'dp', perm).astype(F32)]
    ppermute x10 -> x12, waiting for transfers between devices: 20.9 us -> 15.5 us  [swap(): return lax.ppermute(value, axis, [(i, i ^ bits) for i in range(size)])]
    unnamed x16 -> x10, local copies, waits for them, and re-layouts: 6.76 us -> 1.59 us
    dot_general x4 -> x3, matrix products: 14.5 us -> 11.1 us  [dot(): return lax.dot_general(a, b, (dims, ((), ())), preferred_element_type=F32)]
    ppermute x10 -> x12, starting transfers between devices: 28 us -> 30.9 us  [swap(): return lax.ppermute(value, axis, [(i, i ^ bits) for i in range(size)])]
    pallas_call x0 -> x1, Pallas kernels: none -> 2.86 us  [weight_blocks(): pl.pallas_call(lambda *refs: weight_kernel(scale, rows, *refs), out_shape...]
    psum x1, blocking collectives: 9.05 us -> 11.6 us  [body(): lax.psum((jnp.sum(dcentred, axis=1), jnp.sum(dcentred * centred_rows, axi...]
  transfers between devices with their start and end apart: 24 -> 20, of which waited for: 9 -> 10; matrix products, arithmetic and copies ran while one was open for 8% -> 8% of each run, Pallas kernels for 0% -> 2%
where the time goes in v2:
time: 158 us; the launch traced here: 156 us
  starting transfers between devices  64.3 us (41%)
  blocking collectives  32.2 us (20%)
  waiting for transfers between devices  19.8 us (13%)
  between operations  14.5 us (9%)
  matrix products  11.1 us (7%)
  other arithmetic  9.61 us (6%)
  Pallas kernels  2.86 us (2%)
  local copies, waits for them, and re-layouts  1.99 us (1%)
    ppermute x7, starting transfers between devices, hop(): return lax.ppermute(value.astype(BF), 'dp', perm).astype(F32)  33.4 us
    ppermute x12, starting transfers between devices, swap(): return lax.ppermute(value, axis, [(i, i ^ bits) for i in range(size)])  30.9 us
    psum x1, blocking collectives, body(): lax.psum((jnp.sum(values, axis=1), jnp.sum(values * values, axis=1)), 'mx')  20.7 us
    ppermute x12, waiting for transfers between devices, swap(): return lax.ppermute(value, axis, [(i, i ^ bits) for i in range(size)])  15.5 us
    psum x1, blocking collectives, body(): lax.psum((jnp.sum(dcentred, axis=1), jnp.sum(dcentred * centred_rows, axi...  11.6 us
    dot_general x3, matrix products, dot(): return lax.dot_general(a, b, (dims, ((), ())), preferred_element_type=F32)  11.1 us
    ppermute x7, waiting for transfers between devices, hop(): return lax.ppermute(value.astype(BF), 'dp', perm).astype(F32)  4.3 us
  transfers between devices with their start and end apart: 20, of which 10 were waited for; matrix products, arithmetic and copies ran while one was open for 8% of the time, Pallas kernels for 2%

profile of v2, /device:TPU:1, one launch (start us, length us, event | category | flops | bytes accessed | tf_op | source)
XLA Modules:
  0.0 156.5 jit_solution(14869232183527350525)
XLA Ops:
  7.2 0.0 reduce-scatter.2.cloned.1.call-start
  7.2 1.5 convert_reduce_fusion
  8.7 20.7 %all-reduce.1 = (f32[256]{0:T(256)S(1)}, f32[256]{0:T(256)S(1)}) all-reduce(f32[256]{0:T(256)S(1)} %get-tuple-element.41, f32[256]{0:T(256)S(1)} %get-tuple-element.40), channel_id=1, replica_groups=mesh['dp'=32,'mx'=4,'my'=8] {'mx'}, use_global_device_ids=true, to_apply=%region_3.4 | all-reduce | flops 512 | bytes 4096 | tf_op jit(solution)/shard_map/psum | solution.py:86
  29.4 2.6 %fusion = (f32[256,1536]{1,0:T(8,128)}, bf16[256,1536]{1,0:T(8,128)(2,1)S(1)}) fusion(bf16[256,1536]{1,0:T(8,128)(2,1)} %param.4, f32[256]{0:T(256)S(1)} %get-tuple-element.57, f32[256]{0:T(256)S(1)} %get-tuple-element.56, f32[1536]{0:T(1024)} %param.5), kind=kLoop, calls=%fused_computation.12 | loop fusion | flops 1966080 | bytes 3153920 | tf_op jit(solution)/shard_map/mul | solution.py:89
  32.0 3.1 %convolution_convert_fusion = bf16[128,1536]{1,0:T(8,128)(2,1)S(1)} fusion(bf16[1536,1536]{1,0:T(8,128)(2,1)} %param.6, bf16[256,1536]{1,0:T(8,128)(2,1)S(1)} %get-tuple-element.49, s32[]{:T(128)S(6)} %select_n.65), kind=kOutput, calls=%fused_computation | convolution fusion | flops 604176384 | bytes 5505028 | tf_op jit(solution)/shard_map/dot_general | solution.py:29
  35.2 2.7 %collective-permute-start = (bf16[128,1536]{1,0:T(8,128)(2,1)S(1)}, bf16[128,1536]{1,0:T(8,128)(2,1)S(1)}, u32[]{:S(2)}, u32[]{:S(2)}) collective-permute-start(bf16[128,1536]{1,0:T(8,128)(2,1)S(1)} %convolution_convert_fusion), channel_id=1, source_target_pairs={{0,8},{8,0},{16,24},{24,16},{1,9},{9,1},{17,25},{25,17},{2,10},{10... | collective-permute-start | bytes 1179656 | tf_op jit(solution)/shard_map/ppermute | solution.py:21
  37.8 3.1 %fusion.17 = f32[128,1536]{1,0:T(8,128)S(1)} fusion(bf16[1536,1536]{1,0:T(8,128)(2,1)} %param.6, bf16[256,1536]{1,0:T(8,128)(2,1)S(1)} %get-tuple-element.49, s32[]{:T(128)S(6)} %select_n.64), kind=kOutput, calls=%fused_computation.36 | convolution fusion | flops 603979776 | bytes 5898244 | tf_op jit(solution)/shard_map/dot_general | solution.py:29
  41.0 0.1 dynamic-slice_bitcast_fusion.1
  41.0 0.0 collective-permute-done
  41.0 0.8 fusion.15
  41.9 1.9 %collective-permute-start.1 = (bf16[128,1536]{1,0:T(8,128)(2,1)}, bf16[128,1536]{1,0:T(8,128)(2,1)S(1)}, u32[]{:S(2)}, u32[]{:S(2)}) collective-permute-start(bf16[128,1536]{1,0:T(8,128)(2,1)} %fusion.15), channel_id=1, source_target_pairs={{0,16},{8,24},{16,0},{24,8},{1,17},{9,25},{17,1},{25,9},{2,18},{10... | collective-permute-start | bytes 1179656 | tf_op jit(solution)/shard_map/ppermute | solution.py:21
  43.8 0.1 pad_maximum_fusion
  43.9 0.3 copy.8
  44.2 0.0 copy-start.3
  44.2 0.3 fusion.19
  44.6 1.9 %collective-permute-start.4 = (bf16[384,256]{1,0:T(8,128)(2,1)S(1)}, bf16[384,256]{1,0:T(8,128)(2,1)S(1)}, u32[]{:S(2)}, u32[]{:S(2)}) collective-permute-start(bf16[384,256]{1,0:T(8,128)(2,1)S(1)} %bitcast.18), channel_id=1, source_target_pairs={{0,544},{32,512},{64,608},{96,576},{128,672},{160,640},{192,736},{... | collective-permute-start | bytes 589832 | tf_op jit(solution)/shard_map/ppermute | solution.py:21
  46.5 1.9 %collective-permute-start.3 = (bf16[384,256]{1,0:T(8,128)(2,1)S(1)}, bf16[384,256]{1,0:T(8,128)(2,1)S(1)}, u32[]{:S(2)}, u32[]{:S(2)}) collective-permute-start(bf16[384,256]{1,0:T(8,128)(2,1)S(1)} %bitcast.17), channel_id=1, source_target_pairs={{0,32},{32,0},{64,96},{96,64},{128,160},{160,128},{192,224},{224,1... | collective-permute-start | bytes 589832 | tf_op jit(solution)/shard_map/ppermute | solution.py:21
  48.4 4.5 %collective-permute-start.2 = (bf16[384,256]{1,0:T(8,128)(2,1)S(1)}, bf16[384,256]{1,0:T(8,128)(2,1)S(1)}, u32[]{:S(2)}, u32[]{:S(2)}) collective-permute-start(bf16[384,256]{1,0:T(8,128)(2,1)S(1)} %bitcast.16), channel_id=1, source_target_pairs={{0,512},{32,544},{64,576},{96,608},{128,640},{160,672},{192,704},{... | collective-permute-start | bytes 589832 | tf_op jit(solution)/shard_map/ppermute | solution.py:21
  52.9 0.8 collective-permute-done.4.refs_3_
  53.7 1.4 collective-permute-done.3.refs_2_
  55.1 3.1 %collective-permute-done.2.refs_1_ = bf16[384,256]{1,0:T(8,128)(2,1)S(1)} collective-permute-done((bf16[384,256]{1,0:T(8,128)(2,1)S(1)}, bf16[384,256]{1,0:T(8,128)(2,1)S(1)}, u32[]{:S(2)}, u32[]{:S(2)}) %collective-permute-start.2) | collective-permute-done | bytes 196640 | tf_op jit(solution)/shard_map/ppermute | solution.py:21
  58.2 0.0 collective-permute-done.1
  58.2 0.0 copy-done.3
  58.2 0.5 fusion.7.refs_4_
  58.6 2.9 %collective-permute-start.5 = (bf16[128,1536]{1,0:T(8,128)(2,1)S(1)}, bf16[128,1536]{1,0:T(8,128)(2,1)S(1)}, u32[]{:S(2)}, u32[]{:S(2)}) collective-permute-start(bf16[128,1536]{1,0:T(8,128)(2,1)S(1)} %fusion.7.refs_4_), channel_id=1, source_target_pairs={{0,8},{8,0},{16,24},{24,16},{1,9},{9,1},{17,25},{25,17},{2,10},{10... | collective-permute-start | bytes 1179656 | tf_op jit(solution)/shard_map/ppermute | solution.py:21
  61.5 2.8 %collective-permute-start.8 = (bf16[128,1536]{1,0:T(8,128)(2,1)S(1)}, bf16[128,1536]{1,0:T(8,128)(2,1)S(1)}, u32[]{:S(2)}, u32[]{:S(2)}) collective-permute-start(bf16[128,1536]{1,0:T(8,128)(2,1)S(1)} %fusion.7.refs_4_), channel_id=1, source_target_pairs={{0,544},{32,512},{64,608},{96,576},{128,672},{160,640},{192,736},{... | collective-permute-start | bytes 1179656 | tf_op jit(solution)/shard_map/ppermute | solution.py:21
  64.3 3.4 %collective-permute-start.7 = (bf16[128,1536]{1,0:T(8,128)(2,1)S(1)}, bf16[128,1536]{1,0:T(8,128)(2,1)S(1)}, u32[]{:S(2)}, u32[]{:S(2)}) collective-permute-start(bf16[128,1536]{1,0:T(8,128)(2,1)S(1)} %fusion.7.refs_4_), channel_id=1, source_target_pairs={{0,32},{32,0},{64,96},{96,64},{128,160},{160,128},{192,224},{224,1... | collective-permute-start | bytes 1179656 | tf_op jit(solution)/shard_map/ppermute | solution.py:21
  67.7 2.2 %collective-permute-start.6 = (bf16[128,1536]{1,0:T(8,128)(2,1)S(1)}, bf16[128,1536]{1,0:T(8,128)(2,1)S(1)}, u32[]{:S(2)}, u32[]{:S(2)}) collective-permute-start(bf16[128,1536]{1,0:T(8,128)(2,1)S(1)} %fusion.7.refs_4_), channel_id=1, source_target_pairs={{0,512},{32,544},{64,576},{96,608},{128,640},{160,672},{192,704},{... | collective-permute-start | bytes 1179656 | tf_op jit(solution)/shard_map/ppermute | solution.py:21
  69.9 0.0 collective-permute-done.5.refs_5_
  69.9 4.9 %fusion.8 = f32[256,1536]{1,0:T(8,128)} fusion(bf16[1536,1536]{1,0:T(8,128)(2,1)} %param.6, bf16[128,1536]{1,0:T(8,128)(2,1)S(1)} %collective-permute-done.5.refs_5_, bf16[128,1536]{1,0:T(8,128)(2,1)S(1)} %fusion.7.refs_4_, pred[]{:T(512)S(6)} %eq.7), kind=kOutput, calls=%fused_computation.24 | convolution fusion | flops 1211498496 | bytes 7077889 | tf_op jit(solution)/shard_map/dot_general | solution.py:29
  74.8 0.0 copy-done
  74.8 0.3 collective-permute-done.8.refs_10_
  75.1 8.4 %collective-permute-done.7.refs_8_ = bf16[128,1536]{1,0:T(8,128)(2,1)S(1)} collective-permute-done((bf16[128,1536]{1,0:T(8,128)(2,1)S(1)}, bf16[128,1536]{1,0:T(8,128)(2,1)S(1)}, u32[]{:S(2)}, u32[]{:S(2)}) %collective-permute-start.7) | collective-permute-done | bytes 393248 | tf_op jit(solution)/shard_map/ppermute | solution.py:21
  83.5 0.3 collective-permute-done.6.refs_6_
  83.8 0.0 reduce-scatter.2.cloned.1.call-update
  83.8 2.4 %collective-permute-start.9 = (bf16[128,1536]{1,0:T(8,128)(2,1)S(1)}, bf16[128,1536]{1,0:T(8,128)(2,1)S(1)}, u32[]{:S(2)}, u32[]{:S(2)}) collective-permute-start(bf16[128,1536]{1,0:T(8,128)(2,1)S(1)} %collective-permute-done.6.refs_6_), channel_id=1, source_target_pairs={{0,8},{8,0},{16,24},{24,16},{1,9},{9,1},{17,25},{25,17},{2,10},{10... | collective-permute-start | bytes 1179656 | tf_op jit(solution)/shard_map/ppermute | solution.py:21
  86.2 1.9 %collective-permute-start.10 = (bf16[128,1536]{1,0:T(8,128)(2,1)S(1)}, bf16[128,1536]{1,0:T(8,128)(2,1)S(1)}, u32[]{:S(2)}, u32[]{:S(2)}) collective-permute-start(bf16[128,1536]{1,0:T(8,128)(2,1)S(1)} %collective-permute-done.7.refs_8_), channel_id=1, source_target_pairs={{0,8},{8,0},{16,24},{24,16},{1,9},{9,1},{17,25},{25,17},{2,10},{10... | collective-permute-start | bytes 1179656 | tf_op jit(solution)/shard_map/ppermute | solution.py:21
  88.1 2.4 %collective-permute-start.11 = (bf16[128,1536]{1,0:T(8,128)(2,1)S(1)}, bf16[128,1536]{1,0:T(8,128)(2,1)S(1)}, u32[]{:S(2)}, u32[]{:S(2)}) collective-permute-start(bf16[128,1536]{1,0:T(8,128)(2,1)S(1)} %collective-permute-done.8.refs_10_), channel_id=1, source_target_pairs={{0,8},{8,0},{16,24},{24,16},{1,9},{9,1},{17,25},{25,17},{2,10},{10... | collective-permute-start | bytes 1179656 | tf_op jit(solution)/shard_map/ppermute | solution.py:21
  90.5 0.0 collective-permute-done.9.refs_7_
  90.6 0.0 collective-permute-done.10.refs_9_
  90.6 1.3 collective-permute-done.11.refs_11_
  91.9 0.9 copy-done.1
  92.8 2.9 %shard_map.59 = (bf16[48,1536]{1,0:T(8,128)(2,1)S(1)}, bf16[48,1536]{1,0:T(8,128)(2,1)S(1)}, bf16[48,1536]{1,0:T(8,128)(2,1)S(1)}, bf16[48,1536]{1,0:T(8,128)(2,...) custom-call(bf16[384,256]{1,0:T(8,128)(2,1)S(1)} %bitcast.14, ...), custom_call_target="tpu_custom_call" | custom-call | flops 1207959552 | bytes 5111808 | tf_op jit(solution)/shard_map/pallas_call | solution.py:55
  95.7 0.6 copy-done.2
  96.3 2.0 %collective-permute-start.15 = (bf16[48,1536]{1,0:T(8,128)(2,1)}, bf16[48,1536]{1,0:T(8,128)(2,1)S(1)}, u32[]{:S(2)}, u32[]{:S(2)}) collective-permute-start(bf16[48,1536]{1,0:T(8,128)(2,1)} %get-tuple-element.33), channel_id=1, source_target_pairs={{0,64},{32,96},{64,128},{96,160},{128,192},{160,224},{192,256},{22... | collective-permute-start | bytes 442376 | tf_op jit(solution)/shard_map/ppermute | solution.py:133
  98.4 0.1 dynamic_slice.34
  98.4 12.7 %collective-permute-start.12 = (bf16[48,1536]{1,0:T(8,128)(2,1)}, bf16[48,1536]{1,0:T(8,128)(2,1)S(1)}, u32[]{:S(2)}, u32[]{:S(2)}) collective-permute-start(bf16[48,1536]{1,0:T(8,128)(2,1)} %copy-done.2), channel_id=1, source_target_pairs={{0,448},{32,480},{64,0},{96,32},{128,64},{160,96},{192,128},{224,1... | collective-permute-start | bytes 442376 | tf_op jit(solution)/shard_map/ppermute | solution.py:133
  111.1 2.2 %collective-permute-done.15 = bf16[48,1536]{1,0:T(8,128)(2,1)S(1)} collective-permute-done((bf16[48,1536]{1,0:T(8,128)(2,1)}, bf16[48,1536]{1,0:T(8,128)(2,1)S(1)}, u32[]{:S(2)}, u32[]{:S(2)}) %collective-permute-start.15) | collective-permute-done | bytes 147488 | tf_op jit(solution)/shard_map/ppermute | solution.py:133
  113.4 1.9 %collective-permute-start.16 = (bf16[48,1536]{1,0:T(8,128)(2,1)S(1)}, bf16[48,1536]{1,0:T(8,128)(2,1)S(1)}, u32[]{:S(2)}, u32[]{:S(2)}) collective-permute-start(bf16[48,1536]{1,0:T(8,128)(2,1)S(1)} %add_convert_fusion.2), channel_id=1, source_target_pairs={{0,64},{32,96},{64,128},{96,160},{128,192},{160,224},{192,256},{22... | collective-permute-start | bytes 442376 | tf_op jit(solution)/shard_map/ppermute | solution.py:133
  115.3 2.0 %collective-permute-done.12 = bf16[48,1536]{1,0:T(8,128)(2,1)S(1)} collective-permute-done((bf16[48,1536]{1,0:T(8,128)(2,1)}, bf16[48,1536]{1,0:T(8,128)(2,1)S(1)}, u32[]{:S(2)}, u32[]{:S(2)}) %collective-permute-start.12) | collective-permute-done | bytes 147488 | tf_op jit(solution)/shard_map/ppermute | solution.py:133
  117.3 6.3 %collective-permute-start.13 = (bf16[48,1536]{1,0:T(8,128)(2,1)S(1)}, bf16[48,1536]{1,0:T(8,128)(2,1)S(1)}, u32[]{:S(2)}, u32[]{:S(2)}) collective-permute-start(bf16[48,1536]{1,0:T(8,128)(2,1)S(1)} %add_convert_fusion.4), channel_id=1, source_target_pairs={{0,448},{32,480},{64,0},{96,32},{128,64},{160,96},{192,128},{224,1... | collective-permute-start | bytes 442376 | tf_op jit(solution)/shard_map/ppermute | solution.py:133
  123.6 0.0 collective-permute-done.16
  123.7 1.9 %collective-permute-start.17 = (bf16[48,1536]{1,0:T(8,128)(2,1)S(1)}, bf16[48,1536]{1,0:T(8,128)(2,1)S(1)}, u32[]{:S(2)}, u32[]{:S(2)}) collective-permute-start(bf16[48,1536]{1,0:T(8,128)(2,1)S(1)} %add_convert_fusion.1), channel_id=1, source_target_pairs={{0,64},{32,96},{64,128},{96,160},{128,192},{160,224},{192,256},{22... | collective-permute-start | bytes 442376 | tf_op jit(solution)/shard_map/ppermute | solution.py:133
  125.6 0.1 collective-permute-done.13
  125.7 6.0 %collective-permute-start.14 = (bf16[48,1536]{1,0:T(8,128)(2,1)S(1)}, bf16[48,1536]{1,0:T(8,128)(2,1)S(1)}, u32[]{:S(2)}, u32[]{:S(2)}) collective-permute-start(bf16[48,1536]{1,0:T(8,128)(2,1)S(1)} %add_convert_fusion.3), channel_id=1, source_target_pairs={{0,448},{32,480},{64,0},{96,32},{128,64},{160,96},{192,128},{224,1... | collective-permute-start | bytes 442376 | tf_op jit(solution)/shard_map/ppermute | solution.py:133
  131.8 0.0 collective-permute-done.17
  131.8 0.0 reduce-scatter.2.cloned.1.call-done
  131.8 2.5 %collective-permute-start.18 = (bf16[48,1536]{1,0:T(8,128)(2,1)S(1)}, bf16[48,1536]{1,0:T(8,128)(2,1)S(1)}, u32[]{:S(2)}, u32[]{:S(2)}) collective-permute-start(bf16[48,1536]{1,0:T(8,128)(2,1)S(1)} %convert_add_fusion.1), channel_id=1, source_target_pairs={{0,64},{32,96},{64,128},{96,160},{128,192},{160,224},{192,256},{22... | collective-permute-start | bytes 442376 | tf_op jit(solution)/shard_map/ppermute | solution.py:133
  134.4 1.2 multiply_reduce_fusion.1
  135.6 11.6 %all-reduce = (f32[32]{0:T(128)S(1)}, f32[32]{0:T(128)S(1)}) all-reduce(f32[32]{0:T(128)S(1)} %get-tuple-element.43, f32[32]{0:T(128)S(1)} %get-tuple-element.42), channel_id=1, replica_groups=mesh['dp'=32,'mx'=4,'my'=8] {'mx'}, use_global_device_ids=true, to_apply=%region_8.9 | all-reduce | flops 64 | bytes 512 | tf_op jit(solution)/shard_map/psum | solution.py:146
  147.1 1.8 %multiply_convert_fusion.1 = bf16[32,1536]{1,0:T(8,128)(2,1)} fusion(f32[256,1536]{1,0:T(8,128)} %get-tuple-element.48, s32[]{:T(128)S(6)} %select_n.77, f32[32,1536]{1,0:T(8,128)} %reduce-scatter.2.cloned.1.call-done, f32[32]{0:T(128)S(1)} %get-tuple-element.58, f32[32]{0:T(128)S(1)} %get-tuple-element.59, f32[1536]{0:T(1024)S(1)} %copy-done.4, ...), kind=kLoop, calls=%fused_computation.48 | loop fusion | flops 294912 | bytes 498052 | tf_op jit(solution)/shard_map/convert_element_type | solution.py:152
  148.9 0.0 collective-permute-done.14
  148.9 0.0 collective-permute-done.18
  148.9 0.7 fusion.23
  (12 shorter events, 0.2 us)
Async XLA Ops:
  7.2 124.7 %reduce-scatter.2.cloned.1.call-start = ((), (), s32[]{:S(2)}) async-start(), calls=%async_computation.1 | async-start | bytes 1769472 | tf_op jit(solution)/shard_map/reduce_scatter | solution.py:124
  35.2 5.9 %collective-permute-start = (bf16[128,1536]{1,0:T(8,128)(2,1)S(1)}, bf16[128,1536]{1,0:T(8,128)(2,1)S(1)}, u32[]{:S(2)}, u32[]{:S(2)}) collective-permute-start(bf16[128,1536]{1,0:T(8,128)(2,1)S(1)} %convolution_convert_fusion), channel_id=1, source_target_pairs={{0,8},{8,0},{16,24},{24,16},{1,9},{9,1},{17,25},{25,17},{2,10},{10... | collective-permute-start | bytes 1179656 | tf_op jit(solution)/shard_map/ppermute | solution.py:21
  41.9 16.3 %collective-permute-start.1 = (bf16[128,1536]{1,0:T(8,128)(2,1)}, bf16[128,1536]{1,0:T(8,128)(2,1)S(1)}, u32[]{:S(2)}, u32[]{:S(2)}) collective-permute-start(bf16[128,1536]{1,0:T(8,128)(2,1)} %fusion.15), channel_id=1, source_target_pairs={{0,16},{8,24},{16,0},{24,8},{1,17},{9,25},{17,1},{25,9},{2,18},{10... | collective-permute-start | bytes 1179656 | tf_op jit(solution)/shard_map/ppermute | solution.py:21
  44.2 14.0 %copy-start.3 = (bf16[256,1536]{1,0:T(8,128)(2,1)S(1)}, bf16[256,1536]{1,0:T(8,128)(2,1)}, u32[]{:S(2)}) copy-start(bf16[256,1536]{1,0:T(8,128)(2,1)} %param.7) | copy-start | bytes 2359300
  44.6 9.1 %collective-permute-start.4 = (bf16[384,256]{1,0:T(8,128)(2,1)S(1)}, bf16[384,256]{1,0:T(8,128)(2,1)S(1)}, u32[]{:S(2)}, u32[]{:S(2)}) collective-permute-start(bf16[384,256]{1,0:T(8,128)(2,1)S(1)} %bitcast.18), channel_id=1, source_target_pairs={{0,544},{32,512},{64,608},{96,576},{128,672},{160,640},{192,736},{... | collective-permute-start | bytes 589832 | tf_op jit(solution)/shard_map/ppermute | solution.py:21
  46.5 8.6 %collective-permute-start.3 = (bf16[384,256]{1,0:T(8,128)(2,1)S(1)}, bf16[384,256]{1,0:T(8,128)(2,1)S(1)}, u32[]{:S(2)}, u32[]{:S(2)}) collective-permute-start(bf16[384,256]{1,0:T(8,128)(2,1)S(1)} %bitcast.17), channel_id=1, source_target_pairs={{0,32},{32,0},{64,96},{96,64},{128,160},{160,128},{192,224},{224,1... | collective-permute-start | bytes 589832 | tf_op jit(solution)/shard_map/ppermute | solution.py:21
  48.4 9.8 %collective-permute-start.2 = (bf16[384,256]{1,0:T(8,128)(2,1)S(1)}, bf16[384,256]{1,0:T(8,128)(2,1)S(1)}, u32[]{:S(2)}, u32[]{:S(2)}) collective-permute-start(bf16[384,256]{1,0:T(8,128)(2,1)S(1)} %bitcast.16), channel_id=1, source_target_pairs={{0,512},{32,544},{64,576},{96,608},{128,640},{160,672},{192,704},{... | collective-permute-start | bytes 589832 | tf_op jit(solution)/shard_map/ppermute | solution.py:21
  58.2 16.7 %copy-start = (bf16[384,256]{1,0:T(8,128)(2,1)}, bf16[384,256]{1,0:T(8,128)(2,1)S(1)}, u32[]{:S(2)}) copy-start(bf16[384,256]{1,0:T(8,128)(2,1)S(1)} %collective-permute-done.2.refs_1_) | copy-start | bytes 589828
  58.6 11.3 %collective-permute-start.5 = (bf16[128,1536]{1,0:T(8,128)(2,1)S(1)}, bf16[128,1536]{1,0:T(8,128)(2,1)S(1)}, u32[]{:S(2)}, u32[]{:S(2)}) collective-permute-start(bf16[128,1536]{1,0:T(8,128)(2,1)S(1)} %fusion.7.refs_4_), channel_id=1, source_target_pairs={{0,8},{8,0},{16,24},{24,16},{1,9},{9,1},{17,25},{25,17},{2,10},{10... | collective-permute-start | bytes 1179656 | tf_op jit(solution)/shard_map/ppermute | solution.py:21
  61.5 13.6 %collective-permute-start.8 = (bf16[128,1536]{1,0:T(8,128)(2,1)S(1)}, bf16[128,1536]{1,0:T(8,128)(2,1)S(1)}, u32[]{:S(2)}, u32[]{:S(2)}) collective-permute-start(bf16[128,1536]{1,0:T(8,128)(2,1)S(1)} %fusion.7.refs_4_), channel_id=1, source_target_pairs={{0,544},{32,512},{64,608},{96,576},{128,672},{160,640},{192,736},{... | collective-permute-start | bytes 1179656 | tf_op jit(solution)/shard_map/ppermute | solution.py:21
  64.3 19.2 %collective-permute-start.7 = (bf16[128,1536]{1,0:T(8,128)(2,1)S(1)}, bf16[128,1536]{1,0:T(8,128)(2,1)S(1)}, u32[]{:S(2)}, u32[]{:S(2)}) collective-permute-start(bf16[128,1536]{1,0:T(8,128)(2,1)S(1)} %fusion.7.refs_4_), channel_id=1, source_target_pairs={{0,32},{32,0},{64,96},{96,64},{128,160},{160,128},{192,224},{224,1... | collective-permute-start | bytes 1179656 | tf_op jit(solution)/shard_map/ppermute | solution.py:21
  67.7 16.1 %collective-permute-start.6 = (bf16[128,1536]{1,0:T(8,128)(2,1)S(1)}, bf16[128,1536]{1,0:T(8,128)(2,1)S(1)}, u32[]{:S(2)}, u32[]{:S(2)}) collective-permute-start(bf16[128,1536]{1,0:T(8,128)(2,1)S(1)} %fusion.7.refs_4_), channel_id=1, source_target_pairs={{0,512},{32,544},{64,576},{96,608},{128,640},{160,672},{192,704},{... | collective-permute-start | bytes 1179656 | tf_op jit(solution)/shard_map/ppermute | solution.py:21
  83.8 6.8 %collective-permute-start.9 = (bf16[128,1536]{1,0:T(8,128)(2,1)S(1)}, bf16[128,1536]{1,0:T(8,128)(2,1)S(1)}, u32[]{:S(2)}, u32[]{:S(2)}) collective-permute-start(bf16[128,1536]{1,0:T(8,128)(2,1)S(1)} %collective-permute-done.6.refs_6_), channel_id=1, source_target_pairs={{0,8},{8,0},{16,24},{24,16},{1,9},{9,1},{17,25},{25,17},{2,10},{10... | collective-permute-start | bytes 1179656 | tf_op jit(solution)/shard_map/ppermute | solution.py:21
  86.2 4.4 %collective-permute-start.10 = (bf16[128,1536]{1,0:T(8,128)(2,1)S(1)}, bf16[128,1536]{1,0:T(8,128)(2,1)S(1)}, u32[]{:S(2)}, u32[]{:S(2)}) collective-permute-start(bf16[128,1536]{1,0:T(8,128)(2,1)S(1)} %collective-permute-done.7.refs_8_), channel_id=1, source_target_pairs={{0,8},{8,0},{16,24},{24,16},{1,9},{9,1},{17,25},{25,17},{2,10},{10... | collective-permute-start | bytes 1179656 | tf_op jit(solution)/shard_map/ppermute | solution.py:21
  88.1 3.7 %collective-permute-start.11 = (bf16[128,1536]{1,0:T(8,128)(2,1)S(1)}, bf16[128,1536]{1,0:T(8,128)(2,1)S(1)}, u32[]{:S(2)}, u32[]{:S(2)}) collective-permute-start(bf16[128,1536]{1,0:T(8,128)(2,1)S(1)} %collective-permute-done.8.refs_10_), channel_id=1, source_target_pairs={{0,8},{8,0},{16,24},{24,16},{1,9},{9,1},{17,25},{25,17},{2,10},{10... | collective-permute-start | bytes 1179656 | tf_op jit(solution)/shard_map/ppermute | solution.py:21
  91.9 0.9 copy-start.1
  95.7 0.6 copy-start.2
  96.3 38.1 %copy-start.4 = (f32[1536]{0:T(1024)S(1)}, f32[1536]{0:T(1024)}, u32[]{:S(2)}) copy-start(f32[1536]{0:T(1024)} %param.5) | copy-start | bytes 18436
  96.3 17.1 %collective-permute-start.15 = (bf16[48,1536]{1,0:T(8,128)(2,1)}, bf16[48,1536]{1,0:T(8,128)(2,1)S(1)}, u32[]{:S(2)}, u32[]{:S(2)}) collective-permute-start(bf16[48,1536]{1,0:T(8,128)(2,1)} %get-tuple-element.33), channel_id=1, source_target_pairs={{0,64},{32,96},{64,128},{96,160},{128,192},{160,224},{192,256},{22... | collective-permute-start | bytes 442376 | tf_op jit(solution)/shard_map/ppermute | solution.py:133
  98.4 18.9 %collective-permute-start.12 = (bf16[48,1536]{1,0:T(8,128)(2,1)}, bf16[48,1536]{1,0:T(8,128)(2,1)S(1)}, u32[]{:S(2)}, u32[]{:S(2)}) collective-permute-start(bf16[48,1536]{1,0:T(8,128)(2,1)} %copy-done.2), channel_id=1, source_target_pairs={{0,448},{32,480},{64,0},{96,32},{128,64},{160,96},{192,128},{224,1... | collective-permute-start | bytes 442376 | tf_op jit(solution)/shard_map/ppermute | solution.py:133
  113.4 10.2 %collective-permute-start.16 = (bf16[48,1536]{1,0:T(8,128)(2,1)S(1)}, bf16[48,1536]{1,0:T(8,128)(2,1)S(1)}, u32[]{:S(2)}, u32[]{:S(2)}) collective-permute-start(bf16[48,1536]{1,0:T(8,128)(2,1)S(1)} %add_convert_fusion.2), channel_id=1, source_target_pairs={{0,64},{32,96},{64,128},{96,160},{128,192},{160,224},{192,256},{22... | collective-permute-start | bytes 442376 | tf_op jit(solution)/shard_map/ppermute | solution.py:133
  117.3 8.3 %collective-permute-start.13 = (bf16[48,1536]{1,0:T(8,128)(2,1)S(1)}, bf16[48,1536]{1,0:T(8,128)(2,1)S(1)}, u32[]{:S(2)}, u32[]{:S(2)}) collective-permute-start(bf16[48,1536]{1,0:T(8,128)(2,1)S(1)} %add_convert_fusion.4), channel_id=1, source_target_pairs={{0,448},{32,480},{64,0},{96,32},{128,64},{160,96},{192,128},{224,1... | collective-permute-start | bytes 442376 | tf_op jit(solution)/shard_map/ppermute | solution.py:133
  123.7 8.1 %collective-permute-start.17 = (bf16[48,1536]{1,0:T(8,128)(2,1)S(1)}, bf16[48,1536]{1,0:T(8,128)(2,1)S(1)}, u32[]{:S(2)}, u32[]{:S(2)}) collective-permute-start(bf16[48,1536]{1,0:T(8,128)(2,1)S(1)} %add_convert_fusion.1), channel_id=1, source_target_pairs={{0,64},{32,96},{64,128},{96,160},{128,192},{160,224},{192,256},{22... | collective-permute-start | bytes 442376 | tf_op jit(solution)/shard_map/ppermute | solution.py:133
  125.7 23.2 %collective-permute-start.14 = (bf16[48,1536]{1,0:T(8,128)(2,1)S(1)}, bf16[48,1536]{1,0:T(8,128)(2,1)S(1)}, u32[]{:S(2)}, u32[]{:S(2)}) collective-permute-start(bf16[48,1536]{1,0:T(8,128)(2,1)S(1)} %add_convert_fusion.3), channel_id=1, source_target_pairs={{0,448},{32,480},{64,0},{96,32},{128,64},{160,96},{192,128},{224,1... | collective-permute-start | bytes 442376 | tf_op jit(solution)/shard_map/ppermute | solution.py:133
  131.8 17.1 %collective-permute-start.18 = (bf16[48,1536]{1,0:T(8,128)(2,1)S(1)}, bf16[48,1536]{1,0:T(8,128)(2,1)S(1)}, u32[]{:S(2)}, u32[]{:S(2)}) collective-permute-start(bf16[48,1536]{1,0:T(8,128)(2,1)S(1)} %convert_add_fusion.1), channel_id=1, source_target_pairs={{0,64},{32,96},{64,128},{96,160},{128,192},{160,224},{192,256},{22... | collective-permute-start | bytes 442376 | tf_op jit(solution)/shard_map/ppermute | solution.py:133
Sparse Core Ops, SparseCore 0:
  83.9 46.6 reduce-scatter.1

commit v3 on v2

--- a/solution.py
+++ b/solution.py
@@ -55,7 +55,7 @@
     return pl.pallas_call(
         lambda *refs: weight_kernel(scale, rows, *refs),
         out_shape=[jax.ShapeDtypeStruct((rows, hidden), BF)] * count,
-        in_specs=[whole] * (len(left) + len(right)),
+        in_specs=[pl.BlockSpec()] * len(left) + [whole] * len(right),
         out_specs=[whole] * count,
         compiler_params=pltpu.CompilerParams(vmem_limit_bytes=8 * 1024 * 1024),
         cost_estimate=pl.CostEstimate(
@@ -107,7 +107,7 @@
 
     left = [columns(0, 0)]
     for bits in GROUP:
-        left.append(swap(columns(bits // 16, bits % 2), "dp", n_dp, bits))
+        left.append(columns(bits // 16, bits % 2))
     from_x, *left = lax.optimization_barrier((from_x, *left))
 
     pre = kept + from_x.astype(F32)
@@ -120,7 +120,9 @@
 
     in_order = jnp.where(core == 0, jnp.concatenate(right, axis=0), jnp.concatenate(right[::-1], axis=0))
     back = dot(in_order, in_weight, ((1,), (1,)))
-    back, *arrived = lax.optimization_barrier((back, *arrived))
+    back, *left = lax.optimization_barrier((back, *left))
+    left[1:] = [swap(piece, "dp", n_dp, bits) for piece, bits in zip(left[1:], GROUP)]
+    arrived[2], *left = lax.optimization_barrier((arrived[2], *left))
     dnormed = lax.psum_scatter(back, "my", scatter_dimension=0, tiled=True)
     own_rows = tok_rows // n_my
 

time: 158 us -> 160 us (1.013)
  waiting for transfers between devices: 19.8 us -> 27.9 us
  starting transfers between devices: 64.3 us -> 60 us
  blocking collectives: 32.2 us -> 28.4 us
  other arithmetic: 9.61 us -> 11.4 us
    ppermute x7, waiting for transfers between devices: 4.3 us -> 10.9 us  [hop(): return lax.ppermute(value.astype(BF), 'dp', perm).astype(F32)]
    ppermute x7, starting transfers between devices: 33.4 us -> 28.2 us  [hop(): return lax.ppermute(value.astype(BF), 'dp', perm).astype(F32)]
    psum x1, blocking collectives: 11.6 us -> 7.77 us  [body(): lax.psum((jnp.sum(dcentred, axis=1), jnp.sum(dcentred * centred_rows, axi...]
  transfers between devices with their start and end apart: 20 -> 20, of which waited for: 10 -> 7; matrix products, arithmetic and copies ran while one was open for 8% -> 8% of each run, Pallas kernels for 2% -> 2%
where the time goes in v3:
time: 160 us; the launch traced here: 159 us
  starting transfers between devices  60 us (38%)
  blocking collectives  28.4 us (18%)
  waiting for transfers between devices  27.9 us (17%)
  between operations  14.5 us (9%)
  other arithmetic  11.4 us (7%)
  matrix products  11.1 us (7%)
  Pallas kernels  2.86 us (2%)
  local copies, waits for them, and re-layouts  2.66 us (2%)
    ppermute x12, starting transfers between devices, swap(): return lax.ppermute(value, axis, [(i, i ^ bits) for i in range(size)])  31.7 us
    ppermute x7, starting transfers between devices, hop(): return lax.ppermute(value.astype(BF), 'dp', perm).astype(F32)  28.2 us
    psum x1, blocking collectives, body(): lax.psum((jnp.sum(values, axis=1), jnp.sum(values * values, axis=1)), 'mx')  20.7 us
    ppermute x12, waiting for transfers between devices, swap(): return lax.ppermute(value, axis, [(i, i ^ bits) for i in range(size)])  16.9 us
    dot_general x3, matrix products, dot(): return lax.dot_general(a, b, (dims, ((), ())), preferred_element_type=F32)  11.1 us
    ppermute x7, waiting for transfers between devices, hop(): return lax.ppermute(value.astype(BF), 'dp', perm).astype(F32)  10.9 us
    psum x1, blocking collectives, body(): lax.psum((jnp.sum(dcentred, axis=1), jnp.sum(dcentred * centred_rows, axi...  7.77 us
  transfers between devices with their start and end apart: 20, of which 7 were waited for; matrix products, arithmetic and copies ran while one was open for 8% of the time, Pallas kernels for 2%

profile of v3, /device:TPU:1, one launch (start us, length us, event | category | flops | bytes accessed | tf_op | source)
XLA Modules:
  0.0 158.8 jit_solution(3637679287248891141)
XLA Ops:
  7.2 0.0 reduce-scatter.2.cloned.1.call-start
  7.2 1.5 convert_reduce_fusion
  8.7 20.7 %all-reduce.1 = (f32[256]{0:T(256)S(1)}, f32[256]{0:T(256)S(1)}) all-reduce(f32[256]{0:T(256)S(1)} %get-tuple-element.53, f32[256]{0:T(256)S(1)} %get-tuple-element.52), channel_id=1, replica_groups=mesh['dp'=32,'mx'=4,'my'=8] {'mx'}, use_global_device_ids=true, to_apply=%region_3.4 | all-reduce | flops 512 | bytes 4096 | tf_op jit(solution)/shard_map/psum | solution.py:86
  29.4 2.6 %fusion = (f32[256,1536]{1,0:T(8,128)}, bf16[256,1536]{1,0:T(8,128)(2,1)S(1)}) fusion(bf16[256,1536]{1,0:T(8,128)(2,1)} %param.4, f32[256]{0:T(256)S(1)} %get-tuple-element.69, f32[256]{0:T(256)S(1)} %get-tuple-element.68, f32[1536]{0:T(1024)} %param.5), kind=kLoop, calls=%fused_computation.12 | loop fusion | flops 1966080 | bytes 3153920 | tf_op jit(solution)/shard_map/mul | solution.py:89
  32.0 3.1 %convolution_convert_fusion = bf16[128,1536]{1,0:T(8,128)(2,1)S(1)} fusion(bf16[1536,1536]{1,0:T(8,128)(2,1)} %param.6, bf16[256,1536]{1,0:T(8,128)(2,1)S(1)} %get-tuple-element.61, s32[]{:T(128)S(6)} %select_n.65), kind=kOutput, calls=%fused_computation | convolution fusion | flops 604176384 | bytes 5505028 | tf_op jit(solution)/shard_map/dot_general | solution.py:29
  35.2 2.7 %collective-permute-start = (bf16[128,1536]{1,0:T(8,128)(2,1)S(1)}, bf16[128,1536]{1,0:T(8,128)(2,1)S(1)}, u32[]{:S(2)}, u32[]{:S(2)}) collective-permute-start(bf16[128,1536]{1,0:T(8,128)(2,1)S(1)} %convolution_convert_fusion), channel_id=1, source_target_pairs={{0,8},{8,0},{16,24},{24,16},{1,9},{9,1},{17,25},{25,17},{2,10},{10... | collective-permute-start | bytes 1179656 | tf_op jit(solution)/shard_map/ppermute | solution.py:21
  37.8 3.1 %fusion.17 = f32[128,1536]{1,0:T(8,128)S(1)} fusion(bf16[1536,1536]{1,0:T(8,128)(2,1)} %param.6, bf16[256,1536]{1,0:T(8,128)(2,1)S(1)} %get-tuple-element.61, s32[]{:T(128)S(6)} %select_n.64), kind=kOutput, calls=%fused_computation.36 | convolution fusion | flops 603979776 | bytes 5898244 | tf_op jit(solution)/shard_map/dot_general | solution.py:29
  41.0 0.0 collective-permute-done
  41.0 0.8 fusion.15
  41.8 1.9 %collective-permute-start.1 = (bf16[128,1536]{1,0:T(8,128)(2,1)}, bf16[128,1536]{1,0:T(8,128)(2,1)}, u32[]{:S(2)}, u32[]{:S(2)}) collective-permute-start(bf16[128,1536]{1,0:T(8,128)(2,1)} %fusion.15), channel_id=1, source_target_pairs={{0,16},{8,24},{16,0},{24,8},{1,17},{9,25},{17,1},{25,9},{2,18},{10... | collective-permute-start | bytes 1179656 | tf_op jit(solution)/shard_map/ppermute | solution.py:21
  43.7 0.1 dynamic-slice_bitcast_fusion.1
  43.9 0.1 pad_maximum_fusion
  43.9 0.3 copy.8
  44.2 0.0 copy-start.3
  44.2 1.1 fusion.19
  45.3 10.9 %collective-permute-done.1 = bf16[128,1536]{1,0:T(8,128)(2,1)} collective-permute-done((bf16[128,1536]{1,0:T(8,128)(2,1)}, bf16[128,1536]{1,0:T(8,128)(2,1)}, u32[]{:S(2)}, u32[]{:S(2)}) %collective-permute-start.1) | collective-permute-done | bytes 393248 | tf_op jit(solution)/shard_map/ppermute | solution.py:21
  56.2 1.4 fusion.7.refs_4_
  57.7 2.7 %collective-permute-start.3 = (bf16[128,1536]{1,0:T(8,128)(2,1)S(1)}, bf16[128,1536]{1,0:T(8,128)(2,1)S(1)}, u32[]{:S(2)}, u32[]{:S(2)}) collective-permute-start(bf16[128,1536]{1,0:T(8,128)(2,1)S(1)} %fusion.7.refs_4_), channel_id=1, source_target_pairs={{0,8},{8,0},{16,24},{24,16},{1,9},{9,1},{17,25},{25,17},{2,10},{10... | collective-permute-start | bytes 1179656 | tf_op jit(solution)/shard_map/ppermute | solution.py:21
  60.4 1.9 %collective-permute-start.9 = (bf16[128,1536]{1,0:T(8,128)(2,1)S(1)}, bf16[128,1536]{1,0:T(8,128)(2,1)S(1)}, u32[]{:S(2)}, u32[]{:S(2)}) collective-permute-start(bf16[128,1536]{1,0:T(8,128)(2,1)S(1)} %fusion.7.refs_4_), channel_id=1, source_target_pairs={{0,32},{32,0},{64,96},{96,64},{128,160},{160,128},{192,224},{224,1... | collective-permute-start | bytes 1179656 | tf_op jit(solution)/shard_map/ppermute | solution.py:21
  62.3 1.9 %collective-permute-start.7 = (bf16[128,1536]{1,0:T(8,128)(2,1)S(1)}, bf16[128,1536]{1,0:T(8,128)(2,1)S(1)}, u32[]{:S(2)}, u32[]{:S(2)}) collective-permute-start(bf16[128,1536]{1,0:T(8,128)(2,1)S(1)} %fusion.7.refs_4_), channel_id=1, source_target_pairs={{0,512},{32,544},{64,576},{96,608},{128,640},{160,672},{192,704},{... | collective-permute-start | bytes 1179656 | tf_op jit(solution)/shard_map/ppermute | solution.py:21
  64.3 4.5 %collective-permute-start.2 = (bf16[128,1536]{1,0:T(8,128)(2,1)S(1)}, bf16[128,1536]{1,0:T(8,128)(2,1)S(1)}, u32[]{:S(2)}, u32[]{:S(2)}) collective-permute-start(bf16[128,1536]{1,0:T(8,128)(2,1)S(1)} %fusion.7.refs_4_), channel_id=1, source_target_pairs={{0,544},{32,512},{64,608},{96,576},{128,672},{160,640},{192,736},{... | collective-permute-start | bytes 1179656 | tf_op jit(solution)/shard_map/ppermute | solution.py:21
  68.8 0.0 collective-permute-done.3.refs_5_
  68.8 4.9 %fusion.8 = f32[256,1536]{1,0:T(8,128)} fusion(bf16[1536,1536]{1,0:T(8,128)(2,1)} %param.6, bf16[128,1536]{1,0:T(8,128)(2,1)S(1)} %collective-permute-done.3.refs_5_, bf16[128,1536]{1,0:T(8,128)(2,1)S(1)} %fusion.7.refs_4_, pred[]{:T(512)S(6)} %eq.7), kind=kOutput, calls=%fused_computation.24 | convolution fusion | flops 1211498496 | bytes 7077889 | tf_op jit(solution)/shard_map/dot_general | solution.py:29
  73.7 1.9 %collective-permute-start.4 = (bf16[384,256]{1,0:T(8,128)(2,1)}, bf16[384,256]{1,0:T(8,128)(2,1)S(1)}, u32[]{:S(2)}, u32[]{:S(2)}) collective-permute-start(bf16[384,256]{1,0:T(8,128)(2,1)} %bitcast.4), channel_id=1, source_target_pairs={{0,512},{32,544},{64,576},{96,608},{128,640},{160,672},{192,704},{... | collective-permute-start | bytes 589832 | tf_op jit(solution)/shard_map/ppermute | solution.py:21
  75.6 2.2 %collective-permute-start.5 = (bf16[384,256]{1,0:T(8,128)(2,1)}, bf16[384,256]{1,0:T(8,128)(2,1)S(1)}, u32[]{:S(2)}, u32[]{:S(2)}) collective-permute-start(bf16[384,256]{1,0:T(8,128)(2,1)} %bitcast.5), channel_id=1, source_target_pairs={{0,32},{32,0},{64,96},{96,64},{128,160},{160,128},{192,224},{224,1... | collective-permute-start | bytes 589832 | tf_op jit(solution)/shard_map/ppermute | solution.py:21
  77.8 0.0 collective-permute-done.9.refs_8_
  77.8 4.3 %collective-permute-start.6 = (bf16[384,256]{1,0:T(8,128)(2,1)}, bf16[384,256]{1,0:T(8,128)(2,1)S(1)}, u32[]{:S(2)}, u32[]{:S(2)}) collective-permute-start(bf16[384,256]{1,0:T(8,128)(2,1)} %bitcast.16), channel_id=1, source_target_pairs={{0,544},{32,512},{64,608},{96,576},{128,672},{160,640},{192,736},{... | collective-permute-start | bytes 589832 | tf_op jit(solution)/shard_map/ppermute | solution.py:21
  82.1 0.0 reduce-scatter.2.cloned.1.call-update
  82.1 1.3 collective-permute-done.7.refs_6_
  83.4 3.1 %collective-permute-start.10 = (bf16[128,1536]{1,0:T(8,128)(2,1)S(1)}, bf16[128,1536]{1,0:T(8,128)(2,1)S(1)}, u32[]{:S(2)}, u32[]{:S(2)}) collective-permute-start(bf16[128,1536]{1,0:T(8,128)(2,1)S(1)} %collective-permute-done.9.refs_8_), channel_id=1, source_target_pairs={{0,8},{8,0},{16,24},{24,16},{1,9},{9,1},{17,25},{25,17},{2,10},{10... | collective-permute-start | bytes 1179656 | tf_op jit(solution)/shard_map/ppermute | solution.py:21
  86.5 0.0 collective-permute-done.2.refs_10_
  86.5 1.9 %collective-permute-start.8 = (bf16[128,1536]{1,0:T(8,128)(2,1)S(1)}, bf16[128,1536]{1,0:T(8,128)(2,1)S(1)}, u32[]{:S(2)}, u32[]{:S(2)}) collective-permute-start(bf16[128,1536]{1,0:T(8,128)(2,1)S(1)} %collective-permute-done.7.refs_6_), channel_id=1, source_target_pairs={{0,8},{8,0},{16,24},{24,16},{1,9},{9,1},{17,25},{25,17},{2,10},{10... | collective-permute-start | bytes 1179656 | tf_op jit(solution)/shard_map/ppermute | solution.py:21
  88.4 3.4 %collective-permute-done.4.refs_1_ = bf16[384,256]{1,0:T(8,128)(2,1)S(1)} collective-permute-done((bf16[384,256]{1,0:T(8,128)(2,1)}, bf16[384,256]{1,0:T(8,128)(2,1)S(1)}, u32[]{:S(2)}, u32[]{:S(2)}) %collective-permute-start.4) | collective-permute-done | bytes 196640 | tf_op jit(solution)/shard_map/ppermute | solution.py:21
  91.8 0.0 collective-permute-done.5.refs_2_
  91.8 0.0 collective-permute-done.6.refs_3_
  91.8 0.7 copy-done
  92.5 2.7 %collective-permute-start.11 = (bf16[128,1536]{1,0:T(8,128)(2,1)S(1)}, bf16[128,1536]{1,0:T(8,128)(2,1)S(1)}, u32[]{:S(2)}, u32[]{:S(2)}) collective-permute-start(bf16[128,1536]{1,0:T(8,128)(2,1)S(1)} %collective-permute-done.2.refs_10_), channel_id=1, source_target_pairs={{0,8},{8,0},{16,24},{24,16},{1,9},{9,1},{17,25},{25,17},{2,10},{10... | collective-permute-start | bytes 1179656 | tf_op jit(solution)/shard_map/ppermute | solution.py:21
  95.2 0.0 collective-permute-done.10.refs_9_
  95.2 0.0 collective-permute-done.8.refs_7_
  95.2 1.3 collective-permute-done.11.refs_11_
  96.5 0.9 copy-done.1
  97.4 2.9 %shard_map.59 = (bf16[48,1536]{1,0:T(8,128)(2,1)S(1)}, bf16[48,1536]{1,0:T(8,128)(2,1)S(1)}, bf16[48,1536]{1,0:T(8,128)(2,1)S(1)}, bf16[48,1536]{1,0:T(8,128)(2,...) custom-call(bf16[384,256]{1,0:T(8,128)(2,1)S(1)} %bitcast.14, ...), custom_call_target="tpu_custom_call" | custom-call | flops 1207959552 | bytes 5111808 | tf_op jit(solution)/shard_map/pallas_call | solution.py:55
  100.3 0.6 copy-done.2
  101.0 2.0 %collective-permute-start.15 = (bf16[48,1536]{1,0:T(8,128)(2,1)}, bf16[48,1536]{1,0:T(8,128)(2,1)S(1)}, u32[]{:S(2)}, u32[]{:S(2)}) collective-permute-start(bf16[48,1536]{1,0:T(8,128)(2,1)} %get-tuple-element.45), channel_id=1, source_target_pairs={{0,64},{32,96},{64,128},{96,160},{128,192},{160,224},{192,256},{22... | collective-permute-start | bytes 442376 | tf_op jit(solution)/shard_map/ppermute | solution.py:135
  103.0 0.1 dynamic_slice.34
  103.1 9.1 %collective-permute-start.12 = (bf16[48,1536]{1,0:T(8,128)(2,1)}, bf16[48,1536]{1,0:T(8,128)(2,1)S(1)}, u32[]{:S(2)}, u32[]{:S(2)}) collective-permute-start(bf16[48,1536]{1,0:T(8,128)(2,1)} %copy-done.2), channel_id=1, source_target_pairs={{0,448},{32,480},{64,0},{96,32},{128,64},{160,96},{192,128},{224,1... | collective-permute-start | bytes 442376 | tf_op jit(solution)/shard_map/ppermute | solution.py:135
  112.2 5.3 %collective-permute-done.15 = bf16[48,1536]{1,0:T(8,128)(2,1)S(1)} collective-permute-done((bf16[48,1536]{1,0:T(8,128)(2,1)}, bf16[48,1536]{1,0:T(8,128)(2,1)S(1)}, u32[]{:S(2)}, u32[]{:S(2)}) %collective-permute-start.15) | collective-permute-done | bytes 147488 | tf_op jit(solution)/shard_map/ppermute | solution.py:135
  117.6 1.9 %collective-permute-start.16 = (bf16[48,1536]{1,0:T(8,128)(2,1)S(1)}, bf16[48,1536]{1,0:T(8,128)(2,1)S(1)}, u32[]{:S(2)}, u32[]{:S(2)}) collective-permute-start(bf16[48,1536]{1,0:T(8,128)(2,1)S(1)} %add_convert_fusion.2), channel_id=1, source_target_pairs={{0,64},{32,96},{64,128},{96,160},{128,192},{160,224},{192,256},{22... | collective-permute-start | bytes 442376 | tf_op jit(solution)/shard_map/ppermute | solution.py:135
  119.5 0.0 collective-permute-done.12
  119.6 5.5 %collective-permute-start.13 = (bf16[48,1536]{1,0:T(8,128)(2,1)S(1)}, bf16[48,1536]{1,0:T(8,128)(2,1)S(1)}, u32[]{:S(2)}, u32[]{:S(2)}) collective-permute-start(bf16[48,1536]{1,0:T(8,128)(2,1)S(1)} %add_convert_fusion.4), channel_id=1, source_target_pairs={{0,448},{32,480},{64,0},{96,32},{128,64},{160,96},{192,128},{224,1... | collective-permute-start | bytes 442376 | tf_op jit(solution)/shard_map/ppermute | solution.py:135
  125.0 3.5 %collective-permute-done.16 = bf16[48,1536]{1,0:T(8,128)(2,1)S(1)} collective-permute-done((bf16[48,1536]{1,0:T(8,128)(2,1)S(1)}, bf16[48,1536]{1,0:T(8,128)(2,1)S(1)}, u32[]{:S(2)}, u32[]{:S(2)}) %collective-permute-start.16) | collective-permute-done | bytes 147488 | tf_op jit(solution)/shard_map/ppermute | solution.py:135
  128.5 2.1 %collective-permute-start.17 = (bf16[48,1536]{1,0:T(8,128)(2,1)S(1)}, bf16[48,1536]{1,0:T(8,128)(2,1)S(1)}, u32[]{:S(2)}, u32[]{:S(2)}) collective-permute-start(bf16[48,1536]{1,0:T(8,128)(2,1)S(1)} %add_convert_fusion.1), channel_id=1, source_target_pairs={{0,64},{32,96},{64,128},{96,160},{128,192},{160,224},{192,256},{22... | collective-permute-start | bytes 442376 | tf_op jit(solution)/shard_map/ppermute | solution.py:135
  130.7 0.0 collective-permute-done.13
  130.8 5.2 %collective-permute-start.14 = (bf16[48,1536]{1,0:T(8,128)(2,1)S(1)}, bf16[48,1536]{1,0:T(8,128)(2,1)S(1)}, u32[]{:S(2)}, u32[]{:S(2)}) collective-permute-start(bf16[48,1536]{1,0:T(8,128)(2,1)S(1)} %add_convert_fusion.3), channel_id=1, source_target_pairs={{0,448},{32,480},{64,0},{96,32},{128,64},{160,96},{192,128},{224,1... | collective-permute-start | bytes 442376 | tf_op jit(solution)/shard_map/ppermute | solution.py:135
  136.0 2.2 %collective-permute-done.17 = bf16[48,1536]{1,0:T(8,128)(2,1)S(1)} collective-permute-done((bf16[48,1536]{1,0:T(8,128)(2,1)S(1)}, bf16[48,1536]{1,0:T(8,128)(2,1)S(1)}, u32[]{:S(2)}, u32[]{:S(2)}) %collective-permute-start.17) | collective-permute-done | bytes 147488 | tf_op jit(solution)/shard_map/ppermute | solution.py:135
  138.2 0.0 reduce-scatter.2.cloned.1.call-done
  138.2 2.3 %collective-permute-start.18 = (bf16[48,1536]{1,0:T(8,128)(2,1)S(1)}, bf16[48,1536]{1,0:T(8,128)(2,1)S(1)}, u32[]{:S(2)}, u32[]{:S(2)}) collective-permute-start(bf16[48,1536]{1,0:T(8,128)(2,1)S(1)} %convert_add_fusion.1), channel_id=1, source_target_pairs={{0,64},{32,96},{64,128},{96,160},{128,192},{160,224},{192,256},{22... | collective-permute-start | bytes 442376 | tf_op jit(solution)/shard_map/ppermute | solution.py:135
  140.5 0.0 copy-done.4
  140.5 1.2 multiply_reduce_fusion.1
  141.7 7.8 %all-reduce = (f32[32]{0:T(128)S(1)}, f32[32]{0:T(128)S(1)}) all-reduce(f32[32]{0:T(128)S(1)} %get-tuple-element.55, f32[32]{0:T(128)S(1)} %get-tuple-element.54), channel_id=1, replica_groups=mesh['dp'=32,'mx'=4,'my'=8] {'mx'}, use_global_device_ids=true, to_apply=%region_8.9 | all-reduce | flops 64 | bytes 512 | tf_op jit(solution)/shard_map/psum | solution.py:148
  149.5 1.8 %multiply_convert_fusion.1 = bf16[32,1536]{1,0:T(8,128)(2,1)} fusion(f32[256,1536]{1,0:T(8,128)} %get-tuple-element.60, s32[]{:T(128)S(6)} %select_n.77, f32[32,1536]{1,0:T(8,128)} %reduce-scatter.2.cloned.1.call-done, f32[32]{0:T(128)S(1)} %get-tuple-element.70, f32[32]{0:T(128)S(1)} %get-tuple-element.71, f32[1536]{0:T(1024)S(1)} %copy-done.4, ...), kind=kLoop, calls=%fused_computation.48 | loop fusion | flops 294912 | bytes 498052 | tf_op jit(solution)/shard_map/convert_element_type | solution.py:154
  151.2 0.0 collective-permute-done.14
  151.2 0.0 collective-permute-done.18
  151.2 0.7 fusion.23
  (12 shorter events, 0.2 us)
Async XLA Ops:
  7.2 131.1 %reduce-scatter.2.cloned.1.call-start = ((), (), s32[]{:S(2)}) async-start(), calls=%async_computation.1 | async-start | bytes 1769472 | tf_op jit(solution)/shard_map/reduce_scatter | solution.py:126
  35.2 5.8 %collective-permute-start = (bf16[128,1536]{1,0:T(8,128)(2,1)S(1)}, bf16[128,1536]{1,0:T(8,128)(2,1)S(1)}, u32[]{:S(2)}, u32[]{:S(2)}) collective-permute-start(bf16[128,1536]{1,0:T(8,128)(2,1)S(1)} %convolution_convert_fusion), channel_id=1, source_target_pairs={{0,8},{8,0},{16,24},{24,16},{1,9},{9,1},{17,25},{25,17},{2,10},{10... | collective-permute-start | bytes 1179656 | tf_op jit(solution)/shard_map/ppermute | solution.py:21
  41.8 14.4 %collective-permute-start.1 = (bf16[128,1536]{1,0:T(8,128)(2,1)}, bf16[128,1536]{1,0:T(8,128)(2,1)}, u32[]{:S(2)}, u32[]{:S(2)}) collective-permute-start(bf16[128,1536]{1,0:T(8,128)(2,1)} %fusion.15), channel_id=1, source_target_pairs={{0,16},{8,24},{16,0},{24,8},{1,17},{9,25},{17,1},{25,9},{2,18},{10... | collective-permute-start | bytes 1179656 | tf_op jit(solution)/shard_map/ppermute | solution.py:21
  44.2 12.1 %copy-start.3 = (bf16[256,1536]{1,0:T(8,128)(2,1)S(1)}, bf16[256,1536]{1,0:T(8,128)(2,1)}, u32[]{:S(2)}) copy-start(bf16[256,1536]{1,0:T(8,128)(2,1)} %param.7) | copy-start | bytes 2359300
  57.7 11.1 %collective-permute-start.3 = (bf16[128,1536]{1,0:T(8,128)(2,1)S(1)}, bf16[128,1536]{1,0:T(8,128)(2,1)S(1)}, u32[]{:S(2)}, u32[]{:S(2)}) collective-permute-start(bf16[128,1536]{1,0:T(8,128)(2,1)S(1)} %fusion.7.refs_4_), channel_id=1, source_target_pairs={{0,8},{8,0},{16,24},{24,16},{1,9},{9,1},{17,25},{25,17},{2,10},{10... | collective-permute-start | bytes 1179656 | tf_op jit(solution)/shard_map/ppermute | solution.py:21
  60.4 17.4 %collective-permute-start.9 = (bf16[128,1536]{1,0:T(8,128)(2,1)S(1)}, bf16[128,1536]{1,0:T(8,128)(2,1)S(1)}, u32[]{:S(2)}, u32[]{:S(2)}) collective-permute-start(bf16[128,1536]{1,0:T(8,128)(2,1)S(1)} %fusion.7.refs_4_), channel_id=1, source_target_pairs={{0,32},{32,0},{64,96},{96,64},{128,160},{160,128},{192,224},{224,1... | collective-permute-start | bytes 1179656 | tf_op jit(solution)/shard_map/ppermute | solution.py:21
  62.3 21.1 %collective-permute-start.7 = (bf16[128,1536]{1,0:T(8,128)(2,1)S(1)}, bf16[128,1536]{1,0:T(8,128)(2,1)S(1)}, u32[]{:S(2)}, u32[]{:S(2)}) collective-permute-start(bf16[128,1536]{1,0:T(8,128)(2,1)S(1)} %fusion.7.refs_4_), channel_id=1, source_target_pairs={{0,512},{32,544},{64,576},{96,608},{128,640},{160,672},{192,704},{... | collective-permute-start | bytes 1179656 | tf_op jit(solution)/shard_map/ppermute | solution.py:21
  64.3 22.2 %collective-permute-start.2 = (bf16[128,1536]{1,0:T(8,128)(2,1)S(1)}, bf16[128,1536]{1,0:T(8,128)(2,1)S(1)}, u32[]{:S(2)}, u32[]{:S(2)}) collective-permute-start(bf16[128,1536]{1,0:T(8,128)(2,1)S(1)} %fusion.7.refs_4_), channel_id=1, source_target_pairs={{0,544},{32,512},{64,608},{96,576},{128,672},{160,640},{192,736},{... | collective-permute-start | bytes 1179656 | tf_op jit(solution)/shard_map/ppermute | solution.py:21
  73.7 18.1 %collective-permute-start.4 = (bf16[384,256]{1,0:T(8,128)(2,1)}, bf16[384,256]{1,0:T(8,128)(2,1)S(1)}, u32[]{:S(2)}, u32[]{:S(2)}) collective-permute-start(bf16[384,256]{1,0:T(8,128)(2,1)} %bitcast.4), channel_id=1, source_target_pairs={{0,512},{32,544},{64,576},{96,608},{128,640},{160,672},{192,704},{... | collective-permute-start | bytes 589832 | tf_op jit(solution)/shard_map/ppermute | solution.py:21
  75.6 16.2 %collective-permute-start.5 = (bf16[384,256]{1,0:T(8,128)(2,1)}, bf16[384,256]{1,0:T(8,128)(2,1)S(1)}, u32[]{:S(2)}, u32[]{:S(2)}) collective-permute-start(bf16[384,256]{1,0:T(8,128)(2,1)} %bitcast.5), channel_id=1, source_target_pairs={{0,32},{32,0},{64,96},{96,64},{128,160},{160,128},{192,224},{224,1... | collective-permute-start | bytes 589832 | tf_op jit(solution)/shard_map/ppermute | solution.py:21
  77.8 14.0 %collective-permute-start.6 = (bf16[384,256]{1,0:T(8,128)(2,1)}, bf16[384,256]{1,0:T(8,128)(2,1)S(1)}, u32[]{:S(2)}, u32[]{:S(2)}) collective-permute-start(bf16[384,256]{1,0:T(8,128)(2,1)} %bitcast.16), channel_id=1, source_target_pairs={{0,544},{32,512},{64,608},{96,576},{128,672},{160,640},{192,736},{... | collective-permute-start | bytes 589832 | tf_op jit(solution)/shard_map/ppermute | solution.py:21
  83.4 11.8 %collective-permute-start.10 = (bf16[128,1536]{1,0:T(8,128)(2,1)S(1)}, bf16[128,1536]{1,0:T(8,128)(2,1)S(1)}, u32[]{:S(2)}, u32[]{:S(2)}) collective-permute-start(bf16[128,1536]{1,0:T(8,128)(2,1)S(1)} %collective-permute-done.9.refs_8_), channel_id=1, source_target_pairs={{0,8},{8,0},{16,24},{24,16},{1,9},{9,1},{17,25},{25,17},{2,10},{10... | collective-permute-start | bytes 1179656 | tf_op jit(solution)/shard_map/ppermute | solution.py:21
  86.5 8.7 %collective-permute-start.8 = (bf16[128,1536]{1,0:T(8,128)(2,1)S(1)}, bf16[128,1536]{1,0:T(8,128)(2,1)S(1)}, u32[]{:S(2)}, u32[]{:S(2)}) collective-permute-start(bf16[128,1536]{1,0:T(8,128)(2,1)S(1)} %collective-permute-done.7.refs_6_), channel_id=1, source_target_pairs={{0,8},{8,0},{16,24},{24,16},{1,9},{9,1},{17,25},{25,17},{2,10},{10... | collective-permute-start | bytes 1179656 | tf_op jit(solution)/shard_map/ppermute | solution.py:21
  91.8 0.7 copy-start
  92.5 4.0 %collective-permute-start.11 = (bf16[128,1536]{1,0:T(8,128)(2,1)S(1)}, bf16[128,1536]{1,0:T(8,128)(2,1)S(1)}, u32[]{:S(2)}, u32[]{:S(2)}) collective-permute-start(bf16[128,1536]{1,0:T(8,128)(2,1)S(1)} %collective-permute-done.2.refs_10_), channel_id=1, source_target_pairs={{0,8},{8,0},{16,24},{24,16},{1,9},{9,1},{17,25},{25,17},{2,10},{10... | collective-permute-start | bytes 1179656 | tf_op jit(solution)/shard_map/ppermute | solution.py:21
  96.5 0.9 copy-start.1
  100.3 0.6 copy-start.2
  101.0 39.6 %copy-start.4 = (f32[1536]{0:T(1024)S(1)}, f32[1536]{0:T(1024)}, u32[]{:S(2)}) copy-start(f32[1536]{0:T(1024)} %param.5) | copy-start | bytes 18436
  101.0 16.6 %collective-permute-start.15 = (bf16[48,1536]{1,0:T(8,128)(2,1)}, bf16[48,1536]{1,0:T(8,128)(2,1)S(1)}, u32[]{:S(2)}, u32[]{:S(2)}) collective-permute-start(bf16[48,1536]{1,0:T(8,128)(2,1)} %get-tuple-element.45), channel_id=1, source_target_pairs={{0,64},{32,96},{64,128},{96,160},{128,192},{160,224},{192,256},{22... | collective-permute-start | bytes 442376 | tf_op jit(solution)/shard_map/ppermute | solution.py:135
  103.1 16.4 %collective-permute-start.12 = (bf16[48,1536]{1,0:T(8,128)(2,1)}, bf16[48,1536]{1,0:T(8,128)(2,1)S(1)}, u32[]{:S(2)}, u32[]{:S(2)}) collective-permute-start(bf16[48,1536]{1,0:T(8,128)(2,1)} %copy-done.2), channel_id=1, source_target_pairs={{0,448},{32,480},{64,0},{96,32},{128,64},{160,96},{192,128},{224,1... | collective-permute-start | bytes 442376 | tf_op jit(solution)/shard_map/ppermute | solution.py:135
  117.6 10.9 %collective-permute-start.16 = (bf16[48,1536]{1,0:T(8,128)(2,1)S(1)}, bf16[48,1536]{1,0:T(8,128)(2,1)S(1)}, u32[]{:S(2)}, u32[]{:S(2)}) collective-permute-start(bf16[48,1536]{1,0:T(8,128)(2,1)S(1)} %add_convert_fusion.2), channel_id=1, source_target_pairs={{0,64},{32,96},{64,128},{96,160},{128,192},{160,224},{192,256},{22... | collective-permute-start | bytes 442376 | tf_op jit(solution)/shard_map/ppermute | solution.py:135
  119.6 11.1 %collective-permute-start.13 = (bf16[48,1536]{1,0:T(8,128)(2,1)S(1)}, bf16[48,1536]{1,0:T(8,128)(2,1)S(1)}, u32[]{:S(2)}, u32[]{:S(2)}) collective-permute-start(bf16[48,1536]{1,0:T(8,128)(2,1)S(1)} %add_convert_fusion.4), channel_id=1, source_target_pairs={{0,448},{32,480},{64,0},{96,32},{128,64},{160,96},{192,128},{224,1... | collective-permute-start | bytes 442376 | tf_op jit(solution)/shard_map/ppermute | solution.py:135
  128.5 9.6 %collective-permute-start.17 = (bf16[48,1536]{1,0:T(8,128)(2,1)S(1)}, bf16[48,1536]{1,0:T(8,128)(2,1)S(1)}, u32[]{:S(2)}, u32[]{:S(2)}) collective-permute-start(bf16[48,1536]{1,0:T(8,128)(2,1)S(1)} %add_convert_fusion.1), channel_id=1, source_target_pairs={{0,64},{32,96},{64,128},{96,160},{128,192},{160,224},{192,256},{22... | collective-permute-start | bytes 442376 | tf_op jit(solution)/shard_map/ppermute | solution.py:135
  130.8 20.5 %collective-permute-start.14 = (bf16[48,1536]{1,0:T(8,128)(2,1)S(1)}, bf16[48,1536]{1,0:T(8,128)(2,1)S(1)}, u32[]{:S(2)}, u32[]{:S(2)}) collective-permute-start(bf16[48,1536]{1,0:T(8,128)(2,1)S(1)} %add_convert_fusion.3), channel_id=1, source_target_pairs={{0,448},{32,480},{64,0},{96,32},{128,64},{160,96},{192,128},{224,1... | collective-permute-start | bytes 442376 | tf_op jit(solution)/shard_map/ppermute | solution.py:135
  138.2 13.0 %collective-permute-start.18 = (bf16[48,1536]{1,0:T(8,128)(2,1)S(1)}, bf16[48,1536]{1,0:T(8,128)(2,1)S(1)}, u32[]{:S(2)}, u32[]{:S(2)}) collective-permute-start(bf16[48,1536]{1,0:T(8,128)(2,1)S(1)} %convert_add_fusion.1), channel_id=1, source_target_pairs={{0,64},{32,96},{64,128},{96,160},{128,192},{160,224},{192,256},{22... | collective-permute-start | bytes 442376 | tf_op jit(solution)/shard_map/ppermute | solution.py:135
Sparse Core Ops, SparseCore 0:
  82.3 41.4 reduce-scatter.1

commit v4 on v2

v4 whole, which is shorter than its diff:
```python
import math

import jax
import jax.numpy as jnp
from jax import lax
from jax.experimental import pallas as pl
from jax.experimental.pallas import tpu as pltpu
from jax.sharding import PartitionSpec as P

epsilon = 1e-06
BF = jnp.bfloat16
F32 = jnp.float32


def gelu_slope(pre):
    cdf = 0.5 * (1.0 + jax.scipy.special.erf(pre * (1.0 / math.sqrt(2.0))))
    return cdf + pre * jnp.exp(-0.5 * pre * pre) * (1.0 / math.sqrt(2.0 * math.pi))


def swap(value, axis, size, bits):
    return lax.ppermute(value, axis, [(i, i ^ bits) for i in range(size)])


def rows_at(value, start, count):
    return lax.dynamic_slice_in_dim(value, start, count, 0)


def dot(a, b, dims=((1,), (0,))):
    return lax.dot_general(a, b, (dims, ((), ())), preferred_element_type=F32)


def weight_kernel(scale, rows, groups, *refs):
    out = refs[-1]
    hidden = out.shape[1]
    tile = 256

    @pl.loop(0, hidden // tile)
    def _(step):
        cols = pl.ds(pl.multiple_of(step * tile, tile), tile)
        total = None
        for (left, first), pieces in groups:
            tokens = [refs[i][start : start + count, cols] for i, start, count in pieces]
            term = dot(refs[left][first : first + rows], jnp.concatenate(tokens, axis=0))
            total = term if total is None else total + term
        out[:, cols] = (total * scale).astype(BF)


def weight_term(refs, groups, scale, rows):
    hidden = refs[-1].shape[1]
    tokens = sum(count for _, pieces in groups for _, _, count in pieces)
    whole = pl.BlockSpec(memory_space=pltpu.VMEM)
    return pl.pallas_call(
        lambda *r: weight_kernel(scale, rows, groups, *r),
        out_shape=jax.ShapeDtypeStruct((rows, hidden), BF),
        in_specs=[pl.BlockSpec() if r.shape[1] != hidden else whole for r in refs],
        compiler_params=pltpu.CompilerParams(vmem_limit_bytes=8 * 1024 * 1024),
        cost_estimate=pl.CostEstimate(
            flops=2 * rows * tokens * hidden,
            bytes_accessed=2 * (rows * (tokens + hidden) + tokens * hidden),
            transcendentals=0,
        ),
    )(*refs)


Z = 16
ZH = Z // 2


def body(tokens_in, norm_gain, in_weight, cotangent):
    tok_rows, width = tokens_in.shape
    hidden = in_weight.shape[1]
    n_dp, n_mx, n_my = lax.axis_size("dp"), lax.axis_size("mx"), lax.axis_size("my")
    d_all = width * n_mx
    half = tok_rows // 2
    dp, my = lax.axis_index("dp"), lax.axis_index("my")
    core = lax.axis_index("mx") % 2
    x_lo, zl = dp // Z, dp % 2
    block = width // n_dp

    values = tokens_in.astype(F32)
    sum_one, sum_two = lax.psum((jnp.sum(values, axis=1), jnp.sum(values * values, axis=1)), "mx")
    row_mean = sum_one / d_all
    inv_std = lax.rsqrt(sum_two / d_all - row_mean * row_mean + epsilon)
    centred = (values - row_mean[:, None]) * inv_std[:, None]
    normed = (centred * norm_gain[None, :]).astype(BF)

    mine = rows_at(normed, core * half, half)
    other = rows_at(normed, (1 - core) * half, half)
    sent = dot(other, in_weight).astype(BF)
    from_core = swap(sent, "mx", n_mx, 1)
    kept = lax.optimization_barrier(dot(mine, in_weight)) + from_core.astype(F32)
    from_x = swap(kept.astype(BF), "mx", n_mx, 2)

    turned = jnp.concatenate([mine.T, other.T], axis=1).reshape(2, ZH, 2, block, tok_rows)
    columns = ZH * block

    def for_zl(index):
        return lax.dynamic_slice_in_dim(turned, index, 1, 2).reshape(2 * columns, tok_rows)

    here = for_zl(zl)
    near = swap(for_zl(1 - zl), "dp", n_dp, 1)
    from_x, near = lax.optimization_barrier((from_x, near))

    pre = kept + from_x.astype(F32)
    cot = rows_at(cotangent, core * half, half)
    dpre = (cot.astype(F32) * gelu_slope(pre)).astype(BF)

    def across(value, bits):
        n = n_dp * n_mx
        return lax.ppermute(value, ("dp", "mx"), [(i, i ^ (bits * n_mx + 2)) for i in range(n)])

    part = half // 2
    far = []
    for bits in (16, 17):
        far += [swap(dpre[:part], "dp", n_dp, bits), across(dpre[part:], bits)]
    near_dpre = swap(dpre, "dp", n_dp, 1)
    own_pair = swap(dpre, "mx", n_mx, 1)

    theirs = (1 - x_lo) * columns
    beyond = jnp.concatenate([rows_at(here, theirs, columns), rows_at(near, theirs, columns)], axis=0)
    beyond, own_pair = lax.optimization_barrier((beyond, own_pair))
    beyond = swap(beyond, "dp", n_dp, 16)
    own_rows = tok_rows // n_my
    right = [dpre, own_pair]
    in_order = jnp.where(core == 0, jnp.concatenate(right, axis=0), jnp.concatenate(right[::-1], axis=0))
    in_order = in_order.reshape(2, 2, 2, own_rows, hidden).transpose(2, 1, 0, 3, 4).reshape(tok_rows, hidden)
    keep = dot(in_order, in_weight, ((1,), (1,)))

    keep, near_dpre, *far = lax.optimization_barrier((keep, near_dpre, *far))
    far = jnp.concatenate(far, axis=0)
    far, beyond = lax.optimization_barrier((far, beyond))
    far_pair = swap(far, "mx", n_mx, 1)
    near_pair = swap(near_dpre, "mx", n_mx, 1)

    refs = [rows_at(here, x_lo * columns, columns), rows_at(near, x_lo * columns, columns), beyond]
    refs += [dpre, own_pair, near_dpre, near_pair, far, far_pair]
    groups = [
        ((0, 0), [(3, 0, half), (4, 0, half)]),
        ((1, 0), [(5, 0, half), (6, 0, half)]),
        ((2, 0), [(7, 0, half), (8, 0, half)]),
        ((2, columns), [(7, half, half), (8, half, half)]),
    ]
    term = weight_term(refs, groups, 1.0 / math.sqrt(n_dp * tok_rows), columns)
    teams = [[x * Z + h * 2 + l for h in range(ZH)] for x in range(2) for l in range(2)]
    grad_weight = lax.psum_scatter(
        term, "dp", scatter_dimension=0, axis_index_groups=teams, tiled=True
    ).reshape(1, 1, block, hidden)

    for bit in (1, 2, 4):
        rows = keep.shape[0] // 2
        mine_first = my // bit % 2 * rows
        give = rows_at(keep, rows - mine_first, rows).astype(BF)
        keep = rows_at(keep, mine_first, rows) + swap(give, "my", n_my, bit).astype(F32)
    dnormed = keep

    first_row = my * own_rows
    centred_rows = rows_at(centred, first_row, own_rows)
    inv_rows = rows_at(inv_std, first_row, own_rows)
    dcentred = dnormed * norm_gain[None, :]
    total_a, total_b = lax.psum(
        (jnp.sum(dcentred, axis=1), jnp.sum(dcentred * centred_rows, axis=1)), "mx"
    )
    grad_tokens = inv_rows[:, None] * (
        dcentred - total_a[:, None] / d_all - centred_rows * (total_b[:, None] / d_all)
    )
    return (grad_weight, grad_tokens.astype(BF))


def solution(mesh):
    return jax.shard_map(
        body,
        mesh=mesh,
        in_specs=(P("dp", "mx"), P("mx"), P("mx", "my"), P("dp", "my")),
        out_specs=(P("mx", "dp", None, "my"), P(("dp", "my"), "mx")),
        check_vma=False,
    )
```

time: 158 us -> 167 us (1.057)
  the two profiles are of different devices: /device:TPU:1 before, /device:TPU:12 now
where the time goes in v4:
time: 167 us; the launch traced here: 166 us
  waiting for transfers between devices  54.6 us (33%)
  starting transfers between devices  51.3 us (31%)
  blocking collectives  16.3 us (10%)
  between operations  14.5 us (9%)
  matrix products  11.9 us (7%)
  other arithmetic  10.8 us (6%)
  Pallas kernels  4.29 us (3%)
  local copies, waits for them, and re-layouts  2.61 us (2%)
    ppermute x13, starting transfers between devices, swap(): return lax.ppermute(value, axis, [(i, i ^ bits) for i in range(size)])  45.2 us
    ppermute x13, waiting for transfers between devices, swap(): return lax.ppermute(value, axis, [(i, i ^ bits) for i in range(size)])  35.9 us
    reduce_scatter x1, waiting for transfers between devices, body(): lax.psum_scatter(term, 'dp', scatter_dimension=0, axis_index_groups=teams...  18.7 us
    dot_general x3, matrix products, dot(): return lax.dot_general(a, b, (dims, ((), ())), preferred_element_type=F32)  11.9 us
    psum x1, blocking collectives, body(): lax.psum((jnp.sum(dcentred, axis=1), jnp.sum(dcentred * centred_rows, axi...  8.95 us
    psum x1, blocking collectives, body(): lax.psum((jnp.sum(values, axis=1), jnp.sum(values * values, axis=1)), 'mx')  7.38 us
    ppermute x2, starting transfers between devices, across(): lax.ppermute(value, ('dp', 'mx'), [(i, i ^ bits * n_mx + 2) for i in rang...  6.02 us
    pallas_call x1, Pallas kernels, weight_term(): pl.pallas_call(lambda *r: weight_kernel(scale, rows, groups, *r), out_sha...  4.29 us
  transfers between devices with their start and end apart: 16, of which 8 were waited for; matrix products, arithmetic and copies ran while one was open for 10% of the time, Pallas kernels for 3%

profile of v4, /device:TPU:12, one launch (start us, length us, event | category | flops | bytes accessed | tf_op | source)
XLA Modules:
  0.0 166.3 jit_solution(12150191889526930723)
XLA Ops:
  7.2 0.0 reduce-scatter.2.cloned.1.call-start
  7.2 1.5 convert_reduce_fusion
  8.7 7.4 %all-reduce.1 = (f32[256]{0:T(256)S(1)}, f32[256]{0:T(256)S(1)}) all-reduce(f32[256]{0:T(256)S(1)} %get-tuple-element.27, f32[256]{0:T(256)S(1)} %get-tuple-element.26), channel_id=1, replica_groups=mesh['dp'=32,'mx'=4,'my'=8] {'mx'}, use_global_device_ids=true, to_apply=%region_3.4 | all-reduce | flops 512 | bytes 4096 | tf_op jit(solution)/shard_map/psum | solution.py:81
  16.1 2.6 %fusion = (f32[256,1536]{1,0:T(8,128)}, bf16[256,1536]{1,0:T(8,128)(2,1)S(1)}) fusion(bf16[256,1536]{1,0:T(8,128)(2,1)} %param.4, f32[256]{0:T(256)S(1)} %get-tuple-element.47, f32[256]{0:T(256)S(1)} %get-tuple-element.46, f32[1536]{0:T(1024)} %param.5), kind=kLoop, calls=%fused_computation.4 | loop fusion | flops 1966080 | bytes 3153920 | tf_op jit(solution)/shard_map/mul | solution.py:84
  18.7 3.9 %convolution_convert_fusion = bf16[128,1536]{1,0:T(8,128)(2,1)} fusion(bf16[1536,1536]{1,0:T(8,128)(2,1)} %param.6, bf16[256,1536]{1,0:T(8,128)(2,1)S(1)} %get-tuple-element.35, s32[]{:T(128)S(6)} %select_n.91), kind=kOutput, calls=%fused_computation | convolution fusion | flops 604176384 | bytes 5505028 | tf_op jit(solution)/shard_map/dot_general | solution.py:29
  22.6 1.9 %collective-permute-start = (bf16[128,1536]{1,0:T(8,128)(2,1)}, bf16[128,1536]{1,0:T(8,128)(2,1)S(1)}, u32[]{:S(2)}, u32[]{:S(2)}) collective-permute-start(bf16[128,1536]{1,0:T(8,128)(2,1)} %convolution_convert_fusion), channel_id=1, source_target_pairs={{0,8},{8,0},{16,24},{24,16},{1,9},{9,1},{17,25},{25,17},{2,10},{10... | collective-permute-start | bytes 1179656 | tf_op jit(solution)/shard_map/ppermute | solution.py:21
  24.5 0.1 dynamic-slice_bitcast_fusion.1
  24.6 0.1 pad_maximum_fusion
  24.7 0.3 copy.8
  24.9 0.1 constant_dynamic-slice_fusion.3
  25.0 4.3 %collective-permute-start.2 = (bf16[768,256]{1,0:T(8,128)(2,1)S(1)}, bf16[768,256]{1,0:T(8,128)(2,1)S(1)}, u32[]{:S(2)}, u32[]{:S(2)}) collective-permute-start(bf16[768,256]{1,0:T(8,128)(2,1)S(1)} %bitcast.20), channel_id=1, source_target_pairs={{0,32},{32,0},{64,96},{96,64},{128,160},{160,128},{192,224},{224,1... | collective-permute-start | bytes 1179656 | tf_op jit(solution)/shard_map/ppermute | solution.py:21
  29.3 3.1 %fusion.10 = f32[128,1536]{1,0:T(8,128)S(1)} fusion(bf16[1536,1536]{1,0:T(8,128)(2,1)} %param.6, bf16[256,1536]{1,0:T(8,128)(2,1)S(1)} %get-tuple-element.35, s32[]{:T(128)S(6)} %select_n.90), kind=kOutput, calls=%fused_computation.26 | convolution fusion | flops 603979776 | bytes 5898244 | tf_op jit(solution)/shard_map/dot_general | solution.py:29
  32.4 0.0 collective-permute-done
  32.4 0.8 fusion.8
  33.3 5.0 %collective-permute-start.1 = (bf16[128,1536]{1,0:T(8,128)(2,1)}, bf16[128,1536]{1,0:T(8,128)(2,1)S(1)}, u32[]{:S(2)}, u32[]{:S(2)}) collective-permute-start(bf16[128,1536]{1,0:T(8,128)(2,1)} %fusion.8), channel_id=1, source_target_pairs={{0,16},{8,24},{16,0},{24,8},{1,17},{9,25},{17,1},{25,9},{2,18},{10... | collective-permute-start | bytes 1179656 | tf_op jit(solution)/shard_map/ppermute | solution.py:21
  38.3 0.8 collective-permute-done.2
  39.1 9.0 %collective-permute-done.1 = bf16[128,1536]{1,0:T(8,128)(2,1)S(1)} collective-permute-done((bf16[128,1536]{1,0:T(8,128)(2,1)}, bf16[128,1536]{1,0:T(8,128)(2,1)S(1)}, u32[]{:S(2)}, u32[]{:S(2)}) %collective-permute-start.1) | collective-permute-done | bytes 393248 | tf_op jit(solution)/shard_map/ppermute | solution.py:21
  48.1 1.4 fusion.7.r_3_
  49.5 1.9 %collective-permute-start.3 = (bf16[128,1536]{1,0:T(8,128)(2,1)S(1)}, bf16[128,1536]{1,0:T(8,128)(2,1)S(1)}, u32[]{:S(2)}, u32[]{:S(2)}) collective-permute-start(bf16[128,1536]{1,0:T(8,128)(2,1)S(1)} %fusion.7.r_3_), channel_id=1, source_target_pairs={{0,8},{8,0},{16,24},{24,16},{1,9},{9,1},{17,25},{25,17},{2,10},{10... | collective-permute-start | bytes 1179656 | tf_op jit(solution)/shard_map/ppermute | solution.py:21
  51.5 3.8 %collective-permute-start.8 = (bf16[64,1536]{1,0:T(8,128)(2,1)S(1)}, bf16[64,1536]{1,0:T(8,128)(2,1)S(1)}, u32[]{:S(2)}, u32[]{:S(2)}) collective-permute-start(bf16[64,1536]{1,0:T(8,128)(2,1)S(1)} %get-tuple-element.40), channel_id=1, source_target_pairs={{0,560},{8,568},{16,544},{24,552},{32,528},{40,536},{48,512},{56,5... | collective-permute-start | bytes 589832 | tf_op jit(solution)/shard_map/ppermute | solution.py:110
  55.3 2.2 %collective-permute-start.6 = (bf16[64,1536]{1,0:T(8,128)(2,1)S(1)}, bf16[64,1536]{1,0:T(8,128)(2,1)S(1)}, u32[]{:S(2)}, u32[]{:S(2)}) collective-permute-start(bf16[64,1536]{1,0:T(8,128)(2,1)S(1)} %get-tuple-element.40), channel_id=1, source_target_pairs={{0,528},{8,536},{16,512},{24,520},{32,560},{40,568},{48,544},{56,5... | collective-permute-start | bytes 589832 | tf_op jit(solution)/shard_map/ppermute | solution.py:110
  57.5 6.0 %collective-permute-start.7 = (bf16[64,1536]{1,0:T(8,128)(2,1)S(1)}, bf16[64,1536]{1,0:T(8,128)(2,1)S(1)}, u32[]{:S(2)}, u32[]{:S(2)}) collective-permute-start(bf16[64,1536]{1,0:T(8,128)(2,1)S(1)} %get-tuple-element.41), channel_id=1, source_target_pairs={{0,544},{32,512},{64,608},{96,576},{128,672},{160,640},{192,736},{... | collective-permute-start | bytes 589832 | tf_op jit(solution)/shard_map/ppermute | solution.py:21
  63.5 1.9 %collective-permute-start.5 = (bf16[64,1536]{1,0:T(8,128)(2,1)S(1)}, bf16[64,1536]{1,0:T(8,128)(2,1)S(1)}, u32[]{:S(2)}, u32[]{:S(2)}) collective-permute-start(bf16[64,1536]{1,0:T(8,128)(2,1)S(1)} %get-tuple-element.41), channel_id=1, source_target_pairs={{0,512},{32,544},{64,576},{96,608},{128,640},{160,672},{192,704},{... | collective-permute-start | bytes 589832 | tf_op jit(solution)/shard_map/ppermute | solution.py:21
  65.5 0.0 collective-permute-done.3.r_4_
  65.5 2.5 %collective-permute-start.4 = (bf16[128,1536]{1,0:T(8,128)(2,1)S(1)}, bf16[128,1536]{1,0:T(8,128)(2,1)S(1)}, u32[]{:S(2)}, u32[]{:S(2)}) collective-permute-start(bf16[128,1536]{1,0:T(8,128)(2,1)S(1)} %fusion.7.r_3_), channel_id=1, source_target_pairs={{0,32},{32,0},{64,96},{96,64},{128,160},{160,128},{192,224},{224,1... | collective-permute-start | bytes 1179656 | tf_op jit(solution)/shard_map/ppermute | solution.py:21
  68.0 0.2 maximum_select_fusion
  68.2 0.1 copy.9
  68.2 0.0 collective-permute-done.8
  68.2 3.6 %collective-permute-start.9 = (bf16[768,256]{1,0:T(8,128)(2,1)S(1)}, bf16[768,256]{1,0:T(8,128)(2,1)S(1)}, u32[]{:S(2)}, u32[]{:S(2)}) collective-permute-start(bf16[768,256]{1,0:T(8,128)(2,1)S(1)} %pad_maximum_fusion.2), channel_id=1, source_target_pairs={{0,512},{32,544},{64,576},{96,608},{128,640},{160,672},{192,704},{... | collective-permute-start | bytes 1179656 | tf_op jit(solution)/shard_map/ppermute | solution.py:21
  71.9 4.9 %fusion.16 = f32[256,1536]{1,0:T(8,128)} fusion(bf16[256,1536]{1,0:T(8,128)(2,1)S(1)} %bitcast.19, bf16[1536,1536]{1,0:T(8,128)(2,1)} %param.6), kind=kOutput, calls=%fused_computation.47 | convolution fusion | flops 1207959552 | bytes 7077888 | tf_op jit(solution)/shard_map/dot_general | solution.py:29
  76.8 0.0 collective-permute-done.6
  76.8 0.0 collective-permute-done.7
  76.8 0.0 collective-permute-done.5
  76.8 1.3 collective-permute-done.4.r_5_
  78.1 0.1 pad_maximum_fusion.1.r_7_
  78.1 3.0 %collective-permute-done.9.r_2_ = bf16[768,256]{1,0:T(8,128)(2,1)S(1)} collective-permute-done((bf16[768,256]{1,0:T(8,128)(2,1)S(1)}, bf16[768,256]{1,0:T(8,128)(2,1)S(1)}, u32[]{:S(2)}, u32[]{:S(2)}) %collective-permute-start.9) | collective-permute-done | bytes 393248 | tf_op jit(solution)/shard_map/ppermute | solution.py:21
  81.1 1.9 %collective-permute-start.11 = (bf16[256,1536]{1,0:T(8,128)(2,1)S(1)}, bf16[256,1536]{1,0:T(8,128)(2,1)S(1)}, u32[]{:S(2)}, u32[]{:S(2)}) collective-permute-start(bf16[256,1536]{1,0:T(8,128)(2,1)S(1)} %pad_maximum_fusion.1.r_7_), channel_id=1, source_target_pairs={{0,8},{8,0},{16,24},{24,16},{1,9},{9,1},{17,25},{25,17},{2,10},{10... | collective-permute-start | bytes 2359304 | tf_op jit(solution)/shard_map/ppermute | solution.py:21
  83.1 2.4 %collective-permute-start.10 = (bf16[128,1536]{1,0:T(8,128)(2,1)S(1)}, bf16[128,1536]{1,0:T(8,128)(2,1)}, u32[]{:S(2)}, u32[]{:S(2)}) collective-permute-start(bf16[128,1536]{1,0:T(8,128)(2,1)S(1)} %collective-permute-done.4.r_5_), channel_id=1, source_target_pairs={{0,8},{8,0},{16,24},{24,16},{1,9},{9,1},{17,25},{25,17},{2,10},{10... | collective-permute-start | bytes 1179656 | tf_op jit(solution)/shard_map/ppermute | solution.py:21
  85.5 1.9 %dynamic-slice_convert_fusion = bf16[128,1536]{1,0:T(8,128)(2,1)} fusion(f32[256,1536]{1,0:T(8,128)} %fusion.16, s32[]{:T(128)S(6)} %select_n.104), kind=kLoop, calls=%fused_computation.18 | loop fusion | bytes 786436 | tf_op jit(solution)/shard_map/convert_element_type | solution.py:152
  87.4 10.0 %collective-permute-start.12 = (bf16[128,1536]{1,0:T(8,128)(2,1)}, bf16[128,1536]{1,0:T(8,128)(2,1)}, u32[]{:S(2)}, u32[]{:S(2)}) collective-permute-start(bf16[128,1536]{1,0:T(8,128)(2,1)} %dynamic-slice_convert_fusion), channel_id=1, source_target_pairs={{0,1},{1,0},{2,3},{3,2},{4,5},{5,4},{6,7},{7,6},{8,9},{9,8},{10,11... | collective-permute-start | bytes 1179656 | tf_op jit(solution)/shard_map/ppermute | solution.py:21
  97.5 0.0 collective-permute-done.10.r_6_
  97.5 0.0 collective-permute-done.11.r_8_
  97.5 4.3 %shard_map.59 = bf16[384,1536]{1,0:T(8,128)(2,1)} custom-call(bf16[384,256]{1,0:T(8,128)(2,1)S(1)} %get-tuple-element.43.r_0_, bf16[384,256]{1,0:T(8,128)(2,1)S(1)} %get-tuple-element.45.r_1_, bf16[768,256]{1,0:T(8,128)(2,1)S(1)} %collective-permute-done.9.r_2_, bf16[128,1536]{1,0:T(8,128)(2,1)S(1)} %fusion.7.r_3_, ...), custom_call_target="tpu_custom_call" | custom-call | flops 1207959552 | bytes 5111808 | tf_op jit(solution)/shard_map/pallas_call | solution.py:52
  101.8 0.0 reduce-scatter.2.cloned.1.call-update
  101.8 0.0 copy-start
  101.8 5.2 %collective-permute-done.12 = bf16[128,1536]{1,0:T(8,128)(2,1)} collective-permute-done((bf16[128,1536]{1,0:T(8,128)(2,1)}, bf16[128,1536]{1,0:T(8,128)(2,1)}, u32[]{:S(2)}, u32[]{:S(2)}) %collective-permute-start.12) | collective-permute-done | bytes 393248 | tf_op jit(solution)/shard_map/ppermute | solution.py:21
  107.0 1.3 convert_add_fusion
  108.4 1.9 %collective-permute-start.13 = (bf16[64,1536]{1,0:T(8,128)(2,1)S(1)}, bf16[64,1536]{1,0:T(8,128)(2,1)S(1)}, u32[]{:S(2)}, u32[]{:S(2)}) collective-permute-start(bf16[64,1536]{1,0:T(8,128)(2,1)S(1)} %dynamic-slice_convert_fusion.1), channel_id=1, source_target_pairs={{0,2},{1,3},{2,0},{3,1},{4,6},{5,7},{6,4},{7,5},{8,10},{9,11},{10,... | collective-permute-start | bytes 589832 | tf_op jit(solution)/shard_map/ppermute | solution.py:21
  110.3 8.2 %collective-permute-done.13 = bf16[64,1536]{1,0:T(8,128)(2,1)S(1)} collective-permute-done((bf16[64,1536]{1,0:T(8,128)(2,1)S(1)}, bf16[64,1536]{1,0:T(8,128)(2,1)S(1)}, u32[]{:S(2)}, u32[]{:S(2)}) %collective-permute-start.13) | collective-permute-done | bytes 196640 | tf_op jit(solution)/shard_map/ppermute | solution.py:21
  118.7 1.9 %collective-permute-start.14 = (bf16[32,1536]{1,0:T(8,128)(2,1)S(1)}, bf16[32,1536]{1,0:T(8,128)(2,1)S(1)}, u32[]{:S(2)}, u32[]{:S(2)}) collective-permute-start(bf16[32,1536]{1,0:T(8,128)(2,1)S(1)} %dynamic-slice_convert_fusion.2), channel_id=1, source_target_pairs={{0,4},{1,5},{2,6},{3,7},{4,0},{5,1},{6,2},{7,3},{8,12},{9,13},{10,... | collective-permute-start | bytes 294920 | tf_op jit(solution)/shard_map/ppermute | solution.py:21
  120.6 0.1 dynamic_slice.60
  120.7 8.4 %collective-permute-done.14 = bf16[32,1536]{1,0:T(8,128)(2,1)S(1)} collective-permute-done((bf16[32,1536]{1,0:T(8,128)(2,1)S(1)}, bf16[32,1536]{1,0:T(8,128)(2,1)S(1)}, u32[]{:S(2)}, u32[]{:S(2)}) %collective-permute-start.14) | collective-permute-done | bytes 98336 | tf_op jit(solution)/shard_map/ppermute | solution.py:21
  129.1 0.0 copy-done
  129.1 1.1 fusion.12
  130.2 9.0 %all-reduce = (f32[32]{0:T(128)S(1)}, f32[32]{0:T(128)S(1)}) all-reduce(f32[32]{0:T(128)S(1)} %get-tuple-element.29, f32[32]{0:T(128)S(1)} %get-tuple-element.28), channel_id=1, replica_groups=mesh['dp'=32,'mx'=4,'my'=8] {'mx'}, use_global_device_ids=true, to_apply=%region_8.9 | all-reduce | flops 64 | bytes 512 | tf_op jit(solution)/shard_map/psum | solution.py:160
  139.1 1.7 %multiply_convert_fusion.1 = bf16[32,1536]{1,0:T(8,128)(2,1)} fusion(f32[256,1536]{1,0:T(8,128)} %get-tuple-element.34, s32[]{:T(128)S(6)} %select_n.101, f32[32]{0:T(128)S(1)} %get-tuple-element.48, f32[32]{0:T(128)S(1)} %get-tuple-element.49, f32[32]{0:T(128)S(1)} %dynamic_slice.60, f32[1536]{0:T(1024)S(1)} %copy-done, ...), kind=kLoop, calls=%fused_computation.29 | loop fusion | flops 393216 | bytes 596360 | tf_op jit(solution)/shard_map/convert_element_type | solution.py:166
  140.8 18.7 %reduce-scatter.2.cloned.1.call-done = bf16[48,1536]{1,0:T(8,128)(2,1)} async-done(((bf16[384,1536]{1,0:T(8,128)(2,1)}), bf16[48,1536]{1,0:T(8,128)(2,1)}) %reduce-scatter.2.cloned.1.call-update) | async-done | bytes 147472 | tf_op jit(solution)/shard_map/reduce_scatter | solution.py:145
  (9 shorter events, 0.2 us)
Async XLA Ops:
  7.2 152.3 %reduce-scatter.2.cloned.1.call-start = ((), (), s32[]{:S(2)}) async-start(), calls=%async_computation.1 | async-start | bytes 1327104 | tf_op jit(solution)/shard_map/reduce_scatter | solution.py:145
  22.6 9.8 %collective-permute-start = (bf16[128,1536]{1,0:T(8,128)(2,1)}, bf16[128,1536]{1,0:T(8,128)(2,1)S(1)}, u32[]{:S(2)}, u32[]{:S(2)}) collective-permute-start(bf16[128,1536]{1,0:T(8,128)(2,1)} %convolution_convert_fusion), channel_id=1, source_target_pairs={{0,8},{8,0},{16,24},{24,16},{1,9},{9,1},{17,25},{25,17},{2,10},{10... | collective-permute-start | bytes 1179656 | tf_op jit(solution)/shard_map/ppermute | solution.py:21
  25.0 14.1 %collective-permute-start.2 = (bf16[768,256]{1,0:T(8,128)(2,1)S(1)}, bf16[768,256]{1,0:T(8,128)(2,1)S(1)}, u32[]{:S(2)}, u32[]{:S(2)}) collective-permute-start(bf16[768,256]{1,0:T(8,128)(2,1)S(1)} %bitcast.20), channel_id=1, source_target_pairs={{0,32},{32,0},{64,96},{96,64},{128,160},{160,128},{192,224},{224,1... | collective-permute-start | bytes 1179656 | tf_op jit(solution)/shard_map/ppermute | solution.py:21
  33.3 14.8 %collective-permute-start.1 = (bf16[128,1536]{1,0:T(8,128)(2,1)}, bf16[128,1536]{1,0:T(8,128)(2,1)S(1)}, u32[]{:S(2)}, u32[]{:S(2)}) collective-permute-start(bf16[128,1536]{1,0:T(8,128)(2,1)} %fusion.8), channel_id=1, source_target_pairs={{0,16},{8,24},{16,0},{24,8},{1,17},{9,25},{17,1},{25,9},{2,18},{10... | collective-permute-start | bytes 1179656 | tf_op jit(solution)/shard_map/ppermute | solution.py:21
  49.5 16.0 %collective-permute-start.3 = (bf16[128,1536]{1,0:T(8,128)(2,1)S(1)}, bf16[128,1536]{1,0:T(8,128)(2,1)S(1)}, u32[]{:S(2)}, u32[]{:S(2)}) collective-permute-start(bf16[128,1536]{1,0:T(8,128)(2,1)S(1)} %fusion.7.r_3_), channel_id=1, source_target_pairs={{0,8},{8,0},{16,24},{24,16},{1,9},{9,1},{17,25},{25,17},{2,10},{10... | collective-permute-start | bytes 1179656 | tf_op jit(solution)/shard_map/ppermute | solution.py:21
  51.5 16.7 %collective-permute-start.8 = (bf16[64,1536]{1,0:T(8,128)(2,1)S(1)}, bf16[64,1536]{1,0:T(8,128)(2,1)S(1)}, u32[]{:S(2)}, u32[]{:S(2)}) collective-permute-start(bf16[64,1536]{1,0:T(8,128)(2,1)S(1)} %get-tuple-element.40), channel_id=1, source_target_pairs={{0,560},{8,568},{16,544},{24,552},{32,528},{40,536},{48,512},{56,5... | collective-permute-start | bytes 589832 | tf_op jit(solution)/shard_map/ppermute | solution.py:110
  55.3 21.5 %collective-permute-start.6 = (bf16[64,1536]{1,0:T(8,128)(2,1)S(1)}, bf16[64,1536]{1,0:T(8,128)(2,1)S(1)}, u32[]{:S(2)}, u32[]{:S(2)}) collective-permute-start(bf16[64,1536]{1,0:T(8,128)(2,1)S(1)} %get-tuple-element.40), channel_id=1, source_target_pairs={{0,528},{8,536},{16,512},{24,520},{32,560},{40,568},{48,544},{56,5... | collective-permute-start | bytes 589832 | tf_op jit(solution)/shard_map/ppermute | solution.py:110
  57.5 19.3 %collective-permute-start.7 = (bf16[64,1536]{1,0:T(8,128)(2,1)S(1)}, bf16[64,1536]{1,0:T(8,128)(2,1)S(1)}, u32[]{:S(2)}, u32[]{:S(2)}) collective-permute-start(bf16[64,1536]{1,0:T(8,128)(2,1)S(1)} %get-tuple-element.41), channel_id=1, source_target_pairs={{0,544},{32,512},{64,608},{96,576},{128,672},{160,640},{192,736},{... | collective-permute-start | bytes 589832 | tf_op jit(solution)/shard_map/ppermute | solution.py:21
  63.5 13.3 %collective-permute-start.5 = (bf16[64,1536]{1,0:T(8,128)(2,1)S(1)}, bf16[64,1536]{1,0:T(8,128)(2,1)S(1)}, u32[]{:S(2)}, u32[]{:S(2)}) collective-permute-start(bf16[64,1536]{1,0:T(8,128)(2,1)S(1)} %get-tuple-element.41), channel_id=1, source_target_pairs={{0,512},{32,544},{64,576},{96,608},{128,640},{160,672},{192,704},{... | collective-permute-start | bytes 589832 | tf_op jit(solution)/shard_map/ppermute | solution.py:21
  65.5 12.6 %collective-permute-start.4 = (bf16[128,1536]{1,0:T(8,128)(2,1)S(1)}, bf16[128,1536]{1,0:T(8,128)(2,1)S(1)}, u32[]{:S(2)}, u32[]{:S(2)}) collective-permute-start(bf16[128,1536]{1,0:T(8,128)(2,1)S(1)} %fusion.7.r_3_), channel_id=1, source_target_pairs={{0,32},{32,0},{64,96},{96,64},{128,160},{160,128},{192,224},{224,1... | collective-permute-start | bytes 1179656 | tf_op jit(solution)/shard_map/ppermute | solution.py:21
  68.2 12.9 %collective-permute-start.9 = (bf16[768,256]{1,0:T(8,128)(2,1)S(1)}, bf16[768,256]{1,0:T(8,128)(2,1)S(1)}, u32[]{:S(2)}, u32[]{:S(2)}) collective-permute-start(bf16[768,256]{1,0:T(8,128)(2,1)S(1)} %pad_maximum_fusion.2), channel_id=1, source_target_pairs={{0,512},{32,544},{64,576},{96,608},{128,640},{160,672},{192,704},{... | collective-permute-start | bytes 1179656 | tf_op jit(solution)/shard_map/ppermute | solution.py:21
  81.1 16.3 %collective-permute-start.11 = (bf16[256,1536]{1,0:T(8,128)(2,1)S(1)}, bf16[256,1536]{1,0:T(8,128)(2,1)S(1)}, u32[]{:S(2)}, u32[]{:S(2)}) collective-permute-start(bf16[256,1536]{1,0:T(8,128)(2,1)S(1)} %pad_maximum_fusion.1.r_7_), channel_id=1, source_target_pairs={{0,8},{8,0},{16,24},{24,16},{1,9},{9,1},{17,25},{25,17},{2,10},{10... | collective-permute-start | bytes 2359304 | tf_op jit(solution)/shard_map/ppermute | solution.py:21
  83.1 14.4 %collective-permute-start.10 = (bf16[128,1536]{1,0:T(8,128)(2,1)S(1)}, bf16[128,1536]{1,0:T(8,128)(2,1)}, u32[]{:S(2)}, u32[]{:S(2)}) collective-permute-start(bf16[128,1536]{1,0:T(8,128)(2,1)S(1)} %collective-permute-done.4.r_5_), channel_id=1, source_target_pairs={{0,8},{8,0},{16,24},{24,16},{1,9},{9,1},{17,25},{25,17},{2,10},{10... | collective-permute-start | bytes 1179656 | tf_op jit(solution)/shard_map/ppermute | solution.py:21
  87.4 19.6 %collective-permute-start.12 = (bf16[128,1536]{1,0:T(8,128)(2,1)}, bf16[128,1536]{1,0:T(8,128)(2,1)}, u32[]{:S(2)}, u32[]{:S(2)}) collective-permute-start(bf16[128,1536]{1,0:T(8,128)(2,1)} %dynamic-slice_convert_fusion), channel_id=1, source_target_pairs={{0,1},{1,0},{2,3},{3,2},{4,5},{5,4},{6,7},{7,6},{8,9},{9,8},{10,11... | collective-permute-start | bytes 1179656 | tf_op jit(solution)/shard_map/ppermute | solution.py:21
  101.8 27.3 %copy-start = (f32[1536]{0:T(1024)S(1)}, f32[1536]{0:T(1024)}, u32[]{:S(2)}) copy-start(f32[1536]{0:T(1024)} %param.5) | copy-start | bytes 18436
  108.4 10.2 %collective-permute-start.13 = (bf16[64,1536]{1,0:T(8,128)(2,1)S(1)}, bf16[64,1536]{1,0:T(8,128)(2,1)S(1)}, u32[]{:S(2)}, u32[]{:S(2)}) collective-permute-start(bf16[64,1536]{1,0:T(8,128)(2,1)S(1)} %dynamic-slice_convert_fusion.1), channel_id=1, source_target_pairs={{0,2},{1,3},{2,0},{3,1},{4,6},{5,7},{6,4},{7,5},{8,10},{9,11},{10,... | collective-permute-start | bytes 589832 | tf_op jit(solution)/shard_map/ppermute | solution.py:21
  118.7 10.4 %collective-permute-start.14 = (bf16[32,1536]{1,0:T(8,128)(2,1)S(1)}, bf16[32,1536]{1,0:T(8,128)(2,1)S(1)}, u32[]{:S(2)}, u32[]{:S(2)}) collective-permute-start(bf16[32,1536]{1,0:T(8,128)(2,1)S(1)} %dynamic-slice_convert_fusion.2), channel_id=1, source_target_pairs={{0,4},{1,5},{2,6},{3,7},{4,0},{5,1},{6,2},{7,3},{8,12},{9,13},{10,... | collective-permute-start | bytes 294920 | tf_op jit(solution)/shard_map/ppermute | solution.py:21
Sparse Core Ops, SparseCore 0:
  101.9 57.5 reduce-scatter.1

commit v5 on v2

--- a/solution.py
+++ b/solution.py
@@ -30,7 +30,7 @@
 
 
 def weight_kernel(scale, rows, *refs):
-    left, right, out = refs[:4], refs[4:12], refs[12:]
+    left, right, out = refs[:2], refs[2:6], refs[6:]
     hidden = right[0].shape[1]
     tile = 256
 
@@ -38,7 +38,7 @@
     def _(step):
         cols = pl.ds(pl.multiple_of(step * tile, tile), tile)
         total = None
-        for i in range(4):
+        for i in range(2):
             tokens = jnp.concatenate([right[2 * i][:, cols], right[2 * i + 1][:, cols]], axis=0)
             term = dot(left[i][...], tokens)
             total = term if total is None else total + term
@@ -67,8 +67,6 @@
 
 
 Z = 16
-ZH = Z // 2
-GROUP = (16, 1, 17)
 
 
 def body(tokens_in, norm_gain, in_weight, cotangent):
@@ -79,7 +77,7 @@
     half = tok_rows // 2
     dp, my = lax.axis_index("dp"), lax.axis_index("my")
     core = lax.axis_index("mx") % 2
-    zh, x_lo, zl = (dp % Z) // 2, dp // Z, dp % 2
+    z, x_lo = dp % Z, dp // Z
     block = width // n_dp
 
     values = tokens_in.astype(F32)
@@ -96,18 +94,14 @@
     kept = lax.optimization_barrier(dot(mine, in_weight)) + from_core.astype(F32)
     from_x = swap(kept.astype(BF), "mx", n_mx, 2)
 
-    turned = jnp.concatenate([mine.T, other.T], axis=1).reshape(2, ZH, 2, block, tok_rows)
+    turned = jnp.concatenate([mine.T, other.T], axis=1).reshape(2, Z, block, tok_rows)
     turned = jnp.concatenate([turned, turned], axis=1)
 
-    def columns(xb, zb):
-        piece = lax.dynamic_slice(
-            turned, (x_lo ^ xb, zh, zl ^ zb, 0, 0), (1, ZH, 1, block, tok_rows)
-        )
-        return piece.reshape(ZH * block, tok_rows)
+    def columns(index):
+        piece = lax.dynamic_slice(turned, (index, z, 0, 0), (1, Z, block, tok_rows))
+        return piece.reshape(Z * block, tok_rows)
 
-    left = [columns(0, 0)]
-    for bits in GROUP:
-        left.append(swap(columns(bits // 16, bits % 2), "dp", n_dp, bits))
+    left = [columns(x_lo), swap(columns(1 - x_lo), "dp", n_dp, Z)]
     from_x, *left = lax.optimization_barrier((from_x, *left))
 
     pre = kept + from_x.astype(F32)
@@ -116,26 +110,25 @@
 
     own_pair = swap(dpre, "mx", n_mx, 1)
     right = [dpre, own_pair]
-    arrived = [swap(dpre, "dp", n_dp, bits) for bits in GROUP]
+    arrived = swap(dpre, "dp", n_dp, Z)
 
     in_order = jnp.where(core == 0, jnp.concatenate(right, axis=0), jnp.concatenate(right[::-1], axis=0))
     back = dot(in_order, in_weight, ((1,), (1,)))
-    back, *arrived = lax.optimization_barrier((back, *arrived))
+    back, arrived = lax.optimization_barrier((back, arrived))
     dnormed = lax.psum_scatter(back, "my", scatter_dimension=0, tiled=True)
     own_rows = tok_rows // n_my
 
-    for piece in arrived:
-        right += [piece, swap(piece, "mx", n_mx, 1)]
+    right += [arrived, swap(arrived, "mx", n_mx, 1)]
     terms = weight_blocks(left, right, 1.0 / math.sqrt(n_dp * tok_rows), block)
 
     def hop(value, way):
-        perm = [(i, i // Z * Z + (i + 2 * way) % Z) for i in range(n_dp)]
+        perm = [(i, i // Z * Z + (i + way) % Z) for i in range(n_dp)]
         return lax.ppermute(value.astype(BF), "dp", perm).astype(F32)
 
-    ahead, behind = terms[ZH // 2], terms[ZH // 2 + 1]
-    for step in range(1, ZH // 2):
-        ahead = hop(ahead, 1) + terms[ZH // 2 - step].astype(F32)
-        behind = hop(behind, -1) + terms[(ZH // 2 + 1 + step) % ZH].astype(F32)
+    ahead, behind = terms[Z // 2], terms[Z // 2 + 1]
+    for step in range(1, Z // 2):
+        ahead = hop(ahead, 1) + terms[Z // 2 - step].astype(F32)
+        behind = hop(behind, -1) + terms[(Z // 2 + 1 + step) % Z].astype(F32)
     ahead, dnormed = lax.optimization_barrier((ahead, dnormed))
     grad_weight = (behind + hop(ahead, 1)).astype(BF).reshape(1, 1, block, hidden)
 

time: 158 us -> 170 us (1.076)
  starting transfers between devices: 64.3 us -> 68.7 us
  blocking collectives: 32.2 us -> 35.9 us
  waiting for transfers between devices: 19.8 us -> 22.3 us
    ppermute x7 -> x15, starting transfers between devices: 33.4 us -> 53.3 us  [hop(): return lax.ppermute(value.astype(BF), 'dp', perm).astype(F32)]
    ppermute x12 -> x6, starting transfers between devices: 30.9 us -> 15.4 us  [swap(): return lax.ppermute(value, axis, [(i, i ^ bits) for i in range(size)])]
    psum x1, blocking collectives: 11.6 us -> 15.3 us  [body(): lax.psum((jnp.sum(dcentred, axis=1), jnp.sum(dcentred * centred_rows, axi...]
    ppermute x12 -> x6, waiting for transfers between devices: 15.5 us -> 17 us  [swap(): return lax.ppermute(value, axis, [(i, i ^ bits) for i in range(size)])]
    ppermute x7 -> x15, waiting for transfers between devices: 4.3 us -> 5.29 us  [hop(): return lax.ppermute(value.astype(BF), 'dp', perm).astype(F32)]
  transfers between devices with their start and end apart: 20 -> 22, of which waited for: 10 -> 11; matrix products, arithmetic and copies ran while one was open for 8% -> 7% of each run, Pallas kernels for 2% -> 0%
where the time goes in v5:
time: 170 us; the launch traced here: 169 us
  starting transfers between devices  68.7 us (40%)
  blocking collectives  35.9 us (21%)
  waiting for transfers between devices  22.3 us (13%)
  between operations  14.5 us (9%)
  matrix products  12.1 us (7%)
  other arithmetic  10.1 us (6%)
  local copies, waits for them, and re-layouts  3.16 us (2%)
  Pallas kernels  2.22 us (1%)
    ppermute x15, starting transfers between devices, hop(): return lax.ppermute(value.astype(BF), 'dp', perm).astype(F32)  53.3 us
    psum x1, blocking collectives, body(): lax.psum((jnp.sum(values, axis=1), jnp.sum(values * values, axis=1)), 'mx')  20.7 us
    ppermute x6, waiting for transfers between devices, swap(): return lax.ppermute(value, axis, [(i, i ^ bits) for i in range(size)])  17 us
    ppermute x6, starting transfers between devices, swap(): return lax.ppermute(value, axis, [(i, i ^ bits) for i in range(size)])  15.4 us
    psum x1, blocking collectives, body(): lax.psum((jnp.sum(dcentred, axis=1), jnp.sum(dcentred * centred_rows, axi...  15.3 us
    dot_general x3, matrix products, dot(): return lax.dot_general(a, b, (dims, ((), ())), preferred_element_type=F32)  12.1 us
    ppermute x15, waiting for transfers between devices, hop(): return lax.ppermute(value.astype(BF), 'dp', perm).astype(F32)  5.29 us
  transfers between devices with their start and end apart: 22, of which 11 were waited for; matrix products, arithmetic and copies ran while one was open for 7% of the time, Pallas kernels for 0%

profile of v5, /device:TPU:1, one launch (start us, length us, event | category | flops | bytes accessed | tf_op | source)
XLA Modules:
  0.0 169.1 jit_solution(3451246286013879696)
XLA Ops:
  7.2 0.0 reduce-scatter.2.cloned.1.call-start
  7.2 1.5 convert_reduce_fusion
  8.7 20.7 %all-reduce.1 = (f32[256]{0:T(256)S(1)}, f32[256]{0:T(256)S(1)}) all-reduce(f32[256]{0:T(256)S(1)} %get-tuple-element.49, f32[256]{0:T(256)S(1)} %get-tuple-element.48), channel_id=1, replica_groups=mesh['dp'=32,'mx'=4,'my'=8] {'mx'}, use_global_device_ids=true, to_apply=%region_3.4 | all-reduce | flops 512 | bytes 4096 | tf_op jit(solution)/shard_map/psum | solution.py:84
  29.4 2.6 %fusion = (f32[256,1536]{1,0:T(8,128)}, bf16[256,1536]{1,0:T(8,128)(2,1)S(1)}) fusion(bf16[256,1536]{1,0:T(8,128)(2,1)} %param.4, f32[256]{0:T(256)S(1)} %get-tuple-element.63, f32[256]{0:T(256)S(1)} %get-tuple-element.62, f32[1536]{0:T(1024)} %param.5), kind=kLoop, calls=%fused_computation.8 | loop fusion | flops 1966080 | bytes 3153920 | tf_op jit(solution)/shard_map/mul | solution.py:87
  32.0 3.9 %convolution_convert_fusion = bf16[128,1536]{1,0:T(8,128)(2,1)} fusion(bf16[1536,1536]{1,0:T(8,128)(2,1)} %param.6, bf16[256,1536]{1,0:T(8,128)(2,1)S(1)} %get-tuple-element.57, s32[]{:T(128)S(6)} %select_n.46), kind=kOutput, calls=%fused_computation | convolution fusion | flops 604176384 | bytes 5505028 | tf_op jit(solution)/shard_map/dot_general | solution.py:29
  35.9 2.6 %collective-permute-start = (bf16[128,1536]{1,0:T(8,128)(2,1)}, bf16[128,1536]{1,0:T(8,128)(2,1)S(1)}, u32[]{:S(2)}, u32[]{:S(2)}) collective-permute-start(bf16[128,1536]{1,0:T(8,128)(2,1)} %convolution_convert_fusion), channel_id=1, source_target_pairs={{0,8},{8,0},{16,24},{24,16},{1,9},{9,1},{17,25},{25,17},{2,10},{10... | collective-permute-start | bytes 1179656 | tf_op jit(solution)/shard_map/ppermute | solution.py:21
  38.6 0.1 dynamic-slice_bitcast_fusion.1
  38.7 0.1 pad_maximum_fusion
  38.7 0.3 copy.8
  39.0 0.3 fusion.16
  39.4 1.9 %collective-permute-start.2 = (bf16[768,256]{1,0:T(8,128)(2,1)S(1)}, bf16[768,256]{1,0:T(8,128)(2,1)S(1)}, u32[]{:S(2)}, u32[]{:S(2)}) collective-permute-start(bf16[768,256]{1,0:T(8,128)(2,1)S(1)} %bitcast.14), channel_id=1, source_target_pairs={{0,512},{32,544},{64,576},{96,608},{128,640},{160,672},{192,704},{... | collective-permute-start | bytes 1179656 | tf_op jit(solution)/shard_map/ppermute | solution.py:21
  41.3 3.1 %fusion.19 = f32[128,1536]{1,0:T(8,128)S(1)} fusion(bf16[1536,1536]{1,0:T(8,128)(2,1)} %param.6, bf16[256,1536]{1,0:T(8,128)(2,1)S(1)} %get-tuple-element.57, s32[]{:T(128)S(6)} %select_n.45), kind=kOutput, calls=%fused_computation.34 | convolution fusion | flops 603979776 | bytes 5898244 | tf_op jit(solution)/shard_map/dot_general | solution.py:29
  44.4 0.0 copy-start.5
  44.4 0.1 fusion.15
  44.5 2.1 %collective-permute-start.1 = (bf16[128,1536]{1,0:T(8,128)(2,1)S(1)}, bf16[128,1536]{1,0:T(8,128)(2,1)S(1)}, u32[]{:S(2)}, u32[]{:S(2)}) collective-permute-start(bf16[128,1536]{1,0:T(8,128)(2,1)S(1)} %fusion.15), channel_id=1, source_target_pairs={{0,16},{8,24},{16,0},{24,8},{1,17},{9,25},{17,1},{25,9},{2,18},{10... | collective-permute-start | bytes 1179656 | tf_op jit(solution)/shard_map/ppermute | solution.py:21
  46.6 5.4 %collective-permute-done.2.refs_1_ = bf16[768,256]{1,0:T(8,128)(2,1)S(1)} collective-permute-done((bf16[768,256]{1,0:T(8,128)(2,1)S(1)}, bf16[768,256]{1,0:T(8,128)(2,1)S(1)}, u32[]{:S(2)}, u32[]{:S(2)}) %collective-permute-start.2) | collective-permute-done | bytes 393248 | tf_op jit(solution)/shard_map/ppermute | solution.py:21
  52.0 6.8 %collective-permute-done.1 = bf16[128,1536]{1,0:T(8,128)(2,1)S(1)} collective-permute-done((bf16[128,1536]{1,0:T(8,128)(2,1)S(1)}, bf16[128,1536]{1,0:T(8,128)(2,1)S(1)}, u32[]{:S(2)}, u32[]{:S(2)}) %collective-permute-start.1) | collective-permute-done | bytes 393248 | tf_op jit(solution)/shard_map/ppermute | solution.py:21
  58.8 1.4 fusion.7.refs_2_
  60.2 2.7 %collective-permute-start.3 = (bf16[128,1536]{1,0:T(8,128)(2,1)S(1)}, bf16[128,1536]{1,0:T(8,128)(2,1)S(1)}, u32[]{:S(2)}, u32[]{:S(2)}) collective-permute-start(bf16[128,1536]{1,0:T(8,128)(2,1)S(1)} %fusion.7.refs_2_), channel_id=1, source_target_pairs={{0,8},{8,0},{16,24},{24,16},{1,9},{9,1},{17,25},{25,17},{2,10},{10... | collective-permute-start | bytes 1179656 | tf_op jit(solution)/shard_map/ppermute | solution.py:21
  63.0 3.4 %collective-permute-start.4 = (bf16[128,1536]{1,0:T(8,128)(2,1)S(1)}, bf16[128,1536]{1,0:T(8,128)(2,1)S(1)}, u32[]{:S(2)}, u32[]{:S(2)}) collective-permute-start(bf16[128,1536]{1,0:T(8,128)(2,1)S(1)} %fusion.7.refs_2_), channel_id=1, source_target_pairs={{0,512},{32,544},{64,576},{96,608},{128,640},{160,672},{192,704},{... | collective-permute-start | bytes 1179656 | tf_op jit(solution)/shard_map/ppermute | solution.py:21
  66.3 0.0 collective-permute-done.3.refs_3_
  66.3 5.0 %fusion.8 = f32[256,1536]{1,0:T(8,128)} fusion(bf16[1536,1536]{1,0:T(8,128)(2,1)} %param.6, bf16[128,1536]{1,0:T(8,128)(2,1)S(1)} %collective-permute-done.3.refs_3_, bf16[128,1536]{1,0:T(8,128)(2,1)S(1)} %fusion.7.refs_2_, pred[]{:T(512)S(6)} %eq.6), kind=kOutput, calls=%fused_computation.20 | convolution fusion | flops 1211498496 | bytes 7077889 | tf_op jit(solution)/shard_map/dot_general | solution.py:29
  71.4 4.2 %collective-permute-done.4.refs_4_ = bf16[128,1536]{1,0:T(8,128)(2,1)S(1)} collective-permute-done((bf16[128,1536]{1,0:T(8,128)(2,1)S(1)}, bf16[128,1536]{1,0:T(8,128)(2,1)S(1)}, u32[]{:S(2)}, u32[]{:S(2)}) %collective-permute-start.4) | collective-permute-done | bytes 393248 | tf_op jit(solution)/shard_map/ppermute | solution.py:21
  75.6 2.7 %collective-permute-start.5 = (bf16[128,1536]{1,0:T(8,128)(2,1)S(1)}, bf16[128,1536]{1,0:T(8,128)(2,1)S(1)}, u32[]{:S(2)}, u32[]{:S(2)}) collective-permute-start(bf16[128,1536]{1,0:T(8,128)(2,1)S(1)} %collective-permute-done.4.refs_4_), channel_id=1, source_target_pairs={{0,8},{8,0},{16,24},{24,16},{1,9},{9,1},{17,25},{25,17},{2,10},{10... | collective-permute-start | bytes 1179656 | tf_op jit(solution)/shard_map/ppermute | solution.py:21
  78.3 0.7 copy-done.2
  79.0 0.6 collective-permute-done.5.refs_5_
  79.6 1.0 copy-done.1
  80.6 1.0 copy-done.3
  81.6 2.2 %shard_map.59 = (bf16[48,1536]{1,0:T(8,128)(2,1)S(1)}, bf16[48,1536]{1,0:T(8,128)(2,1)S(1)}, bf16[48,1536]{1,0:T(8,128)(2,1)S(1)}, bf16[48,1536]{1,0:T(8,128)(2,...) custom-call(bf16[768,256]{1,0:T(8,128)(2,1)S(1)} %bitcast.12, ...), custom_call_target="tpu_custom_call" | custom-call | flops 1207959552 | bytes 4718592 | tf_op jit(solution)/shard_map/pallas_call | solution.py:55
  83.8 1.9 %collective-permute-start.13 = (bf16[48,1536]{1,0:T(8,128)(2,1)S(1)}, bf16[48,1536]{1,0:T(8,128)(2,1)S(1)}, u32[]{:S(2)}, u32[]{:S(2)}) collective-permute-start(bf16[48,1536]{1,0:T(8,128)(2,1)S(1)} %get-tuple-element.37), channel_id=1, source_target_pairs={{0,32},{32,64},{64,96},{96,128},{128,160},{160,192},{192,224},{224... | collective-permute-start | bytes 442376 | tf_op jit(solution)/shard_map/ppermute | solution.py:126
  85.8 0.1 dynamic_slice.26
  85.8 0.0 reduce-scatter.2.cloned.1.call-update
  85.9 10.1 %collective-permute-start.6 = (bf16[48,1536]{1,0:T(8,128)(2,1)S(1)}, bf16[48,1536]{1,0:T(8,128)(2,1)S(1)}, u32[]{:S(2)}, u32[]{:S(2)}) collective-permute-start(bf16[48,1536]{1,0:T(8,128)(2,1)S(1)} %get-tuple-element.29), channel_id=1, source_target_pairs={{0,480},{32,0},{64,32},{96,64},{128,96},{160,128},{192,160},{224,1... | collective-permute-start | bytes 442376 | tf_op jit(solution)/shard_map/ppermute | solution.py:126
  96.0 1.9 %collective-permute-done.13 = bf16[48,1536]{1,0:T(8,128)(2,1)S(1)} collective-permute-done((bf16[48,1536]{1,0:T(8,128)(2,1)S(1)}, bf16[48,1536]{1,0:T(8,128)(2,1)S(1)}, u32[]{:S(2)}, u32[]{:S(2)}) %collective-permute-start.13) | collective-permute-done | bytes 147488 | tf_op jit(solution)/shard_map/ppermute | solution.py:126
  97.9 1.9 %collective-permute-start.14 = (bf16[48,1536]{1,0:T(8,128)(2,1)S(1)}, bf16[48,1536]{1,0:T(8,128)(2,1)S(1)}, u32[]{:S(2)}, u32[]{:S(2)}) collective-permute-start(bf16[48,1536]{1,0:T(8,128)(2,1)S(1)} %add_convert_fusion.6), channel_id=1, source_target_pairs={{0,32},{32,64},{64,96},{96,128},{128,160},{160,192},{192,224},{224... | collective-permute-start | bytes 442376 | tf_op jit(solution)/shard_map/ppermute | solution.py:126
  99.9 0.0 collective-permute-done.6
  99.9 4.6 %collective-permute-start.7 = (bf16[48,1536]{1,0:T(8,128)(2,1)S(1)}, bf16[48,1536]{1,0:T(8,128)(2,1)S(1)}, u32[]{:S(2)}, u32[]{:S(2)}) collective-permute-start(bf16[48,1536]{1,0:T(8,128)(2,1)S(1)} %add_convert_fusion.12), channel_id=1, source_target_pairs={{0,480},{32,0},{64,32},{96,64},{128,96},{160,128},{192,160},{224,1... | collective-permute-start | bytes 442376 | tf_op jit(solution)/shard_map/ppermute | solution.py:126
  104.5 1.0 collective-permute-done.14
  105.6 1.9 %collective-permute-start.15 = (bf16[48,1536]{1,0:T(8,128)(2,1)S(1)}, bf16[48,1536]{1,0:T(8,128)(2,1)S(1)}, u32[]{:S(2)}, u32[]{:S(2)}) collective-permute-start(bf16[48,1536]{1,0:T(8,128)(2,1)S(1)} %add_convert_fusion.5), channel_id=1, source_target_pairs={{0,32},{32,64},{64,96},{96,128},{128,160},{160,192},{192,224},{224... | collective-permute-start | bytes 442376 | tf_op jit(solution)/shard_map/ppermute | solution.py:126
  107.5 0.0 collective-permute-done.7
  107.5 4.6 %collective-permute-start.8 = (bf16[48,1536]{1,0:T(8,128)(2,1)S(1)}, bf16[48,1536]{1,0:T(8,128)(2,1)S(1)}, u32[]{:S(2)}, u32[]{:S(2)}) collective-permute-start(bf16[48,1536]{1,0:T(8,128)(2,1)S(1)} %add_convert_fusion.11), channel_id=1, source_target_pairs={{0,480},{32,0},{64,32},{96,64},{128,96},{160,128},{192,160},{224,1... | collective-permute-start | bytes 442376 | tf_op jit(solution)/shard_map/ppermute | solution.py:126
  112.1 0.5 collective-permute-done.15
  112.7 1.9 %collective-permute-start.16 = (bf16[48,1536]{1,0:T(8,128)(2,1)S(1)}, bf16[48,1536]{1,0:T(8,128)(2,1)S(1)}, u32[]{:S(2)}, u32[]{:S(2)}) collective-permute-start(bf16[48,1536]{1,0:T(8,128)(2,1)S(1)} %add_convert_fusion.4), channel_id=1, source_target_pairs={{0,32},{32,64},{64,96},{96,128},{128,160},{160,192},{192,224},{224... | collective-permute-start | bytes 442376 | tf_op jit(solution)/shard_map/ppermute | solution.py:126
  114.6 0.0 collective-permute-done.8
  114.7 0.0 copy-start.6
  114.7 4.6 %collective-permute-start.9 = (bf16[48,1536]{1,0:T(8,128)(2,1)S(1)}, bf16[48,1536]{1,0:T(8,128)(2,1)S(1)}, u32[]{:S(2)}, u32[]{:S(2)}) collective-permute-start(bf16[48,1536]{1,0:T(8,128)(2,1)S(1)} %add_convert_fusion.10), channel_id=1, source_target_pairs={{0,480},{32,0},{64,32},{96,64},{128,96},{160,128},{192,160},{224,1... | collective-permute-start | bytes 442376 | tf_op jit(solution)/shard_map/ppermute | solution.py:126
  119.3 0.5 collective-permute-done.16
  119.8 1.9 %collective-permute-start.17 = (bf16[48,1536]{1,0:T(8,128)(2,1)S(1)}, bf16[48,1536]{1,0:T(8,128)(2,1)S(1)}, u32[]{:S(2)}, u32[]{:S(2)}) collective-permute-start(bf16[48,1536]{1,0:T(8,128)(2,1)S(1)} %add_convert_fusion.3), channel_id=1, source_target_pairs={{0,32},{32,64},{64,96},{96,128},{128,160},{160,192},{192,224},{224... | collective-permute-start | bytes 442376 | tf_op jit(solution)/shard_map/ppermute | solution.py:126
  121.8 0.0 collective-permute-done.9
  121.8 4.6 %collective-permute-start.10 = (bf16[48,1536]{1,0:T(8,128)(2,1)S(1)}, bf16[48,1536]{1,0:T(8,128)(2,1)S(1)}, u32[]{:S(2)}, u32[]{:S(2)}) collective-permute-start(bf16[48,1536]{1,0:T(8,128)(2,1)S(1)} %add_convert_fusion.9), channel_id=1, source_target_pairs={{0,480},{32,0},{64,32},{96,64},{128,96},{160,128},{192,160},{224,1... | collective-permute-start | bytes 442376 | tf_op jit(solution)/shard_map/ppermute | solution.py:126
  126.4 0.5 collective-permute-done.17
  127.0 1.9 %collective-permute-start.18 = (bf16[48,1536]{1,0:T(8,128)(2,1)S(1)}, bf16[48,1536]{1,0:T(8,128)(2,1)S(1)}, u32[]{:S(2)}, u32[]{:S(2)}) collective-permute-start(bf16[48,1536]{1,0:T(8,128)(2,1)S(1)} %add_convert_fusion.2), channel_id=1, source_target_pairs={{0,32},{32,64},{64,96},{96,128},{128,160},{160,192},{192,224},{224... | collective-permute-start | bytes 442376 | tf_op jit(solution)/shard_map/ppermute | solution.py:126
  128.9 0.0 collective-permute-done.10
  129.0 4.7 %collective-permute-start.11 = (bf16[48,1536]{1,0:T(8,128)(2,1)S(1)}, bf16[48,1536]{1,0:T(8,128)(2,1)S(1)}, u32[]{:S(2)}, u32[]{:S(2)}) collective-permute-start(bf16[48,1536]{1,0:T(8,128)(2,1)S(1)} %add_convert_fusion.8), channel_id=1, source_target_pairs={{0,480},{32,0},{64,32},{96,64},{128,96},{160,128},{192,160},{224,1... | collective-permute-start | bytes 442376 | tf_op jit(solution)/shard_map/ppermute | solution.py:126
  133.7 0.4 collective-permute-done.18
  134.1 1.9 %collective-permute-start.19 = (bf16[48,1536]{1,0:T(8,128)(2,1)S(1)}, bf16[48,1536]{1,0:T(8,128)(2,1)S(1)}, u32[]{:S(2)}, u32[]{:S(2)}) collective-permute-start(bf16[48,1536]{1,0:T(8,128)(2,1)S(1)} %add_convert_fusion.1), channel_id=1, source_target_pairs={{0,32},{32,64},{64,96},{96,128},{128,160},{160,192},{192,224},{224... | collective-permute-start | bytes 442376 | tf_op jit(solution)/shard_map/ppermute | solution.py:126
  136.1 4.8 %collective-permute-start.12 = (bf16[48,1536]{1,0:T(8,128)(2,1)S(1)}, bf16[48,1536]{1,0:T(8,128)(2,1)S(1)}, u32[]{:S(2)}, u32[]{:S(2)}) collective-permute-start(bf16[48,1536]{1,0:T(8,128)(2,1)S(1)} %add_convert_fusion.7), channel_id=1, source_target_pairs={{0,480},{32,0},{64,32},{96,64},{128,96},{160,128},{192,160},{224,1... | collective-permute-start | bytes 442376 | tf_op jit(solution)/shard_map/ppermute | solution.py:126
  140.9 0.4 collective-permute-done.19
  141.4 0.0 reduce-scatter.2.cloned.1.call-done
  141.4 1.9 %collective-permute-start.20 = (bf16[48,1536]{1,0:T(8,128)(2,1)S(1)}, bf16[48,1536]{1,0:T(8,128)(2,1)S(1)}, u32[]{:S(2)}, u32[]{:S(2)}) collective-permute-start(bf16[48,1536]{1,0:T(8,128)(2,1)S(1)} %convert_add_fusion.1), channel_id=1, source_target_pairs={{0,32},{32,64},{64,96},{96,128},{128,160},{160,192},{192,224},{224... | collective-permute-start | bytes 442376 | tf_op jit(solution)/shard_map/ppermute | solution.py:126
  143.4 1.2 multiply_reduce_fusion.1
  144.5 15.3 %all-reduce = (f32[32]{0:T(128)S(1)}, f32[32]{0:T(128)S(1)}) all-reduce(f32[32]{0:T(128)S(1)} %get-tuple-element.51, f32[32]{0:T(128)S(1)} %get-tuple-element.50), channel_id=1, replica_groups=mesh['dp'=32,'mx'=4,'my'=8] {'mx'}, use_global_device_ids=true, to_apply=%region_8.9 | all-reduce | flops 64 | bytes 512 | tf_op jit(solution)/shard_map/psum | solution.py:139
  159.8 1.8 %multiply_convert_fusion.1 = bf16[32,1536]{1,0:T(8,128)(2,1)} fusion(f32[256,1536]{1,0:T(8,128)} %get-tuple-element.56, s32[]{:T(128)S(6)} %select_n.54, f32[32,1536]{1,0:T(8,128)} %reduce-scatter.2.cloned.1.call-done, f32[32]{0:T(128)S(1)} %get-tuple-element.64, f32[32]{0:T(128)S(1)} %get-tuple-element.65, f32[1536]{0:T(1024)S(1)} %copy-done.6, ...), kind=kLoop, calls=%fused_computation.50 | loop fusion | flops 294912 | bytes 498052 | tf_op jit(solution)/shard_map/convert_element_type | solution.py:145
  161.6 0.7 fusion.21
  (28 shorter events, 0.5 us)
Async XLA Ops:
  7.2 134.2 %reduce-scatter.2.cloned.1.call-start = ((), (), s32[]{:S(2)}) async-start(), calls=%async_computation.1 | async-start | bytes 1769472 | tf_op jit(solution)/shard_map/reduce_scatter | solution.py:118
  35.9 8.5 %collective-permute-start = (bf16[128,1536]{1,0:T(8,128)(2,1)}, bf16[128,1536]{1,0:T(8,128)(2,1)S(1)}, u32[]{:S(2)}, u32[]{:S(2)}) collective-permute-start(bf16[128,1536]{1,0:T(8,128)(2,1)} %convolution_convert_fusion), channel_id=1, source_target_pairs={{0,8},{8,0},{16,24},{24,16},{1,9},{9,1},{17,25},{25,17},{2,10},{10... | collective-permute-start | bytes 1179656 | tf_op jit(solution)/shard_map/ppermute | solution.py:21
  39.4 12.6 %collective-permute-start.2 = (bf16[768,256]{1,0:T(8,128)(2,1)S(1)}, bf16[768,256]{1,0:T(8,128)(2,1)S(1)}, u32[]{:S(2)}, u32[]{:S(2)}) collective-permute-start(bf16[768,256]{1,0:T(8,128)(2,1)S(1)} %bitcast.14), channel_id=1, source_target_pairs={{0,512},{32,544},{64,576},{96,608},{128,640},{160,672},{192,704},{... | collective-permute-start | bytes 1179656 | tf_op jit(solution)/shard_map/ppermute | solution.py:21
  44.4 14.4 %copy-start.5 = (bf16[256,1536]{1,0:T(8,128)(2,1)S(1)}, bf16[256,1536]{1,0:T(8,128)(2,1)}, u32[]{:S(2)}) copy-start(bf16[256,1536]{1,0:T(8,128)(2,1)} %param.7) | copy-start | bytes 2359300
  44.4 14.4 %copy-start.4 = (bf16[128,1536]{1,0:T(8,128)(2,1)}, bf16[128,1536]{1,0:T(8,128)(2,1)S(1)}, u32[]{:S(2)}) copy-start(bf16[128,1536]{1,0:T(8,128)(2,1)S(1)} %collective-permute-done) | copy-start | bytes 1179652
  44.5 14.3 %collective-permute-start.1 = (bf16[128,1536]{1,0:T(8,128)(2,1)S(1)}, bf16[128,1536]{1,0:T(8,128)(2,1)S(1)}, u32[]{:S(2)}, u32[]{:S(2)}) collective-permute-start(bf16[128,1536]{1,0:T(8,128)(2,1)S(1)} %fusion.15), channel_id=1, source_target_pairs={{0,16},{8,24},{16,0},{24,8},{1,17},{9,25},{17,1},{25,9},{2,18},{10... | collective-permute-start | bytes 1179656 | tf_op jit(solution)/shard_map/ppermute | solution.py:21
  60.2 6.1 %collective-permute-start.3 = (bf16[128,1536]{1,0:T(8,128)(2,1)S(1)}, bf16[128,1536]{1,0:T(8,128)(2,1)S(1)}, u32[]{:S(2)}, u32[]{:S(2)}) collective-permute-start(bf16[128,1536]{1,0:T(8,128)(2,1)S(1)} %fusion.7.refs_2_), channel_id=1, source_target_pairs={{0,8},{8,0},{16,24},{24,16},{1,9},{9,1},{17,25},{25,17},{2,10},{10... | collective-permute-start | bytes 1179656 | tf_op jit(solution)/shard_map/ppermute | solution.py:21
  63.0 12.6 %collective-permute-start.4 = (bf16[128,1536]{1,0:T(8,128)(2,1)S(1)}, bf16[128,1536]{1,0:T(8,128)(2,1)S(1)}, u32[]{:S(2)}, u32[]{:S(2)}) collective-permute-start(bf16[128,1536]{1,0:T(8,128)(2,1)S(1)} %fusion.7.refs_2_), channel_id=1, source_target_pairs={{0,512},{32,544},{64,576},{96,608},{128,640},{160,672},{192,704},{... | collective-permute-start | bytes 1179656 | tf_op jit(solution)/shard_map/ppermute | solution.py:21
  66.3 5.0 %copy-start = (bf16[128,1536]{1,0:T(8,128)(2,1)}, bf16[128,1536]{1,0:T(8,128)(2,1)S(1)}, u32[]{:S(2)}) copy-start(bf16[128,1536]{1,0:T(8,128)(2,1)S(1)} %collective-permute-done.3.refs_3_) | copy-start | bytes 1179652
  75.6 4.0 %collective-permute-start.5 = (bf16[128,1536]{1,0:T(8,128)(2,1)S(1)}, bf16[128,1536]{1,0:T(8,128)(2,1)S(1)}, u32[]{:S(2)}, u32[]{:S(2)}) collective-permute-start(bf16[128,1536]{1,0:T(8,128)(2,1)S(1)} %collective-permute-done.4.refs_4_), channel_id=1, source_target_pairs={{0,8},{8,0},{16,24},{24,16},{1,9},{9,1},{17,25},{25,17},{2,10},{10... | collective-permute-start | bytes 1179656 | tf_op jit(solution)/shard_map/ppermute | solution.py:21
  78.3 0.7 copy-start.2
  79.6 1.0 copy-start.1
  80.6 1.0 copy-start.3
  83.8 14.1 %collective-permute-start.13 = (bf16[48,1536]{1,0:T(8,128)(2,1)S(1)}, bf16[48,1536]{1,0:T(8,128)(2,1)S(1)}, u32[]{:S(2)}, u32[]{:S(2)}) collective-permute-start(bf16[48,1536]{1,0:T(8,128)(2,1)S(1)} %get-tuple-element.37), channel_id=1, source_target_pairs={{0,32},{32,64},{64,96},{96,128},{128,160},{160,192},{192,224},{224... | collective-permute-start | bytes 442376 | tf_op jit(solution)/shard_map/ppermute | solution.py:126
  85.9 14.0 %collective-permute-start.6 = (bf16[48,1536]{1,0:T(8,128)(2,1)S(1)}, bf16[48,1536]{1,0:T(8,128)(2,1)S(1)}, u32[]{:S(2)}, u32[]{:S(2)}) collective-permute-start(bf16[48,1536]{1,0:T(8,128)(2,1)S(1)} %get-tuple-element.29), channel_id=1, source_target_pairs={{0,480},{32,0},{64,32},{96,64},{128,96},{160,128},{192,160},{224,1... | collective-permute-start | bytes 442376 | tf_op jit(solution)/shard_map/ppermute | solution.py:126
  97.9 7.6 %collective-permute-start.14 = (bf16[48,1536]{1,0:T(8,128)(2,1)S(1)}, bf16[48,1536]{1,0:T(8,128)(2,1)S(1)}, u32[]{:S(2)}, u32[]{:S(2)}) collective-permute-start(bf16[48,1536]{1,0:T(8,128)(2,1)S(1)} %add_convert_fusion.6), channel_id=1, source_target_pairs={{0,32},{32,64},{64,96},{96,128},{128,160},{160,192},{192,224},{224... | collective-permute-start | bytes 442376 | tf_op jit(solution)/shard_map/ppermute | solution.py:126
  99.9 7.6 %collective-permute-start.7 = (bf16[48,1536]{1,0:T(8,128)(2,1)S(1)}, bf16[48,1536]{1,0:T(8,128)(2,1)S(1)}, u32[]{:S(2)}, u32[]{:S(2)}) collective-permute-start(bf16[48,1536]{1,0:T(8,128)(2,1)S(1)} %add_convert_fusion.12), channel_id=1, source_target_pairs={{0,480},{32,0},{64,32},{96,64},{128,96},{160,128},{192,160},{224,1... | collective-permute-start | bytes 442376 | tf_op jit(solution)/shard_map/ppermute | solution.py:126
  105.6 7.1 %collective-permute-start.15 = (bf16[48,1536]{1,0:T(8,128)(2,1)S(1)}, bf16[48,1536]{1,0:T(8,128)(2,1)S(1)}, u32[]{:S(2)}, u32[]{:S(2)}) collective-permute-start(bf16[48,1536]{1,0:T(8,128)(2,1)S(1)} %add_convert_fusion.5), channel_id=1, source_target_pairs={{0,32},{32,64},{64,96},{96,128},{128,160},{160,192},{192,224},{224... | collective-permute-start | bytes 442376 | tf_op jit(solution)/shard_map/ppermute | solution.py:126
  107.5 7.1 %collective-permute-start.8 = (bf16[48,1536]{1,0:T(8,128)(2,1)S(1)}, bf16[48,1536]{1,0:T(8,128)(2,1)S(1)}, u32[]{:S(2)}, u32[]{:S(2)}) collective-permute-start(bf16[48,1536]{1,0:T(8,128)(2,1)S(1)} %add_convert_fusion.11), channel_id=1, source_target_pairs={{0,480},{32,0},{64,32},{96,64},{128,96},{160,128},{192,160},{224,1... | collective-permute-start | bytes 442376 | tf_op jit(solution)/shard_map/ppermute | solution.py:126
  112.7 7.1 %collective-permute-start.16 = (bf16[48,1536]{1,0:T(8,128)(2,1)S(1)}, bf16[48,1536]{1,0:T(8,128)(2,1)S(1)}, u32[]{:S(2)}, u32[]{:S(2)}) collective-permute-start(bf16[48,1536]{1,0:T(8,128)(2,1)S(1)} %add_convert_fusion.4), channel_id=1, source_target_pairs={{0,32},{32,64},{64,96},{96,128},{128,160},{160,192},{192,224},{224... | collective-permute-start | bytes 442376 | tf_op jit(solution)/shard_map/ppermute | solution.py:126
  114.7 28.7 %copy-start.6 = (f32[1536]{0:T(1024)S(1)}, f32[1536]{0:T(1024)}, u32[]{:S(2)}) copy-start(f32[1536]{0:T(1024)} %param.5) | copy-start | bytes 18436
  114.7 7.1 %collective-permute-start.9 = (bf16[48,1536]{1,0:T(8,128)(2,1)S(1)}, bf16[48,1536]{1,0:T(8,128)(2,1)S(1)}, u32[]{:S(2)}, u32[]{:S(2)}) collective-permute-start(bf16[48,1536]{1,0:T(8,128)(2,1)S(1)} %add_convert_fusion.10), channel_id=1, source_target_pairs={{0,480},{32,0},{64,32},{96,64},{128,96},{160,128},{192,160},{224,1... | collective-permute-start | bytes 442376 | tf_op jit(solution)/shard_map/ppermute | solution.py:126
  119.8 7.1 %collective-permute-start.17 = (bf16[48,1536]{1,0:T(8,128)(2,1)S(1)}, bf16[48,1536]{1,0:T(8,128)(2,1)S(1)}, u32[]{:S(2)}, u32[]{:S(2)}) collective-permute-start(bf16[48,1536]{1,0:T(8,128)(2,1)S(1)} %add_convert_fusion.3), channel_id=1, source_target_pairs={{0,32},{32,64},{64,96},{96,128},{128,160},{160,192},{192,224},{224... | collective-permute-start | bytes 442376 | tf_op jit(solution)/shard_map/ppermute | solution.py:126
  121.8 7.1 %collective-permute-start.10 = (bf16[48,1536]{1,0:T(8,128)(2,1)S(1)}, bf16[48,1536]{1,0:T(8,128)(2,1)S(1)}, u32[]{:S(2)}, u32[]{:S(2)}) collective-permute-start(bf16[48,1536]{1,0:T(8,128)(2,1)S(1)} %add_convert_fusion.9), channel_id=1, source_target_pairs={{0,480},{32,0},{64,32},{96,64},{128,96},{160,128},{192,160},{224,1... | collective-permute-start | bytes 442376 | tf_op jit(solution)/shard_map/ppermute | solution.py:126
  127.0 7.1 %collective-permute-start.18 = (bf16[48,1536]{1,0:T(8,128)(2,1)S(1)}, bf16[48,1536]{1,0:T(8,128)(2,1)S(1)}, u32[]{:S(2)}, u32[]{:S(2)}) collective-permute-start(bf16[48,1536]{1,0:T(8,128)(2,1)S(1)} %add_convert_fusion.2), channel_id=1, source_target_pairs={{0,32},{32,64},{64,96},{96,128},{128,160},{160,192},{192,224},{224... | collective-permute-start | bytes 442376 | tf_op jit(solution)/shard_map/ppermute | solution.py:126
  129.0 7.1 %collective-permute-start.11 = (bf16[48,1536]{1,0:T(8,128)(2,1)S(1)}, bf16[48,1536]{1,0:T(8,128)(2,1)S(1)}, u32[]{:S(2)}, u32[]{:S(2)}) collective-permute-start(bf16[48,1536]{1,0:T(8,128)(2,1)S(1)} %add_convert_fusion.8), channel_id=1, source_target_pairs={{0,480},{32,0},{64,32},{96,64},{128,96},{160,128},{192,160},{224,1... | collective-permute-start | bytes 442376 | tf_op jit(solution)/shard_map/ppermute | solution.py:126
  134.1 7.2 %collective-permute-start.19 = (bf16[48,1536]{1,0:T(8,128)(2,1)S(1)}, bf16[48,1536]{1,0:T(8,128)(2,1)S(1)}, u32[]{:S(2)}, u32[]{:S(2)}) collective-permute-start(bf16[48,1536]{1,0:T(8,128)(2,1)S(1)} %add_convert_fusion.1), channel_id=1, source_target_pairs={{0,32},{32,64},{64,96},{96,128},{128,160},{160,192},{192,224},{224... | collective-permute-start | bytes 442376 | tf_op jit(solution)/shard_map/ppermute | solution.py:126
  136.1 25.5 %collective-permute-start.12 = (bf16[48,1536]{1,0:T(8,128)(2,1)S(1)}, bf16[48,1536]{1,0:T(8,128)(2,1)S(1)}, u32[]{:S(2)}, u32[]{:S(2)}) collective-permute-start(bf16[48,1536]{1,0:T(8,128)(2,1)S(1)} %add_convert_fusion.7), channel_id=1, source_target_pairs={{0,480},{32,0},{64,32},{96,64},{128,96},{160,128},{192,160},{224,1... | collective-permute-start | bytes 442376 | tf_op jit(solution)/shard_map/ppermute | solution.py:126
  141.4 20.1 %collective-permute-start.20 = (bf16[48,1536]{1,0:T(8,128)(2,1)S(1)}, bf16[48,1536]{1,0:T(8,128)(2,1)S(1)}, u32[]{:S(2)}, u32[]{:S(2)}) collective-permute-start(bf16[48,1536]{1,0:T(8,128)(2,1)S(1)} %convert_add_fusion.1), channel_id=1, source_target_pairs={{0,32},{32,64},{64,96},{96,128},{128,160},{160,192},{192,224},{224... | collective-permute-start | bytes 442376 | tf_op jit(solution)/shard_map/ppermute | solution.py:126
Sparse Core Ops, SparseCore 0:
  86.0 44.7 reduce-scatter.1

commit v6 on v2

--- a/solution.py
+++ b/solution.py
@@ -120,7 +120,7 @@
 
     in_order = jnp.where(core == 0, jnp.concatenate(right, axis=0), jnp.concatenate(right[::-1], axis=0))
     back = dot(in_order, in_weight, ((1,), (1,)))
-    back, *arrived = lax.optimization_barrier((back, *arrived))
+    back, arrived[1] = lax.optimization_barrier((back, arrived[1]))
     dnormed = lax.psum_scatter(back, "my", scatter_dimension=0, tiled=True)
     own_rows = tok_rows // n_my
 

time: 158 us -> 157 us (level)
  transfers between devices with their start and end apart: 20 -> 20, of which waited for: 10 -> 8; matrix products, arithmetic and copies ran while one was open for 8% -> 8% of each run, Pallas kernels for 2% -> 2%
where the time goes in v6:
time: 157 us; the launch traced here: 156 us
  starting transfers between devices  64.1 us (41%)
  blocking collectives  32 us (20%)
  waiting for transfers between devices  19.5 us (12%)
  between operations  14.5 us (9%)
  matrix products  11.1 us (7%)
  other arithmetic  9.61 us (6%)
  Pallas kernels  2.86 us (2%)
  local copies, waits for them, and re-layouts  1.99 us (1%)
    ppermute x7, starting transfers between devices, hop(): return lax.ppermute(value.astype(BF), 'dp', perm).astype(F32)  32.8 us
    ppermute x12, starting transfers between devices, swap(): return lax.ppermute(value, axis, [(i, i ^ bits) for i in range(size)])  31.2 us
    psum x1, blocking collectives, body(): lax.psum((jnp.sum(values, axis=1), jnp.sum(values * values, axis=1)), 'mx')  20.7 us
    ppermute x12, waiting for transfers between devices, swap(): return lax.ppermute(value, axis, [(i, i ^ bits) for i in range(size)])  15.2 us
    psum x1, blocking collectives, body(): lax.psum((jnp.sum(dcentred, axis=1), jnp.sum(dcentred * centred_rows, axi...  11.4 us
    dot_general x3, matrix products, dot(): return lax.dot_general(a, b, (dims, ((), ())), preferred_element_type=F32)  11.1 us
    ppermute x7, waiting for transfers between devices, hop(): return lax.ppermute(value.astype(BF), 'dp', perm).astype(F32)  4.31 us
  transfers between devices with their start and end apart: 20, of which 8 were waited for; matrix products, arithmetic and copies ran while one was open for 8% of the time, Pallas kernels for 2%

profile of v6, /device:TPU:1, one launch (start us, length us, event | category | flops | bytes accessed | tf_op | source)
XLA Modules:
  0.0 155.7 jit_solution(7177837375157973607)
XLA Ops:
  7.2 0.0 reduce-scatter.2.cloned.1.call-start
  7.2 1.5 convert_reduce_fusion
  8.7 20.7 %all-reduce.1 = (f32[256]{0:T(256)S(1)}, f32[256]{0:T(256)S(1)}) all-reduce(f32[256]{0:T(256)S(1)} %get-tuple-element.37, f32[256]{0:T(256)S(1)} %get-tuple-element.36), channel_id=1, replica_groups=mesh['dp'=32,'mx'=4,'my'=8] {'mx'}, use_global_device_ids=true, to_apply=%region_3.4 | all-reduce | flops 512 | bytes 4096 | tf_op jit(solution)/shard_map/psum | solution.py:86
  29.4 2.6 %fusion = (f32[256,1536]{1,0:T(8,128)}, bf16[256,1536]{1,0:T(8,128)(2,1)S(1)}) fusion(bf16[256,1536]{1,0:T(8,128)(2,1)} %param.4, f32[256]{0:T(256)S(1)} %get-tuple-element.53, f32[256]{0:T(256)S(1)} %get-tuple-element.52, f32[1536]{0:T(1024)} %param.5), kind=kLoop, calls=%fused_computation.12 | loop fusion | flops 1966080 | bytes 3153920 | tf_op jit(solution)/shard_map/mul | solution.py:89
  32.0 3.1 %convolution_convert_fusion = bf16[128,1536]{1,0:T(8,128)(2,1)S(1)} fusion(bf16[1536,1536]{1,0:T(8,128)(2,1)} %param.6, bf16[256,1536]{1,0:T(8,128)(2,1)S(1)} %get-tuple-element.45, s32[]{:T(128)S(6)} %select_n.65), kind=kOutput, calls=%fused_computation | convolution fusion | flops 604176384 | bytes 5505028 | tf_op jit(solution)/shard_map/dot_general | solution.py:29
  35.2 2.7 %collective-permute-start = (bf16[128,1536]{1,0:T(8,128)(2,1)S(1)}, bf16[128,1536]{1,0:T(8,128)(2,1)S(1)}, u32[]{:S(2)}, u32[]{:S(2)}) collective-permute-start(bf16[128,1536]{1,0:T(8,128)(2,1)S(1)} %convolution_convert_fusion), channel_id=1, source_target_pairs={{0,8},{8,0},{16,24},{24,16},{1,9},{9,1},{17,25},{25,17},{2,10},{10... | collective-permute-start | bytes 1179656 | tf_op jit(solution)/shard_map/ppermute | solution.py:21
  37.8 3.1 %fusion.17 = f32[128,1536]{1,0:T(8,128)S(1)} fusion(bf16[1536,1536]{1,0:T(8,128)(2,1)} %param.6, bf16[256,1536]{1,0:T(8,128)(2,1)S(1)} %get-tuple-element.45, s32[]{:T(128)S(6)} %select_n.64), kind=kOutput, calls=%fused_computation.36 | convolution fusion | flops 603979776 | bytes 5898244 | tf_op jit(solution)/shard_map/dot_general | solution.py:29
  41.0 0.1 dynamic-slice_bitcast_fusion.1
  41.0 0.0 collective-permute-done
  41.0 0.8 fusion.15
  41.9 1.9 %collective-permute-start.1 = (bf16[128,1536]{1,0:T(8,128)(2,1)}, bf16[128,1536]{1,0:T(8,128)(2,1)S(1)}, u32[]{:S(2)}, u32[]{:S(2)}) collective-permute-start(bf16[128,1536]{1,0:T(8,128)(2,1)} %fusion.15), channel_id=1, source_target_pairs={{0,16},{8,24},{16,0},{24,8},{1,17},{9,25},{17,1},{25,9},{2,18},{10... | collective-permute-start | bytes 1179656 | tf_op jit(solution)/shard_map/ppermute | solution.py:21
  43.8 0.1 pad_maximum_fusion
  43.9 0.3 copy.8
  44.2 0.0 copy-start.3
  44.2 0.3 fusion.19
  44.6 1.9 %collective-permute-start.4 = (bf16[384,256]{1,0:T(8,128)(2,1)S(1)}, bf16[384,256]{1,0:T(8,128)(2,1)S(1)}, u32[]{:S(2)}, u32[]{:S(2)}) collective-permute-start(bf16[384,256]{1,0:T(8,128)(2,1)S(1)} %bitcast.18), channel_id=1, source_target_pairs={{0,544},{32,512},{64,608},{96,576},{128,672},{160,640},{192,736},{... | collective-permute-start | bytes 589832 | tf_op jit(solution)/shard_map/ppermute | solution.py:21
  46.5 1.9 %collective-permute-start.3 = (bf16[384,256]{1,0:T(8,128)(2,1)S(1)}, bf16[384,256]{1,0:T(8,128)(2,1)S(1)}, u32[]{:S(2)}, u32[]{:S(2)}) collective-permute-start(bf16[384,256]{1,0:T(8,128)(2,1)S(1)} %bitcast.17), channel_id=1, source_target_pairs={{0,32},{32,0},{64,96},{96,64},{128,160},{160,128},{192,224},{224,1... | collective-permute-start | bytes 589832 | tf_op jit(solution)/shard_map/ppermute | solution.py:21
  48.4 4.5 %collective-permute-start.2 = (bf16[384,256]{1,0:T(8,128)(2,1)S(1)}, bf16[384,256]{1,0:T(8,128)(2,1)S(1)}, u32[]{:S(2)}, u32[]{:S(2)}) collective-permute-start(bf16[384,256]{1,0:T(8,128)(2,1)S(1)} %bitcast.16), channel_id=1, source_target_pairs={{0,512},{32,544},{64,576},{96,608},{128,640},{160,672},{192,704},{... | collective-permute-start | bytes 589832 | tf_op jit(solution)/shard_map/ppermute | solution.py:21
  52.9 0.8 collective-permute-done.4.refs_3_
  53.7 1.4 collective-permute-done.3.refs_2_
  55.1 3.1 %collective-permute-done.2.refs_1_ = bf16[384,256]{1,0:T(8,128)(2,1)S(1)} collective-permute-done((bf16[384,256]{1,0:T(8,128)(2,1)S(1)}, bf16[384,256]{1,0:T(8,128)(2,1)S(1)}, u32[]{:S(2)}, u32[]{:S(2)}) %collective-permute-start.2) | collective-permute-done | bytes 196640 | tf_op jit(solution)/shard_map/ppermute | solution.py:21
  58.2 0.0 collective-permute-done.1
  58.2 0.0 copy-done.3
  58.2 0.5 fusion.7.refs_4_
  58.6 2.9 %collective-permute-start.5 = (bf16[128,1536]{1,0:T(8,128)(2,1)S(1)}, bf16[128,1536]{1,0:T(8,128)(2,1)S(1)}, u32[]{:S(2)}, u32[]{:S(2)}) collective-permute-start(bf16[128,1536]{1,0:T(8,128)(2,1)S(1)} %fusion.7.refs_4_), channel_id=1, source_target_pairs={{0,8},{8,0},{16,24},{24,16},{1,9},{9,1},{17,25},{25,17},{2,10},{10... | collective-permute-start | bytes 1179656 | tf_op jit(solution)/shard_map/ppermute | solution.py:21
  61.5 2.8 %collective-permute-start.10 = (bf16[128,1536]{1,0:T(8,128)(2,1)S(1)}, bf16[128,1536]{1,0:T(8,128)(2,1)S(1)}, u32[]{:S(2)}, u32[]{:S(2)}) collective-permute-start(bf16[128,1536]{1,0:T(8,128)(2,1)S(1)} %fusion.7.refs_4_), channel_id=1, source_target_pairs={{0,544},{32,512},{64,608},{96,576},{128,672},{160,640},{192,736},{... | collective-permute-start | bytes 1179656 | tf_op jit(solution)/shard_map/ppermute | solution.py:21
  64.3 3.4 %collective-permute-start.8 = (bf16[128,1536]{1,0:T(8,128)(2,1)S(1)}, bf16[128,1536]{1,0:T(8,128)(2,1)S(1)}, u32[]{:S(2)}, u32[]{:S(2)}) collective-permute-start(bf16[128,1536]{1,0:T(8,128)(2,1)S(1)} %fusion.7.refs_4_), channel_id=1, source_target_pairs={{0,32},{32,0},{64,96},{96,64},{128,160},{160,128},{192,224},{224,1... | collective-permute-start | bytes 1179656 | tf_op jit(solution)/shard_map/ppermute | solution.py:21
  67.7 2.2 %collective-permute-start.6 = (bf16[128,1536]{1,0:T(8,128)(2,1)S(1)}, bf16[128,1536]{1,0:T(8,128)(2,1)S(1)}, u32[]{:S(2)}, u32[]{:S(2)}) collective-permute-start(bf16[128,1536]{1,0:T(8,128)(2,1)S(1)} %fusion.7.refs_4_), channel_id=1, source_target_pairs={{0,512},{32,544},{64,576},{96,608},{128,640},{160,672},{192,704},{... | collective-permute-start | bytes 1179656 | tf_op jit(solution)/shard_map/ppermute | solution.py:21
  69.9 0.0 collective-permute-done.5.refs_5_
  69.9 4.9 %fusion.8 = f32[256,1536]{1,0:T(8,128)} fusion(bf16[1536,1536]{1,0:T(8,128)(2,1)} %param.6, bf16[128,1536]{1,0:T(8,128)(2,1)S(1)} %collective-permute-done.5.refs_5_, bf16[128,1536]{1,0:T(8,128)(2,1)S(1)} %fusion.7.refs_4_, pred[]{:T(512)S(6)} %eq.7), kind=kOutput, calls=%fused_computation.24 | convolution fusion | flops 1211498496 | bytes 7077889 | tf_op jit(solution)/shard_map/dot_general | solution.py:29
  74.8 0.0 copy-done
  74.8 8.6 %collective-permute-done.8.refs_8_ = bf16[128,1536]{1,0:T(8,128)(2,1)S(1)} collective-permute-done((bf16[128,1536]{1,0:T(8,128)(2,1)S(1)}, bf16[128,1536]{1,0:T(8,128)(2,1)S(1)}, u32[]{:S(2)}, u32[]{:S(2)}) %collective-permute-start.8) | collective-permute-done | bytes 393248 | tf_op jit(solution)/shard_map/ppermute | solution.py:21
  83.5 0.0 reduce-scatter.2.cloned.1.call-update
  83.5 0.0 collective-permute-done.10.refs_10_
  83.5 2.7 %collective-permute-start.11 = (bf16[128,1536]{1,0:T(8,128)(2,1)S(1)}, bf16[128,1536]{1,0:T(8,128)(2,1)S(1)}, u32[]{:S(2)}, u32[]{:S(2)}) collective-permute-start(bf16[128,1536]{1,0:T(8,128)(2,1)S(1)} %collective-permute-done.10.refs_10_), channel_id=1, source_target_pairs={{0,8},{8,0},{16,24},{24,16},{1,9},{9,1},{17,25},{25,17},{2,10},{10... | collective-permute-start | bytes 1179656 | tf_op jit(solution)/shard_map/ppermute | solution.py:21
  86.2 0.0 collective-permute-done.6.refs_6_
  86.2 1.9 %collective-permute-start.7 = (bf16[128,1536]{1,0:T(8,128)(2,1)S(1)}, bf16[128,1536]{1,0:T(8,128)(2,1)S(1)}, u32[]{:S(2)}, u32[]{:S(2)}) collective-permute-start(bf16[128,1536]{1,0:T(8,128)(2,1)S(1)} %collective-permute-done.6.refs_6_), channel_id=1, source_target_pairs={{0,8},{8,0},{16,24},{24,16},{1,9},{9,1},{17,25},{25,17},{2,10},{10... | collective-permute-start | bytes 1179656 | tf_op jit(solution)/shard_map/ppermute | solution.py:21
  88.1 2.4 %collective-permute-start.9 = (bf16[128,1536]{1,0:T(8,128)(2,1)S(1)}, bf16[128,1536]{1,0:T(8,128)(2,1)S(1)}, u32[]{:S(2)}, u32[]{:S(2)}) collective-permute-start(bf16[128,1536]{1,0:T(8,128)(2,1)S(1)} %collective-permute-done.8.refs_8_), channel_id=1, source_target_pairs={{0,8},{8,0},{16,24},{24,16},{1,9},{9,1},{17,25},{25,17},{2,10},{10... | collective-permute-start | bytes 1179656 | tf_op jit(solution)/shard_map/ppermute | solution.py:21
  90.6 0.0 collective-permute-done.11.refs_11_
  90.6 0.0 collective-permute-done.7.refs_7_
  90.6 1.3 collective-permute-done.9.refs_9_
  91.9 0.9 copy-done.1
  92.8 2.9 %shard_map.59 = (bf16[48,1536]{1,0:T(8,128)(2,1)S(1)}, bf16[48,1536]{1,0:T(8,128)(2,1)S(1)}, bf16[48,1536]{1,0:T(8,128)(2,1)S(1)}, bf16[48,1536]{1,0:T(8,128)(2,...) custom-call(bf16[384,256]{1,0:T(8,128)(2,1)S(1)} %bitcast.14, ...), custom_call_target="tpu_custom_call" | custom-call | flops 1207959552 | bytes 5111808 | tf_op jit(solution)/shard_map/pallas_call | solution.py:55
  95.7 0.6 copy-done.2
  96.3 2.0 %collective-permute-start.15 = (bf16[48,1536]{1,0:T(8,128)(2,1)}, bf16[48,1536]{1,0:T(8,128)(2,1)S(1)}, u32[]{:S(2)}, u32[]{:S(2)}) collective-permute-start(bf16[48,1536]{1,0:T(8,128)(2,1)} %get-tuple-element.29), channel_id=1, source_target_pairs={{0,64},{32,96},{64,128},{96,160},{128,192},{160,224},{192,256},{22... | collective-permute-start | bytes 442376 | tf_op jit(solution)/shard_map/ppermute | solution.py:133
  98.4 0.1 dynamic_slice.34
  98.4 11.8 %collective-permute-start.12 = (bf16[48,1536]{1,0:T(8,128)(2,1)}, bf16[48,1536]{1,0:T(8,128)(2,1)S(1)}, u32[]{:S(2)}, u32[]{:S(2)}) collective-permute-start(bf16[48,1536]{1,0:T(8,128)(2,1)} %copy-done.2), channel_id=1, source_target_pairs={{0,448},{32,480},{64,0},{96,32},{128,64},{160,96},{192,128},{224,1... | collective-permute-start | bytes 442376 | tf_op jit(solution)/shard_map/ppermute | solution.py:133
  110.3 2.2 %collective-permute-done.15 = bf16[48,1536]{1,0:T(8,128)(2,1)S(1)} collective-permute-done((bf16[48,1536]{1,0:T(8,128)(2,1)}, bf16[48,1536]{1,0:T(8,128)(2,1)S(1)}, u32[]{:S(2)}, u32[]{:S(2)}) %collective-permute-start.15) | collective-permute-done | bytes 147488 | tf_op jit(solution)/shard_map/ppermute | solution.py:133
  112.5 1.9 %collective-permute-start.16 = (bf16[48,1536]{1,0:T(8,128)(2,1)S(1)}, bf16[48,1536]{1,0:T(8,128)(2,1)S(1)}, u32[]{:S(2)}, u32[]{:S(2)}) collective-permute-start(bf16[48,1536]{1,0:T(8,128)(2,1)S(1)} %add_convert_fusion.2), channel_id=1, source_target_pairs={{0,64},{32,96},{64,128},{96,160},{128,192},{160,224},{192,256},{22... | collective-permute-start | bytes 442376 | tf_op jit(solution)/shard_map/ppermute | solution.py:133
  114.5 2.0 %collective-permute-done.12 = bf16[48,1536]{1,0:T(8,128)(2,1)S(1)} collective-permute-done((bf16[48,1536]{1,0:T(8,128)(2,1)}, bf16[48,1536]{1,0:T(8,128)(2,1)S(1)}, u32[]{:S(2)}, u32[]{:S(2)}) %collective-permute-start.12) | collective-permute-done | bytes 147488 | tf_op jit(solution)/shard_map/ppermute | solution.py:133
  116.5 6.3 %collective-permute-start.13 = (bf16[48,1536]{1,0:T(8,128)(2,1)S(1)}, bf16[48,1536]{1,0:T(8,128)(2,1)S(1)}, u32[]{:S(2)}, u32[]{:S(2)}) collective-permute-start(bf16[48,1536]{1,0:T(8,128)(2,1)S(1)} %add_convert_fusion.4), channel_id=1, source_target_pairs={{0,448},{32,480},{64,0},{96,32},{128,64},{160,96},{192,128},{224,1... | collective-permute-start | bytes 442376 | tf_op jit(solution)/shard_map/ppermute | solution.py:133
  122.7 0.0 collective-permute-done.16
  122.8 1.9 %collective-permute-start.17 = (bf16[48,1536]{1,0:T(8,128)(2,1)S(1)}, bf16[48,1536]{1,0:T(8,128)(2,1)S(1)}, u32[]{:S(2)}, u32[]{:S(2)}) collective-permute-start(bf16[48,1536]{1,0:T(8,128)(2,1)S(1)} %add_convert_fusion.1), channel_id=1, source_target_pairs={{0,64},{32,96},{64,128},{96,160},{128,192},{160,224},{192,256},{22... | collective-permute-start | bytes 442376 | tf_op jit(solution)/shard_map/ppermute | solution.py:133
  124.7 0.1 collective-permute-done.13
  124.9 6.0 %collective-permute-start.14 = (bf16[48,1536]{1,0:T(8,128)(2,1)S(1)}, bf16[48,1536]{1,0:T(8,128)(2,1)S(1)}, u32[]{:S(2)}, u32[]{:S(2)}) collective-permute-start(bf16[48,1536]{1,0:T(8,128)(2,1)S(1)} %add_convert_fusion.3), channel_id=1, source_target_pairs={{0,448},{32,480},{64,0},{96,32},{128,64},{160,96},{192,128},{224,1... | collective-permute-start | bytes 442376 | tf_op jit(solution)/shard_map/ppermute | solution.py:133
  130.9 0.0 collective-permute-done.17
  130.9 0.0 reduce-scatter.2.cloned.1.call-done
  131.0 2.9 %collective-permute-start.18 = (bf16[48,1536]{1,0:T(8,128)(2,1)S(1)}, bf16[48,1536]{1,0:T(8,128)(2,1)S(1)}, u32[]{:S(2)}, u32[]{:S(2)}) collective-permute-start(bf16[48,1536]{1,0:T(8,128)(2,1)S(1)} %convert_add_fusion.1), channel_id=1, source_target_pairs={{0,64},{32,96},{64,128},{96,160},{128,192},{160,224},{192,256},{22... | collective-permute-start | bytes 442376 | tf_op jit(solution)/shard_map/ppermute | solution.py:133
  133.9 1.2 multiply_reduce_fusion.1
  135.0 11.4 %all-reduce = (f32[32]{0:T(128)S(1)}, f32[32]{0:T(128)S(1)}) all-reduce(f32[32]{0:T(128)S(1)} %get-tuple-element.39, f32[32]{0:T(128)S(1)} %get-tuple-element.38), channel_id=1, replica_groups=mesh['dp'=32,'mx'=4,'my'=8] {'mx'}, use_global_device_ids=true, to_apply=%region_8.9 | all-reduce | flops 64 | bytes 512 | tf_op jit(solution)/shard_map/psum | solution.py:146
  146.4 1.8 %multiply_convert_fusion.1 = bf16[32,1536]{1,0:T(8,128)(2,1)} fusion(f32[256,1536]{1,0:T(8,128)} %get-tuple-element.44, s32[]{:T(128)S(6)} %select_n.77, f32[32,1536]{1,0:T(8,128)} %reduce-scatter.2.cloned.1.call-done, f32[32]{0:T(128)S(1)} %get-tuple-element.54, f32[32]{0:T(128)S(1)} %get-tuple-element.55, f32[1536]{0:T(1024)S(1)} %copy-done.4, ...), kind=kLoop, calls=%fused_computation.48 | loop fusion | flops 294912 | bytes 498052 | tf_op jit(solution)/shard_map/convert_element_type | solution.py:152
  148.2 0.0 collective-permute-done.14
  148.2 0.0 collective-permute-done.18
  148.2 0.7 fusion.23
  (12 shorter events, 0.2 us)
Async XLA Ops:
  7.2 123.8 %reduce-scatter.2.cloned.1.call-start = ((), (), s32[]{:S(2)}) async-start(), calls=%async_computation.1 | async-start | bytes 1769472 | tf_op jit(solution)/shard_map/reduce_scatter | solution.py:124
  35.2 5.9 %collective-permute-start = (bf16[128,1536]{1,0:T(8,128)(2,1)S(1)}, bf16[128,1536]{1,0:T(8,128)(2,1)S(1)}, u32[]{:S(2)}, u32[]{:S(2)}) collective-permute-start(bf16[128,1536]{1,0:T(8,128)(2,1)S(1)} %convolution_convert_fusion), channel_id=1, source_target_pairs={{0,8},{8,0},{16,24},{24,16},{1,9},{9,1},{17,25},{25,17},{2,10},{10... | collective-permute-start | bytes 1179656 | tf_op jit(solution)/shard_map/ppermute | solution.py:21
  41.9 16.3 %collective-permute-start.1 = (bf16[128,1536]{1,0:T(8,128)(2,1)}, bf16[128,1536]{1,0:T(8,128)(2,1)S(1)}, u32[]{:S(2)}, u32[]{:S(2)}) collective-permute-start(bf16[128,1536]{1,0:T(8,128)(2,1)} %fusion.15), channel_id=1, source_target_pairs={{0,16},{8,24},{16,0},{24,8},{1,17},{9,25},{17,1},{25,9},{2,18},{10... | collective-permute-start | bytes 1179656 | tf_op jit(solution)/shard_map/ppermute | solution.py:21
  44.2 14.0 %copy-start.3 = (bf16[256,1536]{1,0:T(8,128)(2,1)S(1)}, bf16[256,1536]{1,0:T(8,128)(2,1)}, u32[]{:S(2)}) copy-start(bf16[256,1536]{1,0:T(8,128)(2,1)} %param.7) | copy-start | bytes 2359300
  44.6 9.1 %collective-permute-start.4 = (bf16[384,256]{1,0:T(8,128)(2,1)S(1)}, bf16[384,256]{1,0:T(8,128)(2,1)S(1)}, u32[]{:S(2)}, u32[]{:S(2)}) collective-permute-start(bf16[384,256]{1,0:T(8,128)(2,1)S(1)} %bitcast.18), channel_id=1, source_target_pairs={{0,544},{32,512},{64,608},{96,576},{128,672},{160,640},{192,736},{... | collective-permute-start | bytes 589832 | tf_op jit(solution)/shard_map/ppermute | solution.py:21
  46.5 8.6 %collective-permute-start.3 = (bf16[384,256]{1,0:T(8,128)(2,1)S(1)}, bf16[384,256]{1,0:T(8,128)(2,1)S(1)}, u32[]{:S(2)}, u32[]{:S(2)}) collective-permute-start(bf16[384,256]{1,0:T(8,128)(2,1)S(1)} %bitcast.17), channel_id=1, source_target_pairs={{0,32},{32,0},{64,96},{96,64},{128,160},{160,128},{192,224},{224,1... | collective-permute-start | bytes 589832 | tf_op jit(solution)/shard_map/ppermute | solution.py:21
  48.4 9.8 %collective-permute-start.2 = (bf16[384,256]{1,0:T(8,128)(2,1)S(1)}, bf16[384,256]{1,0:T(8,128)(2,1)S(1)}, u32[]{:S(2)}, u32[]{:S(2)}) collective-permute-start(bf16[384,256]{1,0:T(8,128)(2,1)S(1)} %bitcast.16), channel_id=1, source_target_pairs={{0,512},{32,544},{64,576},{96,608},{128,640},{160,672},{192,704},{... | collective-permute-start | bytes 589832 | tf_op jit(solution)/shard_map/ppermute | solution.py:21
  58.2 16.7 %copy-start = (bf16[384,256]{1,0:T(8,128)(2,1)}, bf16[384,256]{1,0:T(8,128)(2,1)S(1)}, u32[]{:S(2)}) copy-start(bf16[384,256]{1,0:T(8,128)(2,1)S(1)} %collective-permute-done.2.refs_1_) | copy-start | bytes 589828
  58.6 11.3 %collective-permute-start.5 = (bf16[128,1536]{1,0:T(8,128)(2,1)S(1)}, bf16[128,1536]{1,0:T(8,128)(2,1)S(1)}, u32[]{:S(2)}, u32[]{:S(2)}) collective-permute-start(bf16[128,1536]{1,0:T(8,128)(2,1)S(1)} %fusion.7.refs_4_), channel_id=1, source_target_pairs={{0,8},{8,0},{16,24},{24,16},{1,9},{9,1},{17,25},{25,17},{2,10},{10... | collective-permute-start | bytes 1179656 | tf_op jit(solution)/shard_map/ppermute | solution.py:21
  61.5 22.0 %collective-permute-start.10 = (bf16[128,1536]{1,0:T(8,128)(2,1)S(1)}, bf16[128,1536]{1,0:T(8,128)(2,1)S(1)}, u32[]{:S(2)}, u32[]{:S(2)}) collective-permute-start(bf16[128,1536]{1,0:T(8,128)(2,1)S(1)} %fusion.7.refs_4_), channel_id=1, source_target_pairs={{0,544},{32,512},{64,608},{96,576},{128,672},{160,640},{192,736},{... | collective-permute-start | bytes 1179656 | tf_op jit(solution)/shard_map/ppermute | solution.py:21
  64.3 19.2 %collective-permute-start.8 = (bf16[128,1536]{1,0:T(8,128)(2,1)S(1)}, bf16[128,1536]{1,0:T(8,128)(2,1)S(1)}, u32[]{:S(2)}, u32[]{:S(2)}) collective-permute-start(bf16[128,1536]{1,0:T(8,128)(2,1)S(1)} %fusion.7.refs_4_), channel_id=1, source_target_pairs={{0,32},{32,0},{64,96},{96,64},{128,160},{160,128},{192,224},{224,1... | collective-permute-start | bytes 1179656 | tf_op jit(solution)/shard_map/ppermute | solution.py:21
  67.7 18.5 %collective-permute-start.6 = (bf16[128,1536]{1,0:T(8,128)(2,1)S(1)}, bf16[128,1536]{1,0:T(8,128)(2,1)S(1)}, u32[]{:S(2)}, u32[]{:S(2)}) collective-permute-start(bf16[128,1536]{1,0:T(8,128)(2,1)S(1)} %fusion.7.refs_4_), channel_id=1, source_target_pairs={{0,512},{32,544},{64,576},{96,608},{128,640},{160,672},{192,704},{... | collective-permute-start | bytes 1179656 | tf_op jit(solution)/shard_map/ppermute | solution.py:21
  83.5 7.1 %collective-permute-start.11 = (bf16[128,1536]{1,0:T(8,128)(2,1)S(1)}, bf16[128,1536]{1,0:T(8,128)(2,1)S(1)}, u32[]{:S(2)}, u32[]{:S(2)}) collective-permute-start(bf16[128,1536]{1,0:T(8,128)(2,1)S(1)} %collective-permute-done.10.refs_10_), channel_id=1, source_target_pairs={{0,8},{8,0},{16,24},{24,16},{1,9},{9,1},{17,25},{25,17},{2,10},{10... | collective-permute-start | bytes 1179656 | tf_op jit(solution)/shard_map/ppermute | solution.py:21
  86.2 4.4 %collective-permute-start.7 = (bf16[128,1536]{1,0:T(8,128)(2,1)S(1)}, bf16[128,1536]{1,0:T(8,128)(2,1)S(1)}, u32[]{:S(2)}, u32[]{:S(2)}) collective-permute-start(bf16[128,1536]{1,0:T(8,128)(2,1)S(1)} %collective-permute-done.6.refs_6_), channel_id=1, source_target_pairs={{0,8},{8,0},{16,24},{24,16},{1,9},{9,1},{17,25},{25,17},{2,10},{10... | collective-permute-start | bytes 1179656 | tf_op jit(solution)/shard_map/ppermute | solution.py:21
  88.1 3.7 %collective-permute-start.9 = (bf16[128,1536]{1,0:T(8,128)(2,1)S(1)}, bf16[128,1536]{1,0:T(8,128)(2,1)S(1)}, u32[]{:S(2)}, u32[]{:S(2)}) collective-permute-start(bf16[128,1536]{1,0:T(8,128)(2,1)S(1)} %collective-permute-done.8.refs_8_), channel_id=1, source_target_pairs={{0,8},{8,0},{16,24},{24,16},{1,9},{9,1},{17,25},{25,17},{2,10},{10... | collective-permute-start | bytes 1179656 | tf_op jit(solution)/shard_map/ppermute | solution.py:21
  91.9 0.9 copy-start.1
  95.7 0.6 copy-start.2
  96.3 37.5 %copy-start.4 = (f32[1536]{0:T(1024)S(1)}, f32[1536]{0:T(1024)}, u32[]{:S(2)}) copy-start(f32[1536]{0:T(1024)} %param.5) | copy-start | bytes 18436
  96.3 16.2 %collective-permute-start.15 = (bf16[48,1536]{1,0:T(8,128)(2,1)}, bf16[48,1536]{1,0:T(8,128)(2,1)S(1)}, u32[]{:S(2)}, u32[]{:S(2)}) collective-permute-start(bf16[48,1536]{1,0:T(8,128)(2,1)} %get-tuple-element.29), channel_id=1, source_target_pairs={{0,64},{32,96},{64,128},{96,160},{128,192},{160,224},{192,256},{22... | collective-permute-start | bytes 442376 | tf_op jit(solution)/shard_map/ppermute | solution.py:133
  98.4 18.0 %collective-permute-start.12 = (bf16[48,1536]{1,0:T(8,128)(2,1)}, bf16[48,1536]{1,0:T(8,128)(2,1)S(1)}, u32[]{:S(2)}, u32[]{:S(2)}) collective-permute-start(bf16[48,1536]{1,0:T(8,128)(2,1)} %copy-done.2), channel_id=1, source_target_pairs={{0,448},{32,480},{64,0},{96,32},{128,64},{160,96},{192,128},{224,1... | collective-permute-start | bytes 442376 | tf_op jit(solution)/shard_map/ppermute | solution.py:133
  112.5 10.2 %collective-permute-start.16 = (bf16[48,1536]{1,0:T(8,128)(2,1)S(1)}, bf16[48,1536]{1,0:T(8,128)(2,1)S(1)}, u32[]{:S(2)}, u32[]{:S(2)}) collective-permute-start(bf16[48,1536]{1,0:T(8,128)(2,1)S(1)} %add_convert_fusion.2), channel_id=1, source_target_pairs={{0,64},{32,96},{64,128},{96,160},{128,192},{160,224},{192,256},{22... | collective-permute-start | bytes 442376 | tf_op jit(solution)/shard_map/ppermute | solution.py:133
  116.5 8.3 %collective-permute-start.13 = (bf16[48,1536]{1,0:T(8,128)(2,1)S(1)}, bf16[48,1536]{1,0:T(8,128)(2,1)S(1)}, u32[]{:S(2)}, u32[]{:S(2)}) collective-permute-start(bf16[48,1536]{1,0:T(8,128)(2,1)S(1)} %add_convert_fusion.4), channel_id=1, source_target_pairs={{0,448},{32,480},{64,0},{96,32},{128,64},{160,96},{192,128},{224,1... | collective-permute-start | bytes 442376 | tf_op jit(solution)/shard_map/ppermute | solution.py:133
  122.8 8.1 %collective-permute-start.17 = (bf16[48,1536]{1,0:T(8,128)(2,1)S(1)}, bf16[48,1536]{1,0:T(8,128)(2,1)S(1)}, u32[]{:S(2)}, u32[]{:S(2)}) collective-permute-start(bf16[48,1536]{1,0:T(8,128)(2,1)S(1)} %add_convert_fusion.1), channel_id=1, source_target_pairs={{0,64},{32,96},{64,128},{96,160},{128,192},{160,224},{192,256},{22... | collective-permute-start | bytes 442376 | tf_op jit(solution)/shard_map/ppermute | solution.py:133
  124.9 23.3 %collective-permute-start.14 = (bf16[48,1536]{1,0:T(8,128)(2,1)S(1)}, bf16[48,1536]{1,0:T(8,128)(2,1)S(1)}, u32[]{:S(2)}, u32[]{:S(2)}) collective-permute-start(bf16[48,1536]{1,0:T(8,128)(2,1)S(1)} %add_convert_fusion.3), channel_id=1, source_target_pairs={{0,448},{32,480},{64,0},{96,32},{128,64},{160,96},{192,128},{224,1... | collective-permute-start | bytes 442376 | tf_op jit(solution)/shard_map/ppermute | solution.py:133
  131.0 17.2 %collective-permute-start.18 = (bf16[48,1536]{1,0:T(8,128)(2,1)S(1)}, bf16[48,1536]{1,0:T(8,128)(2,1)S(1)}, u32[]{:S(2)}, u32[]{:S(2)}) collective-permute-start(bf16[48,1536]{1,0:T(8,128)(2,1)S(1)} %convert_add_fusion.1), channel_id=1, source_target_pairs={{0,64},{32,96},{64,128},{96,160},{128,192},{160,224},{192,256},{22... | collective-permute-start | bytes 442376 | tf_op jit(solution)/shard_map/ppermute | solution.py:133
Sparse Core Ops, SparseCore 0:
  83.6 46.3 reduce-scatter.1

commit v7 on v6

--- a/solution.py
+++ b/solution.py
@@ -107,7 +107,8 @@
 
     left = [columns(0, 0)]
     for bits in GROUP:
-        left.append(swap(columns(bits // 16, bits % 2), "dp", n_dp, bits))
+        left.append(columns(bits // 16, bits % 2))
+    left[2:] = [swap(piece, "dp", n_dp, bits) for piece, bits in zip(left[2:], GROUP[1:])]
     from_x, *left = lax.optimization_barrier((from_x, *left))
 
     pre = kept + from_x.astype(F32)
@@ -120,7 +121,9 @@
 
     in_order = jnp.where(core == 0, jnp.concatenate(right, axis=0), jnp.concatenate(right[::-1], axis=0))
     back = dot(in_order, in_weight, ((1,), (1,)))
-    back, arrived[1] = lax.optimization_barrier((back, arrived[1]))
+    back, left[1] = lax.optimization_barrier((back, left[1]))
+    left[1] = swap(left[1], "dp", n_dp, GROUP[0])
+    left[1], arrived[1] = lax.optimization_barrier((left[1], arrived[1]))
     dnormed = lax.psum_scatter(back, "my", scatter_dimension=0, tiled=True)
     own_rows = tok_rows // n_my
 

time: 157 us -> 155 us (0.987)
  waiting for transfers between devices: 19.5 us -> 16.1 us
    ppermute x12, waiting for transfers between devices: 15.2 us -> 11.8 us  [swap(): return lax.ppermute(value, axis, [(i, i ^ bits) for i in range(size)])]
  transfers between devices with their start and end apart: 20 -> 20, of which waited for: 8 -> 9; matrix products, arithmetic and copies ran while one was open for 8% -> 8% of each run, Pallas kernels for 2% -> 2%
where the time goes in v7:
time: 155 us; the launch traced here: 154 us
  starting transfers between devices  63.8 us (41%)
  blocking collectives  32.9 us (21%)
  waiting for transfers between devices  16.1 us (10%)
  between operations  14.5 us (9%)
  matrix products  11.1 us (7%)
  other arithmetic  9.53 us (6%)
  Pallas kernels  2.86 us (2%)
  local copies, waits for them, and re-layouts  2.65 us (2%)
    ppermute x12, starting transfers between devices, swap(): return lax.ppermute(value, axis, [(i, i ^ bits) for i in range(size)])  32.4 us
    ppermute x7, starting transfers between devices, hop(): return lax.ppermute(value.astype(BF), 'dp', perm).astype(F32)  31.4 us
    psum x1, blocking collectives, body(): lax.psum((jnp.sum(values, axis=1), jnp.sum(values * values, axis=1)), 'mx')  20.7 us
    psum x1, blocking collectives, body(): lax.psum((jnp.sum(dcentred, axis=1), jnp.sum(dcentred * centred_rows, axi...  12.2 us
    ppermute x12, waiting for transfers between devices, swap(): return lax.ppermute(value, axis, [(i, i ^ bits) for i in range(size)])  11.8 us
    dot_general x3, matrix products, dot(): return lax.dot_general(a, b, (dims, ((), ())), preferred_element_type=F32)  11.1 us
    ppermute x7, waiting for transfers between devices, hop(): return lax.ppermute(value.astype(BF), 'dp', perm).astype(F32)  4.3 us
  transfers between devices with their start and end apart: 20, of which 9 were waited for; matrix products, arithmetic and copies ran while one was open for 8% of the time, Pallas kernels for 2%

profile of v7, /device:TPU:1, one launch (start us, length us, event | category | flops | bytes accessed | tf_op | source)
XLA Modules:
  0.0 153.5 jit_solution(712252007345913140)
XLA Ops:
  7.2 0.0 reduce-scatter.2.cloned.1.call-start
  7.2 1.5 convert_reduce_fusion
  8.7 20.7 %all-reduce.1 = (f32[256]{0:T(256)S(1)}, f32[256]{0:T(256)S(1)}) all-reduce(f32[256]{0:T(256)S(1)} %get-tuple-element.41, f32[256]{0:T(256)S(1)} %get-tuple-element.40), channel_id=1, replica_groups=mesh['dp'=32,'mx'=4,'my'=8] {'mx'}, use_global_device_ids=true, to_apply=%region_3.4 | all-reduce | flops 512 | bytes 4096 | tf_op jit(solution)/shard_map/psum | solution.py:86
  29.4 2.6 %fusion = (f32[256,1536]{1,0:T(8,128)}, bf16[256,1536]{1,0:T(8,128)(2,1)S(1)}) fusion(bf16[256,1536]{1,0:T(8,128)(2,1)} %param.4, f32[256]{0:T(256)S(1)} %get-tuple-element.57, f32[256]{0:T(256)S(1)} %get-tuple-element.56, f32[1536]{0:T(1024)} %param.5), kind=kLoop, calls=%fused_computation.12 | loop fusion | flops 1966080 | bytes 3153920 | tf_op jit(solution)/shard_map/mul | solution.py:89
  32.0 3.1 %convolution_convert_fusion = bf16[128,1536]{1,0:T(8,128)(2,1)S(1)} fusion(bf16[1536,1536]{1,0:T(8,128)(2,1)} %param.6, bf16[256,1536]{1,0:T(8,128)(2,1)S(1)} %get-tuple-element.49, s32[]{:T(128)S(6)} %select_n.65), kind=kOutput, calls=%fused_computation | convolution fusion | flops 604176384 | bytes 5505028 | tf_op jit(solution)/shard_map/dot_general | solution.py:29
  35.2 2.7 %collective-permute-start = (bf16[128,1536]{1,0:T(8,128)(2,1)S(1)}, bf16[128,1536]{1,0:T(8,128)(2,1)S(1)}, u32[]{:S(2)}, u32[]{:S(2)}) collective-permute-start(bf16[128,1536]{1,0:T(8,128)(2,1)S(1)} %convolution_convert_fusion), channel_id=1, source_target_pairs={{0,8},{8,0},{16,24},{24,16},{1,9},{9,1},{17,25},{25,17},{2,10},{10... | collective-permute-start | bytes 1179656 | tf_op jit(solution)/shard_map/ppermute | solution.py:21
  37.8 3.1 %fusion.17 = f32[128,1536]{1,0:T(8,128)S(1)} fusion(bf16[1536,1536]{1,0:T(8,128)(2,1)} %param.6, bf16[256,1536]{1,0:T(8,128)(2,1)S(1)} %get-tuple-element.49, s32[]{:T(128)S(6)} %select_n.64), kind=kOutput, calls=%fused_computation.36 | convolution fusion | flops 603979776 | bytes 5898244 | tf_op jit(solution)/shard_map/dot_general | solution.py:29
  41.0 0.1 dynamic-slice_bitcast_fusion.1
  41.0 0.0 collective-permute-done
  41.0 0.1 fusion.15
  41.1 1.9 %collective-permute-start.1 = (bf16[128,1536]{1,0:T(8,128)(2,1)S(1)}, bf16[128,1536]{1,0:T(8,128)(2,1)S(1)}, u32[]{:S(2)}, u32[]{:S(2)}) collective-permute-start(bf16[128,1536]{1,0:T(8,128)(2,1)S(1)} %fusion.15), channel_id=1, source_target_pairs={{0,16},{8,24},{16,0},{24,8},{1,17},{9,25},{17,1},{25,9},{2,18},{10... | collective-permute-start | bytes 1179656 | tf_op jit(solution)/shard_map/ppermute | solution.py:21
  43.0 0.1 pad_maximum_fusion
  43.2 0.3 copy.8
  43.5 0.0 copy-start.3
  43.5 1.0 fusion.19
  44.5 1.9 %collective-permute-start.3 = (bf16[384,256]{1,0:T(8,128)(2,1)S(1)}, bf16[384,256]{1,0:T(8,128)(2,1)S(1)}, u32[]{:S(2)}, u32[]{:S(2)}) collective-permute-start(bf16[384,256]{1,0:T(8,128)(2,1)S(1)} %bitcast.18), channel_id=1, source_target_pairs={{0,544},{32,512},{64,608},{96,576},{128,672},{160,640},{192,736},{... | collective-permute-start | bytes 589832 | tf_op jit(solution)/shard_map/ppermute | solution.py:21
  46.4 1.9 %collective-permute-start.2 = (bf16[384,256]{1,0:T(8,128)(2,1)S(1)}, bf16[384,256]{1,0:T(8,128)(2,1)S(1)}, u32[]{:S(2)}, u32[]{:S(2)}) collective-permute-start(bf16[384,256]{1,0:T(8,128)(2,1)S(1)} %bitcast.17), channel_id=1, source_target_pairs={{0,32},{32,0},{64,96},{96,64},{128,160},{160,128},{192,224},{224,1... | collective-permute-start | bytes 589832 | tf_op jit(solution)/shard_map/ppermute | solution.py:21
  48.3 5.3 %collective-permute-done.3.refs_3_ = bf16[384,256]{1,0:T(8,128)(2,1)S(1)} collective-permute-done((bf16[384,256]{1,0:T(8,128)(2,1)S(1)}, bf16[384,256]{1,0:T(8,128)(2,1)S(1)}, u32[]{:S(2)}, u32[]{:S(2)}) %collective-permute-start.3) | collective-permute-done | bytes 196640 | tf_op jit(solution)/shard_map/ppermute | solution.py:21
  53.6 1.4 collective-permute-done.2.refs_2_
  55.0 0.3 collective-permute-done.1
  55.2 0.0 copy-done.3
  55.3 0.5 fusion.7.refs_4_
  55.7 2.7 %collective-permute-start.4 = (bf16[128,1536]{1,0:T(8,128)(2,1)S(1)}, bf16[128,1536]{1,0:T(8,128)(2,1)S(1)}, u32[]{:S(2)}, u32[]{:S(2)}) collective-permute-start(bf16[128,1536]{1,0:T(8,128)(2,1)S(1)} %fusion.7.refs_4_), channel_id=1, source_target_pairs={{0,8},{8,0},{16,24},{24,16},{1,9},{9,1},{17,25},{25,17},{2,10},{10... | collective-permute-start | bytes 1179656 | tf_op jit(solution)/shard_map/ppermute | solution.py:21
  58.4 4.1 %collective-permute-start.10 = (bf16[128,1536]{1,0:T(8,128)(2,1)S(1)}, bf16[128,1536]{1,0:T(8,128)(2,1)S(1)}, u32[]{:S(2)}, u32[]{:S(2)}) collective-permute-start(bf16[128,1536]{1,0:T(8,128)(2,1)S(1)} %fusion.7.refs_4_), channel_id=1, source_target_pairs={{0,544},{32,512},{64,608},{96,576},{128,672},{160,640},{192,736},{... | collective-permute-start | bytes 1179656 | tf_op jit(solution)/shard_map/ppermute | solution.py:21
  62.5 2.9 %collective-permute-start.7 = (bf16[128,1536]{1,0:T(8,128)(2,1)S(1)}, bf16[128,1536]{1,0:T(8,128)(2,1)S(1)}, u32[]{:S(2)}, u32[]{:S(2)}) collective-permute-start(bf16[128,1536]{1,0:T(8,128)(2,1)S(1)} %fusion.7.refs_4_), channel_id=1, source_target_pairs={{0,512},{32,544},{64,576},{96,608},{128,640},{160,672},{192,704},{... | collective-permute-start | bytes 1179656 | tf_op jit(solution)/shard_map/ppermute | solution.py:21
  65.4 3.1 %collective-permute-start.6 = (bf16[128,1536]{1,0:T(8,128)(2,1)S(1)}, bf16[128,1536]{1,0:T(8,128)(2,1)S(1)}, u32[]{:S(2)}, u32[]{:S(2)}) collective-permute-start(bf16[128,1536]{1,0:T(8,128)(2,1)S(1)} %fusion.7.refs_4_), channel_id=1, source_target_pairs={{0,32},{32,0},{64,96},{96,64},{128,160},{160,128},{192,224},{224,1... | collective-permute-start | bytes 1179656 | tf_op jit(solution)/shard_map/ppermute | solution.py:21
  68.5 0.0 collective-permute-done.4.refs_5_
  68.6 4.9 %fusion.8 = f32[256,1536]{1,0:T(8,128)} fusion(bf16[1536,1536]{1,0:T(8,128)(2,1)} %param.6, bf16[128,1536]{1,0:T(8,128)(2,1)S(1)} %collective-permute-done.4.refs_5_, bf16[128,1536]{1,0:T(8,128)(2,1)S(1)} %fusion.7.refs_4_, pred[]{:T(512)S(6)} %eq.7), kind=kOutput, calls=%fused_computation.24 | convolution fusion | flops 1211498496 | bytes 7077889 | tf_op jit(solution)/shard_map/dot_general | solution.py:29
  73.5 3.4 %collective-permute-start.5 = (bf16[384,256]{1,0:T(8,128)(2,1)S(1)}, bf16[384,256]{1,0:T(8,128)(2,1)S(1)}, u32[]{:S(2)}, u32[]{:S(2)}) collective-permute-start(bf16[384,256]{1,0:T(8,128)(2,1)S(1)} %bitcast.16), channel_id=1, source_target_pairs={{0,512},{32,544},{64,576},{96,608},{128,640},{160,672},{192,704},{... | collective-permute-start | bytes 589832 | tf_op jit(solution)/shard_map/ppermute | solution.py:21
  76.8 0.0 reduce-scatter.2.cloned.1.call-update
  76.8 0.0 collective-permute-done.10.refs_10_
  76.9 3.0 %collective-permute-start.11 = (bf16[128,1536]{1,0:T(8,128)(2,1)S(1)}, bf16[128,1536]{1,0:T(8,128)(2,1)S(1)}, u32[]{:S(2)}, u32[]{:S(2)}) collective-permute-start(bf16[128,1536]{1,0:T(8,128)(2,1)S(1)} %collective-permute-done.10.refs_10_), channel_id=1, source_target_pairs={{0,8},{8,0},{16,24},{24,16},{1,9},{9,1},{17,25},{25,17},{2,10},{10... | collective-permute-start | bytes 1179656 | tf_op jit(solution)/shard_map/ppermute | solution.py:21
  79.9 1.8 %collective-permute-done.7.refs_6_ = bf16[128,1536]{1,0:T(8,128)(2,1)S(1)} collective-permute-done((bf16[128,1536]{1,0:T(8,128)(2,1)S(1)}, bf16[128,1536]{1,0:T(8,128)(2,1)S(1)}, u32[]{:S(2)}, u32[]{:S(2)}) %collective-permute-start.7) | collective-permute-done | bytes 393248 | tf_op jit(solution)/shard_map/ppermute | solution.py:21
  81.7 2.4 %collective-permute-start.8 = (bf16[128,1536]{1,0:T(8,128)(2,1)S(1)}, bf16[128,1536]{1,0:T(8,128)(2,1)S(1)}, u32[]{:S(2)}, u32[]{:S(2)}) collective-permute-start(bf16[128,1536]{1,0:T(8,128)(2,1)S(1)} %collective-permute-done.7.refs_6_), channel_id=1, source_target_pairs={{0,8},{8,0},{16,24},{24,16},{1,9},{9,1},{17,25},{25,17},{2,10},{10... | collective-permute-start | bytes 1179656 | tf_op jit(solution)/shard_map/ppermute | solution.py:21
  84.1 0.0 collective-permute-done.6.refs_8_
  84.1 1.8 %collective-permute-done.5.refs_1_ = bf16[384,256]{1,0:T(8,128)(2,1)S(1)} collective-permute-done((bf16[384,256]{1,0:T(8,128)(2,1)S(1)}, bf16[384,256]{1,0:T(8,128)(2,1)S(1)}, u32[]{:S(2)}, u32[]{:S(2)}) %collective-permute-start.5) | collective-permute-done | bytes 196640 | tf_op jit(solution)/shard_map/ppermute | solution.py:21
  85.9 0.7 copy-done
  86.6 2.4 %collective-permute-start.9 = (bf16[128,1536]{1,0:T(8,128)(2,1)S(1)}, bf16[128,1536]{1,0:T(8,128)(2,1)S(1)}, u32[]{:S(2)}, u32[]{:S(2)}) collective-permute-start(bf16[128,1536]{1,0:T(8,128)(2,1)S(1)} %collective-permute-done.6.refs_8_), channel_id=1, source_target_pairs={{0,8},{8,0},{16,24},{24,16},{1,9},{9,1},{17,25},{25,17},{2,10},{10... | collective-permute-start | bytes 1179656 | tf_op jit(solution)/shard_map/ppermute | solution.py:21
  88.9 0.0 collective-permute-done.11.refs_11_
  88.9 0.0 collective-permute-done.8.refs_7_
  89.0 1.3 collective-permute-done.9.refs_9_
  90.3 0.9 copy-done.1
  91.2 2.9 %shard_map.59 = (bf16[48,1536]{1,0:T(8,128)(2,1)S(1)}, bf16[48,1536]{1,0:T(8,128)(2,1)S(1)}, bf16[48,1536]{1,0:T(8,128)(2,1)S(1)}, bf16[48,1536]{1,0:T(8,128)(2,...) custom-call(bf16[384,256]{1,0:T(8,128)(2,1)S(1)} %bitcast.14, ...), custom_call_target="tpu_custom_call" | custom-call | flops 1207959552 | bytes 5111808 | tf_op jit(solution)/shard_map/pallas_call | solution.py:55
  94.1 0.6 copy-done.2
  94.7 2.0 %collective-permute-start.15 = (bf16[48,1536]{1,0:T(8,128)(2,1)}, bf16[48,1536]{1,0:T(8,128)(2,1)S(1)}, u32[]{:S(2)}, u32[]{:S(2)}) collective-permute-start(bf16[48,1536]{1,0:T(8,128)(2,1)} %get-tuple-element.33), channel_id=1, source_target_pairs={{0,64},{32,96},{64,128},{96,160},{128,192},{160,224},{192,256},{22... | collective-permute-start | bytes 442376 | tf_op jit(solution)/shard_map/ppermute | solution.py:136
  96.8 0.1 dynamic_slice.34
  96.8 11.3 %collective-permute-start.12 = (bf16[48,1536]{1,0:T(8,128)(2,1)}, bf16[48,1536]{1,0:T(8,128)(2,1)S(1)}, u32[]{:S(2)}, u32[]{:S(2)}) collective-permute-start(bf16[48,1536]{1,0:T(8,128)(2,1)} %copy-done.2), channel_id=1, source_target_pairs={{0,448},{32,480},{64,0},{96,32},{128,64},{160,96},{192,128},{224,1... | collective-permute-start | bytes 442376 | tf_op jit(solution)/shard_map/ppermute | solution.py:136
  108.1 2.2 %collective-permute-done.15 = bf16[48,1536]{1,0:T(8,128)(2,1)S(1)} collective-permute-done((bf16[48,1536]{1,0:T(8,128)(2,1)}, bf16[48,1536]{1,0:T(8,128)(2,1)S(1)}, u32[]{:S(2)}, u32[]{:S(2)}) %collective-permute-start.15) | collective-permute-done | bytes 147488 | tf_op jit(solution)/shard_map/ppermute | solution.py:136
  110.4 1.9 %collective-permute-start.16 = (bf16[48,1536]{1,0:T(8,128)(2,1)S(1)}, bf16[48,1536]{1,0:T(8,128)(2,1)S(1)}, u32[]{:S(2)}, u32[]{:S(2)}) collective-permute-start(bf16[48,1536]{1,0:T(8,128)(2,1)S(1)} %add_convert_fusion.2), channel_id=1, source_target_pairs={{0,64},{32,96},{64,128},{96,160},{128,192},{160,224},{192,256},{22... | collective-permute-start | bytes 442376 | tf_op jit(solution)/shard_map/ppermute | solution.py:136
  112.3 2.0 %collective-permute-done.12 = bf16[48,1536]{1,0:T(8,128)(2,1)S(1)} collective-permute-done((bf16[48,1536]{1,0:T(8,128)(2,1)}, bf16[48,1536]{1,0:T(8,128)(2,1)S(1)}, u32[]{:S(2)}, u32[]{:S(2)}) %collective-permute-start.12) | collective-permute-done | bytes 147488 | tf_op jit(solution)/shard_map/ppermute | solution.py:136
  114.4 6.3 %collective-permute-start.13 = (bf16[48,1536]{1,0:T(8,128)(2,1)S(1)}, bf16[48,1536]{1,0:T(8,128)(2,1)S(1)}, u32[]{:S(2)}, u32[]{:S(2)}) collective-permute-start(bf16[48,1536]{1,0:T(8,128)(2,1)S(1)} %add_convert_fusion.4), channel_id=1, source_target_pairs={{0,448},{32,480},{64,0},{96,32},{128,64},{160,96},{192,128},{224,1... | collective-permute-start | bytes 442376 | tf_op jit(solution)/shard_map/ppermute | solution.py:136
  120.6 0.0 collective-permute-done.16
  120.7 1.9 %collective-permute-start.17 = (bf16[48,1536]{1,0:T(8,128)(2,1)S(1)}, bf16[48,1536]{1,0:T(8,128)(2,1)S(1)}, u32[]{:S(2)}, u32[]{:S(2)}) collective-permute-start(bf16[48,1536]{1,0:T(8,128)(2,1)S(1)} %add_convert_fusion.1), channel_id=1, source_target_pairs={{0,64},{32,96},{64,128},{96,160},{128,192},{160,224},{192,256},{22... | collective-permute-start | bytes 442376 | tf_op jit(solution)/shard_map/ppermute | solution.py:136
  122.6 0.1 collective-permute-done.13
  122.7 6.0 %collective-permute-start.14 = (bf16[48,1536]{1,0:T(8,128)(2,1)S(1)}, bf16[48,1536]{1,0:T(8,128)(2,1)S(1)}, u32[]{:S(2)}, u32[]{:S(2)}) collective-permute-start(bf16[48,1536]{1,0:T(8,128)(2,1)S(1)} %add_convert_fusion.3), channel_id=1, source_target_pairs={{0,448},{32,480},{64,0},{96,32},{128,64},{160,96},{192,128},{224,1... | collective-permute-start | bytes 442376 | tf_op jit(solution)/shard_map/ppermute | solution.py:136
  128.8 0.0 collective-permute-done.17
  128.8 0.0 reduce-scatter.2.cloned.1.call-done
  128.8 1.9 %collective-permute-start.18 = (bf16[48,1536]{1,0:T(8,128)(2,1)S(1)}, bf16[48,1536]{1,0:T(8,128)(2,1)S(1)}, u32[]{:S(2)}, u32[]{:S(2)}) collective-permute-start(bf16[48,1536]{1,0:T(8,128)(2,1)S(1)} %convert_add_fusion.1), channel_id=1, source_target_pairs={{0,64},{32,96},{64,128},{96,160},{128,192},{160,224},{192,256},{22... | collective-permute-start | bytes 442376 | tf_op jit(solution)/shard_map/ppermute | solution.py:136
  130.8 1.2 multiply_reduce_fusion.1
  131.9 12.2 %all-reduce = (f32[32]{0:T(128)S(1)}, f32[32]{0:T(128)S(1)}) all-reduce(f32[32]{0:T(128)S(1)} %get-tuple-element.43, f32[32]{0:T(128)S(1)} %get-tuple-element.42), channel_id=1, replica_groups=mesh['dp'=32,'mx'=4,'my'=8] {'mx'}, use_global_device_ids=true, to_apply=%region_8.9 | all-reduce | flops 64 | bytes 512 | tf_op jit(solution)/shard_map/psum | solution.py:149
  144.2 1.8 %multiply_convert_fusion.1 = bf16[32,1536]{1,0:T(8,128)(2,1)} fusion(f32[256,1536]{1,0:T(8,128)} %get-tuple-element.48, s32[]{:T(128)S(6)} %select_n.77, f32[32,1536]{1,0:T(8,128)} %reduce-scatter.2.cloned.1.call-done, f32[32]{0:T(128)S(1)} %get-tuple-element.58, f32[32]{0:T(128)S(1)} %get-tuple-element.59, f32[1536]{0:T(1024)S(1)} %copy-done.5, ...), kind=kLoop, calls=%fused_computation.48 | loop fusion | flops 294912 | bytes 498052 | tf_op jit(solution)/shard_map/convert_element_type | solution.py:155
  146.0 0.0 collective-permute-done.14
  146.0 0.0 collective-permute-done.18
  146.0 0.7 fusion.23
  (14 shorter events, 0.2 us)
Async XLA Ops:
  7.2 121.7 %reduce-scatter.2.cloned.1.call-start = ((), (), s32[]{:S(2)}) async-start(), calls=%async_computation.1 | async-start | bytes 1769472 | tf_op jit(solution)/shard_map/reduce_scatter | solution.py:127
  35.2 5.9 %collective-permute-start = (bf16[128,1536]{1,0:T(8,128)(2,1)S(1)}, bf16[128,1536]{1,0:T(8,128)(2,1)S(1)}, u32[]{:S(2)}, u32[]{:S(2)}) collective-permute-start(bf16[128,1536]{1,0:T(8,128)(2,1)S(1)} %convolution_convert_fusion), channel_id=1, source_target_pairs={{0,8},{8,0},{16,24},{24,16},{1,9},{9,1},{17,25},{25,17},{2,10},{10... | collective-permute-start | bytes 1179656 | tf_op jit(solution)/shard_map/ppermute | solution.py:21
  41.1 14.1 %collective-permute-start.1 = (bf16[128,1536]{1,0:T(8,128)(2,1)S(1)}, bf16[128,1536]{1,0:T(8,128)(2,1)S(1)}, u32[]{:S(2)}, u32[]{:S(2)}) collective-permute-start(bf16[128,1536]{1,0:T(8,128)(2,1)S(1)} %fusion.15), channel_id=1, source_target_pairs={{0,16},{8,24},{16,0},{24,8},{1,17},{9,25},{17,1},{25,9},{2,18},{10... | collective-permute-start | bytes 1179656 | tf_op jit(solution)/shard_map/ppermute | solution.py:21
  43.5 11.8 %copy-start.3 = (bf16[256,1536]{1,0:T(8,128)(2,1)S(1)}, bf16[256,1536]{1,0:T(8,128)(2,1)}, u32[]{:S(2)}) copy-start(bf16[256,1536]{1,0:T(8,128)(2,1)} %param.7) | copy-start | bytes 2359300
  44.5 9.1 %collective-permute-start.3 = (bf16[384,256]{1,0:T(8,128)(2,1)S(1)}, bf16[384,256]{1,0:T(8,128)(2,1)S(1)}, u32[]{:S(2)}, u32[]{:S(2)}) collective-permute-start(bf16[384,256]{1,0:T(8,128)(2,1)S(1)} %bitcast.18), channel_id=1, source_target_pairs={{0,544},{32,512},{64,608},{96,576},{128,672},{160,640},{192,736},{... | collective-permute-start | bytes 589832 | tf_op jit(solution)/shard_map/ppermute | solution.py:21
  46.4 8.6 %collective-permute-start.2 = (bf16[384,256]{1,0:T(8,128)(2,1)S(1)}, bf16[384,256]{1,0:T(8,128)(2,1)S(1)}, u32[]{:S(2)}, u32[]{:S(2)}) collective-permute-start(bf16[384,256]{1,0:T(8,128)(2,1)S(1)} %bitcast.17), channel_id=1, source_target_pairs={{0,32},{32,0},{64,96},{96,64},{128,160},{160,128},{192,224},{224,1... | collective-permute-start | bytes 589832 | tf_op jit(solution)/shard_map/ppermute | solution.py:21
  55.7 12.8 %collective-permute-start.4 = (bf16[128,1536]{1,0:T(8,128)(2,1)S(1)}, bf16[128,1536]{1,0:T(8,128)(2,1)S(1)}, u32[]{:S(2)}, u32[]{:S(2)}) collective-permute-start(bf16[128,1536]{1,0:T(8,128)(2,1)S(1)} %fusion.7.refs_4_), channel_id=1, source_target_pairs={{0,8},{8,0},{16,24},{24,16},{1,9},{9,1},{17,25},{25,17},{2,10},{10... | collective-permute-start | bytes 1179656 | tf_op jit(solution)/shard_map/ppermute | solution.py:21
  58.4 15.0 %copy-start.4 = (bf16[1,8,1,48,256]{4,3,2,1,0:T(8,128)(2,1)S(1)}, bf16[1,8,1,48,256]{4,3,2,1,0:T(8,128)(2,1)}, u32[]{:S(2)}) copy-start(bf16[1,8,1,48,256]{4,3,2,1,0:T(8,128)(2,1)} %get-tuple-element.53) | copy-start | bytes 589828
  58.4 18.4 %collective-permute-start.10 = (bf16[128,1536]{1,0:T(8,128)(2,1)S(1)}, bf16[128,1536]{1,0:T(8,128)(2,1)S(1)}, u32[]{:S(2)}, u32[]{:S(2)}) collective-permute-start(bf16[128,1536]{1,0:T(8,128)(2,1)S(1)} %fusion.7.refs_4_), channel_id=1, source_target_pairs={{0,544},{32,512},{64,608},{96,576},{128,672},{160,640},{192,736},{... | collective-permute-start | bytes 1179656 | tf_op jit(solution)/shard_map/ppermute | solution.py:21
  62.5 19.2 %collective-permute-start.7 = (bf16[128,1536]{1,0:T(8,128)(2,1)S(1)}, bf16[128,1536]{1,0:T(8,128)(2,1)S(1)}, u32[]{:S(2)}, u32[]{:S(2)}) collective-permute-start(bf16[128,1536]{1,0:T(8,128)(2,1)S(1)} %fusion.7.refs_4_), channel_id=1, source_target_pairs={{0,512},{32,544},{64,576},{96,608},{128,640},{160,672},{192,704},{... | collective-permute-start | bytes 1179656 | tf_op jit(solution)/shard_map/ppermute | solution.py:21
  65.4 18.7 %collective-permute-start.6 = (bf16[128,1536]{1,0:T(8,128)(2,1)S(1)}, bf16[128,1536]{1,0:T(8,128)(2,1)S(1)}, u32[]{:S(2)}, u32[]{:S(2)}) collective-permute-start(bf16[128,1536]{1,0:T(8,128)(2,1)S(1)} %fusion.7.refs_4_), channel_id=1, source_target_pairs={{0,32},{32,0},{64,96},{96,64},{128,160},{160,128},{192,224},{224,1... | collective-permute-start | bytes 1179656 | tf_op jit(solution)/shard_map/ppermute | solution.py:21
  73.5 12.4 %collective-permute-start.5 = (bf16[384,256]{1,0:T(8,128)(2,1)S(1)}, bf16[384,256]{1,0:T(8,128)(2,1)S(1)}, u32[]{:S(2)}, u32[]{:S(2)}) collective-permute-start(bf16[384,256]{1,0:T(8,128)(2,1)S(1)} %bitcast.16), channel_id=1, source_target_pairs={{0,512},{32,544},{64,576},{96,608},{128,640},{160,672},{192,704},{... | collective-permute-start | bytes 589832 | tf_op jit(solution)/shard_map/ppermute | solution.py:21
  76.9 12.1 %collective-permute-start.11 = (bf16[128,1536]{1,0:T(8,128)(2,1)S(1)}, bf16[128,1536]{1,0:T(8,128)(2,1)S(1)}, u32[]{:S(2)}, u32[]{:S(2)}) collective-permute-start(bf16[128,1536]{1,0:T(8,128)(2,1)S(1)} %collective-permute-done.10.refs_10_), channel_id=1, source_target_pairs={{0,8},{8,0},{16,24},{24,16},{1,9},{9,1},{17,25},{25,17},{2,10},{10... | collective-permute-start | bytes 1179656 | tf_op jit(solution)/shard_map/ppermute | solution.py:21
  81.7 7.3 %collective-permute-start.8 = (bf16[128,1536]{1,0:T(8,128)(2,1)S(1)}, bf16[128,1536]{1,0:T(8,128)(2,1)S(1)}, u32[]{:S(2)}, u32[]{:S(2)}) collective-permute-start(bf16[128,1536]{1,0:T(8,128)(2,1)S(1)} %collective-permute-done.7.refs_6_), channel_id=1, source_target_pairs={{0,8},{8,0},{16,24},{24,16},{1,9},{9,1},{17,25},{25,17},{2,10},{10... | collective-permute-start | bytes 1179656 | tf_op jit(solution)/shard_map/ppermute | solution.py:21
  85.9 0.7 copy-start
  86.6 3.7 %collective-permute-start.9 = (bf16[128,1536]{1,0:T(8,128)(2,1)S(1)}, bf16[128,1536]{1,0:T(8,128)(2,1)S(1)}, u32[]{:S(2)}, u32[]{:S(2)}) collective-permute-start(bf16[128,1536]{1,0:T(8,128)(2,1)S(1)} %collective-permute-done.6.refs_8_), channel_id=1, source_target_pairs={{0,8},{8,0},{16,24},{24,16},{1,9},{9,1},{17,25},{25,17},{2,10},{10... | collective-permute-start | bytes 1179656 | tf_op jit(solution)/shard_map/ppermute | solution.py:21
  90.3 0.9 copy-start.1
  94.1 0.6 copy-start.2
  94.7 36.1 %copy-start.5 = (f32[1536]{0:T(1024)S(1)}, f32[1536]{0:T(1024)}, u32[]{:S(2)}) copy-start(f32[1536]{0:T(1024)} %param.5) | copy-start | bytes 18436
  94.7 15.7 %collective-permute-start.15 = (bf16[48,1536]{1,0:T(8,128)(2,1)}, bf16[48,1536]{1,0:T(8,128)(2,1)S(1)}, u32[]{:S(2)}, u32[]{:S(2)}) collective-permute-start(bf16[48,1536]{1,0:T(8,128)(2,1)} %get-tuple-element.33), channel_id=1, source_target_pairs={{0,64},{32,96},{64,128},{96,160},{128,192},{160,224},{192,256},{22... | collective-permute-start | bytes 442376 | tf_op jit(solution)/shard_map/ppermute | solution.py:136
  96.8 17.5 %collective-permute-start.12 = (bf16[48,1536]{1,0:T(8,128)(2,1)}, bf16[48,1536]{1,0:T(8,128)(2,1)S(1)}, u32[]{:S(2)}, u32[]{:S(2)}) collective-permute-start(bf16[48,1536]{1,0:T(8,128)(2,1)} %copy-done.2), channel_id=1, source_target_pairs={{0,448},{32,480},{64,0},{96,32},{128,64},{160,96},{192,128},{224,1... | collective-permute-start | bytes 442376 | tf_op jit(solution)/shard_map/ppermute | solution.py:136
  110.4 10.2 %collective-permute-start.16 = (bf16[48,1536]{1,0:T(8,128)(2,1)S(1)}, bf16[48,1536]{1,0:T(8,128)(2,1)S(1)}, u32[]{:S(2)}, u32[]{:S(2)}) collective-permute-start(bf16[48,1536]{1,0:T(8,128)(2,1)S(1)} %add_convert_fusion.2), channel_id=1, source_target_pairs={{0,64},{32,96},{64,128},{96,160},{128,192},{160,224},{192,256},{22... | collective-permute-start | bytes 442376 | tf_op jit(solution)/shard_map/ppermute | solution.py:136
  114.4 8.3 %collective-permute-start.13 = (bf16[48,1536]{1,0:T(8,128)(2,1)S(1)}, bf16[48,1536]{1,0:T(8,128)(2,1)S(1)}, u32[]{:S(2)}, u32[]{:S(2)}) collective-permute-start(bf16[48,1536]{1,0:T(8,128)(2,1)S(1)} %add_convert_fusion.4), channel_id=1, source_target_pairs={{0,448},{32,480},{64,0},{96,32},{128,64},{160,96},{192,128},{224,1... | collective-permute-start | bytes 442376 | tf_op jit(solution)/shard_map/ppermute | solution.py:136
  120.7 8.1 %collective-permute-start.17 = (bf16[48,1536]{1,0:T(8,128)(2,1)S(1)}, bf16[48,1536]{1,0:T(8,128)(2,1)S(1)}, u32[]{:S(2)}, u32[]{:S(2)}) collective-permute-start(bf16[48,1536]{1,0:T(8,128)(2,1)S(1)} %add_convert_fusion.1), channel_id=1, source_target_pairs={{0,64},{32,96},{64,128},{96,160},{128,192},{160,224},{192,256},{22... | collective-permute-start | bytes 442376 | tf_op jit(solution)/shard_map/ppermute | solution.py:136
  122.7 23.2 %collective-permute-start.14 = (bf16[48,1536]{1,0:T(8,128)(2,1)S(1)}, bf16[48,1536]{1,0:T(8,128)(2,1)S(1)}, u32[]{:S(2)}, u32[]{:S(2)}) collective-permute-start(bf16[48,1536]{1,0:T(8,128)(2,1)S(1)} %add_convert_fusion.3), channel_id=1, source_target_pairs={{0,448},{32,480},{64,0},{96,32},{128,64},{160,96},{192,128},{224,1... | collective-permute-start | bytes 442376 | tf_op jit(solution)/shard_map/ppermute | solution.py:136
  128.8 17.1 %collective-permute-start.18 = (bf16[48,1536]{1,0:T(8,128)(2,1)S(1)}, bf16[48,1536]{1,0:T(8,128)(2,1)S(1)}, u32[]{:S(2)}, u32[]{:S(2)}) collective-permute-start(bf16[48,1536]{1,0:T(8,128)(2,1)S(1)} %convert_add_fusion.1), channel_id=1, source_target_pairs={{0,64},{32,96},{64,128},{96,160},{128,192},{160,224},{192,256},{22... | collective-permute-start | bytes 442376 | tf_op jit(solution)/shard_map/ppermute | solution.py:136
Sparse Core Ops, SparseCore 0:
  77.0 43.1 reduce-scatter.1

commit v8 on v7

--- a/solution.py
+++ b/solution.py
@@ -116,13 +116,14 @@
     dpre = (cot.astype(F32) * gelu_slope(pre)).astype(BF)
 
     own_pair = swap(dpre, "mx", n_mx, 1)
+    own_pair, left[1] = lax.optimization_barrier((own_pair, left[1]))
+    left[1] = swap(left[1], "dp", n_dp, GROUP[0])
     right = [dpre, own_pair]
     arrived = [swap(dpre, "dp", n_dp, bits) for bits in GROUP]
 
     in_order = jnp.where(core == 0, jnp.concatenate(right, axis=0), jnp.concatenate(right[::-1], axis=0))
     back = dot(in_order, in_weight, ((1,), (1,)))
-    back, left[1] = lax.optimization_barrier((back, left[1]))
-    left[1] = swap(left[1], "dp", n_dp, GROUP[0])
+    back, arrived[2] = lax.optimization_barrier((back, arrived[2]))
     left[1], arrived[1] = lax.optimization_barrier((left[1], arrived[1]))
     dnormed = lax.psum_scatter(back, "my", scatter_dimension=0, tiled=True)
     own_rows = tok_rows // n_my

time: 155 us -> 155 us (level)
  no operation moved by 1% of the time
where the time goes in v8:
time: 155 us; the launch traced here: 153 us
  starting transfers between devices  63.7 us (41%)
  blocking collectives  32.9 us (21%)
  waiting for transfers between devices  16.1 us (10%)
  between operations  14.5 us (9%)
  matrix products  11.1 us (7%)
  other arithmetic  9.53 us (6%)
  Pallas kernels  2.86 us (2%)
  local copies, waits for them, and re-layouts  2.65 us (2%)
    ppermute x12, starting transfers between devices, swap(): return lax.ppermute(value, axis, [(i, i ^ bits) for i in range(size)])  32.3 us
    ppermute x7, starting transfers between devices, hop(): return lax.ppermute(value.astype(BF), 'dp', perm).astype(F32)  31.4 us
    psum x1, blocking collectives, body(): lax.psum((jnp.sum(values, axis=1), jnp.sum(values * values, axis=1)), 'mx')  20.7 us
    psum x1, blocking collectives, body(): lax.psum((jnp.sum(dcentred, axis=1), jnp.sum(dcentred * centred_rows, axi...  12.2 us
    ppermute x12, waiting for transfers between devices, swap(): return lax.ppermute(value, axis, [(i, i ^ bits) for i in range(size)])  11.8 us
    dot_general x3, matrix products, dot(): return lax.dot_general(a, b, (dims, ((), ())), preferred_element_type=F32)  11.1 us
    ppermute x7, waiting for transfers between devices, hop(): return lax.ppermute(value.astype(BF), 'dp', perm).astype(F32)  4.31 us
  transfers between devices with their start and end apart: 20, of which 9 were waited for; matrix products, arithmetic and copies ran while one was open for 8% of the time, Pallas kernels for 2%

profile of v8, /device:TPU:1, one launch (start us, length us, event | category | flops | bytes accessed | tf_op | source)
XLA Modules:
  0.0 153.4 jit_solution(6542977879159229864)
XLA Ops:
  7.2 0.0 reduce-scatter.2.cloned.1.call-start
  7.2 1.5 convert_reduce_fusion
  8.7 20.7 %all-reduce.1 = (f32[256]{0:T(256)S(1)}, f32[256]{0:T(256)S(1)}) all-reduce(f32[256]{0:T(256)S(1)} %get-tuple-element.45, f32[256]{0:T(256)S(1)} %get-tuple-element.44), channel_id=1, replica_groups=mesh['dp'=32,'mx'=4,'my'=8] {'mx'}, use_global_device_ids=true, to_apply=%region_3.4 | all-reduce | flops 512 | bytes 4096 | tf_op jit(solution)/shard_map/psum | solution.py:86
  29.4 2.6 %fusion = (f32[256,1536]{1,0:T(8,128)}, bf16[256,1536]{1,0:T(8,128)(2,1)S(1)}) fusion(bf16[256,1536]{1,0:T(8,128)(2,1)} %param.4, f32[256]{0:T(256)S(1)} %get-tuple-element.61, f32[256]{0:T(256)S(1)} %get-tuple-element.60, f32[1536]{0:T(1024)} %param.5), kind=kLoop, calls=%fused_computation.12 | loop fusion | flops 1966080 | bytes 3153920 | tf_op jit(solution)/shard_map/mul | solution.py:89
  32.0 3.1 %convolution_convert_fusion = bf16[128,1536]{1,0:T(8,128)(2,1)S(1)} fusion(bf16[1536,1536]{1,0:T(8,128)(2,1)} %param.6, bf16[256,1536]{1,0:T(8,128)(2,1)S(1)} %get-tuple-element.53, s32[]{:T(128)S(6)} %select_n.65), kind=kOutput, calls=%fused_computation | convolution fusion | flops 604176384 | bytes 5505028 | tf_op jit(solution)/shard_map/dot_general | solution.py:29
  35.2 2.7 %collective-permute-start = (bf16[128,1536]{1,0:T(8,128)(2,1)S(1)}, bf16[128,1536]{1,0:T(8,128)(2,1)S(1)}, u32[]{:S(2)}, u32[]{:S(2)}) collective-permute-start(bf16[128,1536]{1,0:T(8,128)(2,1)S(1)} %convolution_convert_fusion), channel_id=1, source_target_pairs={{0,8},{8,0},{16,24},{24,16},{1,9},{9,1},{17,25},{25,17},{2,10},{10... | collective-permute-start | bytes 1179656 | tf_op jit(solution)/shard_map/ppermute | solution.py:21
  37.8 3.1 %fusion.17 = f32[128,1536]{1,0:T(8,128)S(1)} fusion(bf16[1536,1536]{1,0:T(8,128)(2,1)} %param.6, bf16[256,1536]{1,0:T(8,128)(2,1)S(1)} %get-tuple-element.53, s32[]{:T(128)S(6)} %select_n.64), kind=kOutput, calls=%fused_computation.36 | convolution fusion | flops 603979776 | bytes 5898244 | tf_op jit(solution)/shard_map/dot_general | solution.py:29
  41.0 0.1 dynamic-slice_bitcast_fusion.1
  41.0 0.0 collective-permute-done
  41.0 0.1 fusion.15
  41.1 1.9 %collective-permute-start.1 = (bf16[128,1536]{1,0:T(8,128)(2,1)S(1)}, bf16[128,1536]{1,0:T(8,128)(2,1)S(1)}, u32[]{:S(2)}, u32[]{:S(2)}) collective-permute-start(bf16[128,1536]{1,0:T(8,128)(2,1)S(1)} %fusion.15), channel_id=1, source_target_pairs={{0,16},{8,24},{16,0},{24,8},{1,17},{9,25},{17,1},{25,9},{2,18},{10... | collective-permute-start | bytes 1179656 | tf_op jit(solution)/shard_map/ppermute | solution.py:21
  43.0 0.1 pad_maximum_fusion
  43.2 0.3 copy.8
  43.5 0.0 copy-start.3
  43.5 1.0 fusion.19
  44.5 1.9 %collective-permute-start.3 = (bf16[384,256]{1,0:T(8,128)(2,1)S(1)}, bf16[384,256]{1,0:T(8,128)(2,1)S(1)}, u32[]{:S(2)}, u32[]{:S(2)}) collective-permute-start(bf16[384,256]{1,0:T(8,128)(2,1)S(1)} %bitcast.18), channel_id=1, source_target_pairs={{0,544},{32,512},{64,608},{96,576},{128,672},{160,640},{192,736},{... | collective-permute-start | bytes 589832 | tf_op jit(solution)/shard_map/ppermute | solution.py:21
  46.4 1.9 %collective-permute-start.2 = (bf16[384,256]{1,0:T(8,128)(2,1)S(1)}, bf16[384,256]{1,0:T(8,128)(2,1)S(1)}, u32[]{:S(2)}, u32[]{:S(2)}) collective-permute-start(bf16[384,256]{1,0:T(8,128)(2,1)S(1)} %bitcast.17), channel_id=1, source_target_pairs={{0,32},{32,0},{64,96},{96,64},{128,160},{160,128},{192,224},{224,1... | collective-permute-start | bytes 589832 | tf_op jit(solution)/shard_map/ppermute | solution.py:21
  48.3 5.3 %collective-permute-done.3.refs_3_ = bf16[384,256]{1,0:T(8,128)(2,1)S(1)} collective-permute-done((bf16[384,256]{1,0:T(8,128)(2,1)S(1)}, bf16[384,256]{1,0:T(8,128)(2,1)S(1)}, u32[]{:S(2)}, u32[]{:S(2)}) %collective-permute-start.3) | collective-permute-done | bytes 196640 | tf_op jit(solution)/shard_map/ppermute | solution.py:21
  53.6 1.4 collective-permute-done.2.refs_2_
  55.0 0.3 collective-permute-done.1
  55.3 0.5 fusion.7.refs_4_
  55.7 2.7 %collective-permute-start.4 = (bf16[128,1536]{1,0:T(8,128)(2,1)S(1)}, bf16[128,1536]{1,0:T(8,128)(2,1)S(1)}, u32[]{:S(2)}, u32[]{:S(2)}) collective-permute-start(bf16[128,1536]{1,0:T(8,128)(2,1)S(1)} %fusion.7.refs_4_), channel_id=1, source_target_pairs={{0,8},{8,0},{16,24},{24,16},{1,9},{9,1},{17,25},{25,17},{2,10},{10... | collective-permute-start | bytes 1179656 | tf_op jit(solution)/shard_map/ppermute | solution.py:21
  58.4 3.9 %collective-permute-start.10 = (bf16[128,1536]{1,0:T(8,128)(2,1)S(1)}, bf16[128,1536]{1,0:T(8,128)(2,1)S(1)}, u32[]{:S(2)}, u32[]{:S(2)}) collective-permute-start(bf16[128,1536]{1,0:T(8,128)(2,1)S(1)} %fusion.7.refs_4_), channel_id=1, source_target_pairs={{0,544},{32,512},{64,608},{96,576},{128,672},{160,640},{192,736},{... | collective-permute-start | bytes 1179656 | tf_op jit(solution)/shard_map/ppermute | solution.py:21
  62.4 2.9 %collective-permute-start.7 = (bf16[128,1536]{1,0:T(8,128)(2,1)S(1)}, bf16[128,1536]{1,0:T(8,128)(2,1)S(1)}, u32[]{:S(2)}, u32[]{:S(2)}) collective-permute-start(bf16[128,1536]{1,0:T(8,128)(2,1)S(1)} %fusion.7.refs_4_), channel_id=1, source_target_pairs={{0,512},{32,544},{64,576},{96,608},{128,640},{160,672},{192,704},{... | collective-permute-start | bytes 1179656 | tf_op jit(solution)/shard_map/ppermute | solution.py:21
  65.3 3.1 %collective-permute-start.6 = (bf16[128,1536]{1,0:T(8,128)(2,1)S(1)}, bf16[128,1536]{1,0:T(8,128)(2,1)S(1)}, u32[]{:S(2)}, u32[]{:S(2)}) collective-permute-start(bf16[128,1536]{1,0:T(8,128)(2,1)S(1)} %fusion.7.refs_4_), channel_id=1, source_target_pairs={{0,32},{32,0},{64,96},{96,64},{128,160},{160,128},{192,224},{224,1... | collective-permute-start | bytes 1179656 | tf_op jit(solution)/shard_map/ppermute | solution.py:21
  68.4 0.0 collective-permute-done.4.refs_5_
  68.4 3.4 %collective-permute-start.5 = (bf16[384,256]{1,0:T(8,128)(2,1)S(1)}, bf16[384,256]{1,0:T(8,128)(2,1)S(1)}, u32[]{:S(2)}, u32[]{:S(2)}) collective-permute-start(bf16[384,256]{1,0:T(8,128)(2,1)S(1)} %bitcast.16), channel_id=1, source_target_pairs={{0,512},{32,544},{64,576},{96,608},{128,640},{160,672},{192,704},{... | collective-permute-start | bytes 589832 | tf_op jit(solution)/shard_map/ppermute | solution.py:21
  71.8 4.9 %fusion.8 = f32[256,1536]{1,0:T(8,128)} fusion(bf16[1536,1536]{1,0:T(8,128)(2,1)} %param.6, bf16[128,1536]{1,0:T(8,128)(2,1)S(1)} %collective-permute-done.4.refs_5_, bf16[128,1536]{1,0:T(8,128)(2,1)S(1)} %fusion.7.refs_4_, pred[]{:T(512)S(6)} %eq.7), kind=kOutput, calls=%fused_computation.24 | convolution fusion | flops 1211498496 | bytes 7077889 | tf_op jit(solution)/shard_map/dot_general | solution.py:29
  76.7 0.0 collective-permute-done.10.refs_10_
  76.7 0.0 reduce-scatter.2.cloned.1.call-update
  76.7 3.0 %collective-permute-start.11 = (bf16[128,1536]{1,0:T(8,128)(2,1)S(1)}, bf16[128,1536]{1,0:T(8,128)(2,1)S(1)}, u32[]{:S(2)}, u32[]{:S(2)}) collective-permute-start(bf16[128,1536]{1,0:T(8,128)(2,1)S(1)} %collective-permute-done.10.refs_10_), channel_id=1, source_target_pairs={{0,8},{8,0},{16,24},{24,16},{1,9},{9,1},{17,25},{25,17},{2,10},{10... | collective-permute-start | bytes 1179656 | tf_op jit(solution)/shard_map/ppermute | solution.py:21
  79.8 1.8 %collective-permute-done.7.refs_6_ = bf16[128,1536]{1,0:T(8,128)(2,1)S(1)} collective-permute-done((bf16[128,1536]{1,0:T(8,128)(2,1)S(1)}, bf16[128,1536]{1,0:T(8,128)(2,1)S(1)}, u32[]{:S(2)}, u32[]{:S(2)}) %collective-permute-start.7) | collective-permute-done | bytes 393248 | tf_op jit(solution)/shard_map/ppermute | solution.py:21
  81.6 2.4 %collective-permute-start.8 = (bf16[128,1536]{1,0:T(8,128)(2,1)S(1)}, bf16[128,1536]{1,0:T(8,128)(2,1)S(1)}, u32[]{:S(2)}, u32[]{:S(2)}) collective-permute-start(bf16[128,1536]{1,0:T(8,128)(2,1)S(1)} %collective-permute-done.7.refs_6_), channel_id=1, source_target_pairs={{0,8},{8,0},{16,24},{24,16},{1,9},{9,1},{17,25},{25,17},{2,10},{10... | collective-permute-start | bytes 1179656 | tf_op jit(solution)/shard_map/ppermute | solution.py:21
  84.0 0.0 collective-permute-done.6.refs_8_
  84.0 1.8 %collective-permute-done.5.refs_1_ = bf16[384,256]{1,0:T(8,128)(2,1)S(1)} collective-permute-done((bf16[384,256]{1,0:T(8,128)(2,1)S(1)}, bf16[384,256]{1,0:T(8,128)(2,1)S(1)}, u32[]{:S(2)}, u32[]{:S(2)}) %collective-permute-start.5) | collective-permute-done | bytes 196640 | tf_op jit(solution)/shard_map/ppermute | solution.py:21
  85.8 0.7 copy-done
  86.4 2.4 %collective-permute-start.9 = (bf16[128,1536]{1,0:T(8,128)(2,1)S(1)}, bf16[128,1536]{1,0:T(8,128)(2,1)S(1)}, u32[]{:S(2)}, u32[]{:S(2)}) collective-permute-start(bf16[128,1536]{1,0:T(8,128)(2,1)S(1)} %collective-permute-done.6.refs_8_), channel_id=1, source_target_pairs={{0,8},{8,0},{16,24},{24,16},{1,9},{9,1},{17,25},{25,17},{2,10},{10... | collective-permute-start | bytes 1179656 | tf_op jit(solution)/shard_map/ppermute | solution.py:21
  88.8 0.0 collective-permute-done.8.refs_7_
  88.8 0.0 collective-permute-done.11.refs_11_
  88.8 1.3 collective-permute-done.9.refs_9_
  90.1 0.9 copy-done.1
  91.1 2.9 %shard_map.59 = (bf16[48,1536]{1,0:T(8,128)(2,1)S(1)}, bf16[48,1536]{1,0:T(8,128)(2,1)S(1)}, bf16[48,1536]{1,0:T(8,128)(2,1)S(1)}, bf16[48,1536]{1,0:T(8,128)(2,...) custom-call(bf16[384,256]{1,0:T(8,128)(2,1)S(1)} %bitcast.14, ...), custom_call_target="tpu_custom_call" | custom-call | flops 1207959552 | bytes 5111808 | tf_op jit(solution)/shard_map/pallas_call | solution.py:55
  93.9 0.6 copy-done.2
  94.6 2.0 %collective-permute-start.15 = (bf16[48,1536]{1,0:T(8,128)(2,1)}, bf16[48,1536]{1,0:T(8,128)(2,1)S(1)}, u32[]{:S(2)}, u32[]{:S(2)}) collective-permute-start(bf16[48,1536]{1,0:T(8,128)(2,1)} %get-tuple-element.37), channel_id=1, source_target_pairs={{0,64},{32,96},{64,128},{96,160},{128,192},{160,224},{192,256},{22... | collective-permute-start | bytes 442376 | tf_op jit(solution)/shard_map/ppermute | solution.py:137
  96.6 0.1 dynamic_slice.34
  96.7 11.3 %collective-permute-start.12 = (bf16[48,1536]{1,0:T(8,128)(2,1)}, bf16[48,1536]{1,0:T(8,128)(2,1)S(1)}, u32[]{:S(2)}, u32[]{:S(2)}) collective-permute-start(bf16[48,1536]{1,0:T(8,128)(2,1)} %copy-done.2), channel_id=1, source_target_pairs={{0,448},{32,480},{64,0},{96,32},{128,64},{160,96},{192,128},{224,1... | collective-permute-start | bytes 442376 | tf_op jit(solution)/shard_map/ppermute | solution.py:137
  108.0 2.2 %collective-permute-done.15 = bf16[48,1536]{1,0:T(8,128)(2,1)S(1)} collective-permute-done((bf16[48,1536]{1,0:T(8,128)(2,1)}, bf16[48,1536]{1,0:T(8,128)(2,1)S(1)}, u32[]{:S(2)}, u32[]{:S(2)}) %collective-permute-start.15) | collective-permute-done | bytes 147488 | tf_op jit(solution)/shard_map/ppermute | solution.py:137
  110.3 1.9 %collective-permute-start.16 = (bf16[48,1536]{1,0:T(8,128)(2,1)S(1)}, bf16[48,1536]{1,0:T(8,128)(2,1)S(1)}, u32[]{:S(2)}, u32[]{:S(2)}) collective-permute-start(bf16[48,1536]{1,0:T(8,128)(2,1)S(1)} %add_convert_fusion.2), channel_id=1, source_target_pairs={{0,64},{32,96},{64,128},{96,160},{128,192},{160,224},{192,256},{22... | collective-permute-start | bytes 442376 | tf_op jit(solution)/shard_map/ppermute | solution.py:137
  112.2 2.0 %collective-permute-done.12 = bf16[48,1536]{1,0:T(8,128)(2,1)S(1)} collective-permute-done((bf16[48,1536]{1,0:T(8,128)(2,1)}, bf16[48,1536]{1,0:T(8,128)(2,1)S(1)}, u32[]{:S(2)}, u32[]{:S(2)}) %collective-permute-start.12) | collective-permute-done | bytes 147488 | tf_op jit(solution)/shard_map/ppermute | solution.py:137
  114.2 6.3 %collective-permute-start.13 = (bf16[48,1536]{1,0:T(8,128)(2,1)S(1)}, bf16[48,1536]{1,0:T(8,128)(2,1)S(1)}, u32[]{:S(2)}, u32[]{:S(2)}) collective-permute-start(bf16[48,1536]{1,0:T(8,128)(2,1)S(1)} %add_convert_fusion.4), channel_id=1, source_target_pairs={{0,448},{32,480},{64,0},{96,32},{128,64},{160,96},{192,128},{224,1... | collective-permute-start | bytes 442376 | tf_op jit(solution)/shard_map/ppermute | solution.py:137
  120.5 0.0 collective-permute-done.16
  120.5 1.9 %collective-permute-start.17 = (bf16[48,1536]{1,0:T(8,128)(2,1)S(1)}, bf16[48,1536]{1,0:T(8,128)(2,1)S(1)}, u32[]{:S(2)}, u32[]{:S(2)}) collective-permute-start(bf16[48,1536]{1,0:T(8,128)(2,1)S(1)} %add_convert_fusion.1), channel_id=1, source_target_pairs={{0,64},{32,96},{64,128},{96,160},{128,192},{160,224},{192,256},{22... | collective-permute-start | bytes 442376 | tf_op jit(solution)/shard_map/ppermute | solution.py:137
  122.5 0.1 collective-permute-done.13
  122.6 6.0 %collective-permute-start.14 = (bf16[48,1536]{1,0:T(8,128)(2,1)S(1)}, bf16[48,1536]{1,0:T(8,128)(2,1)S(1)}, u32[]{:S(2)}, u32[]{:S(2)}) collective-permute-start(bf16[48,1536]{1,0:T(8,128)(2,1)S(1)} %add_convert_fusion.3), channel_id=1, source_target_pairs={{0,448},{32,480},{64,0},{96,32},{128,64},{160,96},{192,128},{224,1... | collective-permute-start | bytes 442376 | tf_op jit(solution)/shard_map/ppermute | solution.py:137
  128.6 0.0 collective-permute-done.17
  128.7 0.0 reduce-scatter.2.cloned.1.call-done
  128.7 1.9 %collective-permute-start.18 = (bf16[48,1536]{1,0:T(8,128)(2,1)S(1)}, bf16[48,1536]{1,0:T(8,128)(2,1)S(1)}, u32[]{:S(2)}, u32[]{:S(2)}) collective-permute-start(bf16[48,1536]{1,0:T(8,128)(2,1)S(1)} %convert_add_fusion.1), channel_id=1, source_target_pairs={{0,64},{32,96},{64,128},{96,160},{128,192},{160,224},{192,256},{22... | collective-permute-start | bytes 442376 | tf_op jit(solution)/shard_map/ppermute | solution.py:137
  130.6 0.0 copy-done.5
  130.6 1.2 multiply_reduce_fusion.1
  131.8 12.2 %all-reduce = (f32[32]{0:T(128)S(1)}, f32[32]{0:T(128)S(1)}) all-reduce(f32[32]{0:T(128)S(1)} %get-tuple-element.47, f32[32]{0:T(128)S(1)} %get-tuple-element.46), channel_id=1, replica_groups=mesh['dp'=32,'mx'=4,'my'=8] {'mx'}, use_global_device_ids=true, to_apply=%region_8.9 | all-reduce | flops 64 | bytes 512 | tf_op jit(solution)/shard_map/psum | solution.py:150
  144.1 1.8 %multiply_convert_fusion.1 = bf16[32,1536]{1,0:T(8,128)(2,1)} fusion(f32[256,1536]{1,0:T(8,128)} %get-tuple-element.52, s32[]{:T(128)S(6)} %select_n.77, f32[32,1536]{1,0:T(8,128)} %reduce-scatter.2.cloned.1.call-done, f32[32]{0:T(128)S(1)} %get-tuple-element.62, f32[32]{0:T(128)S(1)} %get-tuple-element.63, f32[1536]{0:T(1024)S(1)} %copy-done.5, ...), kind=kLoop, calls=%fused_computation.48 | loop fusion | flops 294912 | bytes 498052 | tf_op jit(solution)/shard_map/convert_element_type | solution.py:156
  145.8 0.0 collective-permute-done.14
  145.8 0.0 collective-permute-done.18
  145.8 0.7 fusion.23
  (14 shorter events, 0.2 us)
Async XLA Ops:
  7.2 121.5 %reduce-scatter.2.cloned.1.call-start = ((), (), s32[]{:S(2)}) async-start(), calls=%async_computation.1 | async-start | bytes 1769472 | tf_op jit(solution)/shard_map/reduce_scatter | solution.py:128
  35.2 5.9 %collective-permute-start = (bf16[128,1536]{1,0:T(8,128)(2,1)S(1)}, bf16[128,1536]{1,0:T(8,128)(2,1)S(1)}, u32[]{:S(2)}, u32[]{:S(2)}) collective-permute-start(bf16[128,1536]{1,0:T(8,128)(2,1)S(1)} %convolution_convert_fusion), channel_id=1, source_target_pairs={{0,8},{8,0},{16,24},{24,16},{1,9},{9,1},{17,25},{25,17},{2,10},{10... | collective-permute-start | bytes 1179656 | tf_op jit(solution)/shard_map/ppermute | solution.py:21
  41.1 14.1 %collective-permute-start.1 = (bf16[128,1536]{1,0:T(8,128)(2,1)S(1)}, bf16[128,1536]{1,0:T(8,128)(2,1)S(1)}, u32[]{:S(2)}, u32[]{:S(2)}) collective-permute-start(bf16[128,1536]{1,0:T(8,128)(2,1)S(1)} %fusion.15), channel_id=1, source_target_pairs={{0,16},{8,24},{16,0},{24,8},{1,17},{9,25},{17,1},{25,9},{2,18},{10... | collective-permute-start | bytes 1179656 | tf_op jit(solution)/shard_map/ppermute | solution.py:21
  43.5 11.8 %copy-start.3 = (bf16[256,1536]{1,0:T(8,128)(2,1)S(1)}, bf16[256,1536]{1,0:T(8,128)(2,1)}, u32[]{:S(2)}) copy-start(bf16[256,1536]{1,0:T(8,128)(2,1)} %param.7) | copy-start | bytes 2359300
  44.5 9.1 %collective-permute-start.3 = (bf16[384,256]{1,0:T(8,128)(2,1)S(1)}, bf16[384,256]{1,0:T(8,128)(2,1)S(1)}, u32[]{:S(2)}, u32[]{:S(2)}) collective-permute-start(bf16[384,256]{1,0:T(8,128)(2,1)S(1)} %bitcast.18), channel_id=1, source_target_pairs={{0,544},{32,512},{64,608},{96,576},{128,672},{160,640},{192,736},{... | collective-permute-start | bytes 589832 | tf_op jit(solution)/shard_map/ppermute | solution.py:21
  46.4 8.6 %collective-permute-start.2 = (bf16[384,256]{1,0:T(8,128)(2,1)S(1)}, bf16[384,256]{1,0:T(8,128)(2,1)S(1)}, u32[]{:S(2)}, u32[]{:S(2)}) collective-permute-start(bf16[384,256]{1,0:T(8,128)(2,1)S(1)} %bitcast.17), channel_id=1, source_target_pairs={{0,32},{32,0},{64,96},{96,64},{128,160},{160,128},{192,224},{224,1... | collective-permute-start | bytes 589832 | tf_op jit(solution)/shard_map/ppermute | solution.py:21
  55.2 13.2 %copy-start.4 = (bf16[1,8,1,48,256]{4,3,2,1,0:T(8,128)(2,1)S(1)}, bf16[1,8,1,48,256]{4,3,2,1,0:T(8,128)(2,1)}, u32[]{:S(2)}) copy-start(bf16[1,8,1,48,256]{4,3,2,1,0:T(8,128)(2,1)} %get-tuple-element.57) | copy-start | bytes 589828
  55.7 12.7 %collective-permute-start.4 = (bf16[128,1536]{1,0:T(8,128)(2,1)S(1)}, bf16[128,1536]{1,0:T(8,128)(2,1)S(1)}, u32[]{:S(2)}, u32[]{:S(2)}) collective-permute-start(bf16[128,1536]{1,0:T(8,128)(2,1)S(1)} %fusion.7.refs_4_), channel_id=1, source_target_pairs={{0,8},{8,0},{16,24},{24,16},{1,9},{9,1},{17,25},{25,17},{2,10},{10... | collective-permute-start | bytes 1179656 | tf_op jit(solution)/shard_map/ppermute | solution.py:21
  58.4 18.3 %collective-permute-start.10 = (bf16[128,1536]{1,0:T(8,128)(2,1)S(1)}, bf16[128,1536]{1,0:T(8,128)(2,1)S(1)}, u32[]{:S(2)}, u32[]{:S(2)}) collective-permute-start(bf16[128,1536]{1,0:T(8,128)(2,1)S(1)} %fusion.7.refs_4_), channel_id=1, source_target_pairs={{0,544},{32,512},{64,608},{96,576},{128,672},{160,640},{192,736},{... | collective-permute-start | bytes 1179656 | tf_op jit(solution)/shard_map/ppermute | solution.py:21
  62.4 19.2 %collective-permute-start.7 = (bf16[128,1536]{1,0:T(8,128)(2,1)S(1)}, bf16[128,1536]{1,0:T(8,128)(2,1)S(1)}, u32[]{:S(2)}, u32[]{:S(2)}) collective-permute-start(bf16[128,1536]{1,0:T(8,128)(2,1)S(1)} %fusion.7.refs_4_), channel_id=1, source_target_pairs={{0,512},{32,544},{64,576},{96,608},{128,640},{160,672},{192,704},{... | collective-permute-start | bytes 1179656 | tf_op jit(solution)/shard_map/ppermute | solution.py:21
  65.3 18.7 %collective-permute-start.6 = (bf16[128,1536]{1,0:T(8,128)(2,1)S(1)}, bf16[128,1536]{1,0:T(8,128)(2,1)S(1)}, u32[]{:S(2)}, u32[]{:S(2)}) collective-permute-start(bf16[128,1536]{1,0:T(8,128)(2,1)S(1)} %fusion.7.refs_4_), channel_id=1, source_target_pairs={{0,32},{32,0},{64,96},{96,64},{128,160},{160,128},{192,224},{224,1... | collective-permute-start | bytes 1179656 | tf_op jit(solution)/shard_map/ppermute | solution.py:21
  68.4 17.3 %collective-permute-start.5 = (bf16[384,256]{1,0:T(8,128)(2,1)S(1)}, bf16[384,256]{1,0:T(8,128)(2,1)S(1)}, u32[]{:S(2)}, u32[]{:S(2)}) collective-permute-start(bf16[384,256]{1,0:T(8,128)(2,1)S(1)} %bitcast.16), channel_id=1, source_target_pairs={{0,512},{32,544},{64,576},{96,608},{128,640},{160,672},{192,704},{... | collective-permute-start | bytes 589832 | tf_op jit(solution)/shard_map/ppermute | solution.py:21
  76.7 12.1 %collective-permute-start.11 = (bf16[128,1536]{1,0:T(8,128)(2,1)S(1)}, bf16[128,1536]{1,0:T(8,128)(2,1)S(1)}, u32[]{:S(2)}, u32[]{:S(2)}) collective-permute-start(bf16[128,1536]{1,0:T(8,128)(2,1)S(1)} %collective-permute-done.10.refs_10_), channel_id=1, source_target_pairs={{0,8},{8,0},{16,24},{24,16},{1,9},{9,1},{17,25},{25,17},{2,10},{10... | collective-permute-start | bytes 1179656 | tf_op jit(solution)/shard_map/ppermute | solution.py:21
  81.6 7.3 %collective-permute-start.8 = (bf16[128,1536]{1,0:T(8,128)(2,1)S(1)}, bf16[128,1536]{1,0:T(8,128)(2,1)S(1)}, u32[]{:S(2)}, u32[]{:S(2)}) collective-permute-start(bf16[128,1536]{1,0:T(8,128)(2,1)S(1)} %collective-permute-done.7.refs_6_), channel_id=1, source_target_pairs={{0,8},{8,0},{16,24},{24,16},{1,9},{9,1},{17,25},{25,17},{2,10},{10... | collective-permute-start | bytes 1179656 | tf_op jit(solution)/shard_map/ppermute | solution.py:21
  85.8 0.7 copy-start
  86.4 3.7 %collective-permute-start.9 = (bf16[128,1536]{1,0:T(8,128)(2,1)S(1)}, bf16[128,1536]{1,0:T(8,128)(2,1)S(1)}, u32[]{:S(2)}, u32[]{:S(2)}) collective-permute-start(bf16[128,1536]{1,0:T(8,128)(2,1)S(1)} %collective-permute-done.6.refs_8_), channel_id=1, source_target_pairs={{0,8},{8,0},{16,24},{24,16},{1,9},{9,1},{17,25},{25,17},{2,10},{10... | collective-permute-start | bytes 1179656 | tf_op jit(solution)/shard_map/ppermute | solution.py:21
  90.1 0.9 copy-start.1
  93.9 0.6 copy-start.2
  94.6 36.1 %copy-start.5 = (f32[1536]{0:T(1024)S(1)}, f32[1536]{0:T(1024)}, u32[]{:S(2)}) copy-start(f32[1536]{0:T(1024)} %param.5) | copy-start | bytes 18436
  94.6 15.7 %collective-permute-start.15 = (bf16[48,1536]{1,0:T(8,128)(2,1)}, bf16[48,1536]{1,0:T(8,128)(2,1)S(1)}, u32[]{:S(2)}, u32[]{:S(2)}) collective-permute-start(bf16[48,1536]{1,0:T(8,128)(2,1)} %get-tuple-element.37), channel_id=1, source_target_pairs={{0,64},{32,96},{64,128},{96,160},{128,192},{160,224},{192,256},{22... | collective-permute-start | bytes 442376 | tf_op jit(solution)/shard_map/ppermute | solution.py:137
  96.7 17.5 %collective-permute-start.12 = (bf16[48,1536]{1,0:T(8,128)(2,1)}, bf16[48,1536]{1,0:T(8,128)(2,1)S(1)}, u32[]{:S(2)}, u32[]{:S(2)}) collective-permute-start(bf16[48,1536]{1,0:T(8,128)(2,1)} %copy-done.2), channel_id=1, source_target_pairs={{0,448},{32,480},{64,0},{96,32},{128,64},{160,96},{192,128},{224,1... | collective-permute-start | bytes 442376 | tf_op jit(solution)/shard_map/ppermute | solution.py:137
  110.3 10.2 %collective-permute-start.16 = (bf16[48,1536]{1,0:T(8,128)(2,1)S(1)}, bf16[48,1536]{1,0:T(8,128)(2,1)S(1)}, u32[]{:S(2)}, u32[]{:S(2)}) collective-permute-start(bf16[48,1536]{1,0:T(8,128)(2,1)S(1)} %add_convert_fusion.2), channel_id=1, source_target_pairs={{0,64},{32,96},{64,128},{96,160},{128,192},{160,224},{192,256},{22... | collective-permute-start | bytes 442376 | tf_op jit(solution)/shard_map/ppermute | solution.py:137
  114.2 8.3 %collective-permute-start.13 = (bf16[48,1536]{1,0:T(8,128)(2,1)S(1)}, bf16[48,1536]{1,0:T(8,128)(2,1)S(1)}, u32[]{:S(2)}, u32[]{:S(2)}) collective-permute-start(bf16[48,1536]{1,0:T(8,128)(2,1)S(1)} %add_convert_fusion.4), channel_id=1, source_target_pairs={{0,448},{32,480},{64,0},{96,32},{128,64},{160,96},{192,128},{224,1... | collective-permute-start | bytes 442376 | tf_op jit(solution)/shard_map/ppermute | solution.py:137
  120.5 8.1 %collective-permute-start.17 = (bf16[48,1536]{1,0:T(8,128)(2,1)S(1)}, bf16[48,1536]{1,0:T(8,128)(2,1)S(1)}, u32[]{:S(2)}, u32[]{:S(2)}) collective-permute-start(bf16[48,1536]{1,0:T(8,128)(2,1)S(1)} %add_convert_fusion.1), channel_id=1, source_target_pairs={{0,64},{32,96},{64,128},{96,160},{128,192},{160,224},{192,256},{22... | collective-permute-start | bytes 442376 | tf_op jit(solution)/shard_map/ppermute | solution.py:137
  122.6 23.2 %collective-permute-start.14 = (bf16[48,1536]{1,0:T(8,128)(2,1)S(1)}, bf16[48,1536]{1,0:T(8,128)(2,1)S(1)}, u32[]{:S(2)}, u32[]{:S(2)}) collective-permute-start(bf16[48,1536]{1,0:T(8,128)(2,1)S(1)} %add_convert_fusion.3), channel_id=1, source_target_pairs={{0,448},{32,480},{64,0},{96,32},{128,64},{160,96},{192,128},{224,1... | collective-permute-start | bytes 442376 | tf_op jit(solution)/shard_map/ppermute | solution.py:137
  128.7 17.1 %collective-permute-start.18 = (bf16[48,1536]{1,0:T(8,128)(2,1)S(1)}, bf16[48,1536]{1,0:T(8,128)(2,1)S(1)}, u32[]{:S(2)}, u32[]{:S(2)}) collective-permute-start(bf16[48,1536]{1,0:T(8,128)(2,1)S(1)} %convert_add_fusion.1), channel_id=1, source_target_pairs={{0,64},{32,96},{64,128},{96,160},{128,192},{160,224},{192,256},{22... | collective-permute-start | bytes 442376 | tf_op jit(solution)/shard_map/ppermute | solution.py:137
Sparse Core Ops, SparseCore 0:
  76.9 43.2 reduce-scatter.1

commit v9 on v8

--- a/solution.py
+++ b/solution.py
@@ -119,7 +119,8 @@
     own_pair, left[1] = lax.optimization_barrier((own_pair, left[1]))
     left[1] = swap(left[1], "dp", n_dp, GROUP[0])
     right = [dpre, own_pair]
-    arrived = [swap(dpre, "dp", n_dp, bits) for bits in GROUP]
+    later, own_pair = lax.optimization_barrier((dpre, own_pair))
+    arrived = [swap(dpre if bits == 1 else later, "dp", n_dp, bits) for bits in GROUP]
 
     in_order = jnp.where(core == 0, jnp.concatenate(right, axis=0), jnp.concatenate(right[::-1], axis=0))
     back = dot(in_order, in_weight, ((1,), (1,)))

time: 155 us -> 163 us (1.052)
  waiting for transfers between devices: 16.1 us -> 27 us
  starting transfers between devices: 63.7 us -> 61.6 us
    ppermute x12, waiting for transfers between devices: 11.8 us -> 22.6 us  [swap(): return lax.ppermute(value, axis, [(i, i ^ bits) for i in range(size)])]
    ppermute x7, starting transfers between devices: 31.4 us -> 29.5 us  [hop(): return lax.ppermute(value.astype(BF), 'dp', perm).astype(F32)]
where the time goes in v9:
time: 163 us; the launch traced here: 162 us
  starting transfers between devices  61.6 us (38%)
  blocking collectives  32.9 us (20%)
  waiting for transfers between devices  27 us (17%)
  between operations  14.5 us (9%)
  matrix products  11.1 us (7%)
  other arithmetic  9.53 us (6%)
  Pallas kernels  2.86 us (2%)
  local copies, waits for them, and re-layouts  2.66 us (2%)
    ppermute x12, starting transfers between devices, swap(): return lax.ppermute(value, axis, [(i, i ^ bits) for i in range(size)])  32.1 us
    ppermute x7, starting transfers between devices, hop(): return lax.ppermute(value.astype(BF), 'dp', perm).astype(F32)  29.5 us
    ppermute x12, waiting for transfers between devices, swap(): return lax.ppermute(value, axis, [(i, i ^ bits) for i in range(size)])  22.6 us
    psum x1, blocking collectives, body(): lax.psum((jnp.sum(values, axis=1), jnp.sum(values * values, axis=1)), 'mx')  20.7 us
    psum x1, blocking collectives, body(): lax.psum((jnp.sum(dcentred, axis=1), jnp.sum(dcentred * centred_rows, axi...  12.2 us
    dot_general x3, matrix products, dot(): return lax.dot_general(a, b, (dims, ((), ())), preferred_element_type=F32)  11.1 us
    ppermute x7, waiting for transfers between devices, hop(): return lax.ppermute(value.astype(BF), 'dp', perm).astype(F32)  4.31 us
  transfers between devices with their start and end apart: 20, of which 9 were waited for; matrix products, arithmetic and copies ran while one was open for 8% of the time, Pallas kernels for 2%

profile of v9, /device:TPU:1, one launch (start us, length us, event | category | flops | bytes accessed | tf_op | source)
XLA Modules:
  0.0 162.2 jit_solution(7442135516753800844)
XLA Ops:
  7.2 0.0 reduce-scatter.2.cloned.1.call-start
  7.2 1.5 convert_reduce_fusion
  8.7 20.7 %all-reduce.1 = (f32[256]{0:T(256)S(1)}, f32[256]{0:T(256)S(1)}) all-reduce(f32[256]{0:T(256)S(1)} %get-tuple-element.47, f32[256]{0:T(256)S(1)} %get-tuple-element.46), channel_id=1, replica_groups=mesh['dp'=32,'mx'=4,'my'=8] {'mx'}, use_global_device_ids=true, to_apply=%region_3.4 | all-reduce | flops 512 | bytes 4096 | tf_op jit(solution)/shard_map/psum | solution.py:86
  29.4 2.6 %fusion = (f32[256,1536]{1,0:T(8,128)}, bf16[256,1536]{1,0:T(8,128)(2,1)S(1)}) fusion(bf16[256,1536]{1,0:T(8,128)(2,1)} %param.4, f32[256]{0:T(256)S(1)} %get-tuple-element.63, f32[256]{0:T(256)S(1)} %get-tuple-element.62, f32[1536]{0:T(1024)} %param.5), kind=kLoop, calls=%fused_computation.12 | loop fusion | flops 1966080 | bytes 3153920 | tf_op jit(solution)/shard_map/mul | solution.py:89
  32.0 3.1 %convolution_convert_fusion = bf16[128,1536]{1,0:T(8,128)(2,1)S(1)} fusion(bf16[1536,1536]{1,0:T(8,128)(2,1)} %param.6, bf16[256,1536]{1,0:T(8,128)(2,1)S(1)} %get-tuple-element.55, s32[]{:T(128)S(6)} %select_n.65), kind=kOutput, calls=%fused_computation | convolution fusion | flops 604176384 | bytes 5505028 | tf_op jit(solution)/shard_map/dot_general | solution.py:29
  35.2 2.7 %collective-permute-start = (bf16[128,1536]{1,0:T(8,128)(2,1)S(1)}, bf16[128,1536]{1,0:T(8,128)(2,1)S(1)}, u32[]{:S(2)}, u32[]{:S(2)}) collective-permute-start(bf16[128,1536]{1,0:T(8,128)(2,1)S(1)} %convolution_convert_fusion), channel_id=1, source_target_pairs={{0,8},{8,0},{16,24},{24,16},{1,9},{9,1},{17,25},{25,17},{2,10},{10... | collective-permute-start | bytes 1179656 | tf_op jit(solution)/shard_map/ppermute | solution.py:21
  37.8 3.1 %fusion.17 = f32[128,1536]{1,0:T(8,128)S(1)} fusion(bf16[1536,1536]{1,0:T(8,128)(2,1)} %param.6, bf16[256,1536]{1,0:T(8,128)(2,1)S(1)} %get-tuple-element.55, s32[]{:T(128)S(6)} %select_n.64), kind=kOutput, calls=%fused_computation.36 | convolution fusion | flops 603979776 | bytes 5898244 | tf_op jit(solution)/shard_map/dot_general | solution.py:29
  41.0 0.1 dynamic-slice_bitcast_fusion.1
  41.0 0.0 collective-permute-done
  41.0 0.1 fusion.15
  41.1 1.9 %collective-permute-start.1 = (bf16[128,1536]{1,0:T(8,128)(2,1)S(1)}, bf16[128,1536]{1,0:T(8,128)(2,1)S(1)}, u32[]{:S(2)}, u32[]{:S(2)}) collective-permute-start(bf16[128,1536]{1,0:T(8,128)(2,1)S(1)} %fusion.15), channel_id=1, source_target_pairs={{0,16},{8,24},{16,0},{24,8},{1,17},{9,25},{17,1},{25,9},{2,18},{10... | collective-permute-start | bytes 1179656 | tf_op jit(solution)/shard_map/ppermute | solution.py:21
  43.0 0.1 pad_maximum_fusion
  43.2 0.3 copy.8
  43.5 0.0 copy-start.3
  43.5 1.0 fusion.19
  44.5 1.9 %collective-permute-start.3 = (bf16[384,256]{1,0:T(8,128)(2,1)S(1)}, bf16[384,256]{1,0:T(8,128)(2,1)S(1)}, u32[]{:S(2)}, u32[]{:S(2)}) collective-permute-start(bf16[384,256]{1,0:T(8,128)(2,1)S(1)} %bitcast.18), channel_id=1, source_target_pairs={{0,544},{32,512},{64,608},{96,576},{128,672},{160,640},{192,736},{... | collective-permute-start | bytes 589832 | tf_op jit(solution)/shard_map/ppermute | solution.py:21
  46.4 1.9 %collective-permute-start.2 = (bf16[384,256]{1,0:T(8,128)(2,1)S(1)}, bf16[384,256]{1,0:T(8,128)(2,1)S(1)}, u32[]{:S(2)}, u32[]{:S(2)}) collective-permute-start(bf16[384,256]{1,0:T(8,128)(2,1)S(1)} %bitcast.17), channel_id=1, source_target_pairs={{0,32},{32,0},{64,96},{96,64},{128,160},{160,128},{192,224},{224,1... | collective-permute-start | bytes 589832 | tf_op jit(solution)/shard_map/ppermute | solution.py:21
  48.3 5.3 %collective-permute-done.3.refs_3_ = bf16[384,256]{1,0:T(8,128)(2,1)S(1)} collective-permute-done((bf16[384,256]{1,0:T(8,128)(2,1)S(1)}, bf16[384,256]{1,0:T(8,128)(2,1)S(1)}, u32[]{:S(2)}, u32[]{:S(2)}) %collective-permute-start.3) | collective-permute-done | bytes 196640 | tf_op jit(solution)/shard_map/ppermute | solution.py:21
  53.6 1.4 collective-permute-done.2.refs_2_
  55.0 0.3 collective-permute-done.1
  55.3 0.5 fusion.7.refs_4_
  55.7 2.7 %collective-permute-start.4 = (bf16[128,1536]{1,0:T(8,128)(2,1)S(1)}, bf16[128,1536]{1,0:T(8,128)(2,1)S(1)}, u32[]{:S(2)}, u32[]{:S(2)}) collective-permute-start(bf16[128,1536]{1,0:T(8,128)(2,1)S(1)} %fusion.7.refs_4_), channel_id=1, source_target_pairs={{0,8},{8,0},{16,24},{24,16},{1,9},{9,1},{17,25},{25,17},{2,10},{10... | collective-permute-start | bytes 1179656 | tf_op jit(solution)/shard_map/ppermute | solution.py:21
  58.4 3.8 %collective-permute-start.6 = (bf16[128,1536]{1,0:T(8,128)(2,1)S(1)}, bf16[128,1536]{1,0:T(8,128)(2,1)S(1)}, u32[]{:S(2)}, u32[]{:S(2)}) collective-permute-start(bf16[128,1536]{1,0:T(8,128)(2,1)S(1)} %fusion.7.refs_4_), channel_id=1, source_target_pairs={{0,32},{32,0},{64,96},{96,64},{128,160},{160,128},{192,224},{224,1... | collective-permute-start | bytes 1179656 | tf_op jit(solution)/shard_map/ppermute | solution.py:21
  62.2 0.0 collective-permute-done.4.refs_5_
  62.2 4.3 %collective-permute-start.10 = (bf16[128,1536]{1,0:T(8,128)(2,1)S(1)}, bf16[128,1536]{1,0:T(8,128)(2,1)S(1)}, u32[]{:S(2)}, u32[]{:S(2)}) collective-permute-start(bf16[128,1536]{1,0:T(8,128)(2,1)S(1)} %fusion.7.refs_4_), channel_id=1, source_target_pairs={{0,544},{32,512},{64,608},{96,576},{128,672},{160,640},{192,736},{... | collective-permute-start | bytes 1179656 | tf_op jit(solution)/shard_map/ppermute | solution.py:21
  66.5 1.9 %collective-permute-start.7 = (bf16[128,1536]{1,0:T(8,128)(2,1)S(1)}, bf16[128,1536]{1,0:T(8,128)(2,1)S(1)}, u32[]{:S(2)}, u32[]{:S(2)}) collective-permute-start(bf16[128,1536]{1,0:T(8,128)(2,1)S(1)} %fusion.7.refs_4_), channel_id=1, source_target_pairs={{0,512},{32,544},{64,576},{96,608},{128,640},{160,672},{192,704},{... | collective-permute-start | bytes 1179656 | tf_op jit(solution)/shard_map/ppermute | solution.py:21
  68.4 3.4 %collective-permute-start.5 = (bf16[384,256]{1,0:T(8,128)(2,1)S(1)}, bf16[384,256]{1,0:T(8,128)(2,1)S(1)}, u32[]{:S(2)}, u32[]{:S(2)}) collective-permute-start(bf16[384,256]{1,0:T(8,128)(2,1)S(1)} %bitcast.16), channel_id=1, source_target_pairs={{0,512},{32,544},{64,576},{96,608},{128,640},{160,672},{192,704},{... | collective-permute-start | bytes 589832 | tf_op jit(solution)/shard_map/ppermute | solution.py:21
  71.8 4.9 %fusion.8 = f32[256,1536]{1,0:T(8,128)} fusion(bf16[1536,1536]{1,0:T(8,128)(2,1)} %param.6, bf16[128,1536]{1,0:T(8,128)(2,1)S(1)} %collective-permute-done.4.refs_5_, bf16[128,1536]{1,0:T(8,128)(2,1)S(1)} %fusion.7.refs_4_, pred[]{:T(512)S(6)} %eq.7), kind=kOutput, calls=%fused_computation.24 | convolution fusion | flops 1211498496 | bytes 7077889 | tf_op jit(solution)/shard_map/dot_general | solution.py:29
  76.7 5.6 %collective-permute-done.10.refs_10_ = bf16[128,1536]{1,0:T(8,128)(2,1)S(1)} collective-permute-done((bf16[128,1536]{1,0:T(8,128)(2,1)S(1)}, bf16[128,1536]{1,0:T(8,128)(2,1)S(1)}, u32[]{:S(2)}, u32[]{:S(2)}) %collective-permute-start.10) | collective-permute-done | bytes 393248 | tf_op jit(solution)/shard_map/ppermute | solution.py:21
  82.3 0.0 reduce-scatter.2.cloned.1.call-update
  82.3 0.0 collective-permute-done.6.refs_8_
  82.3 8.8 %collective-permute-done.5.refs_1_ = bf16[384,256]{1,0:T(8,128)(2,1)S(1)} collective-permute-done((bf16[384,256]{1,0:T(8,128)(2,1)S(1)}, bf16[384,256]{1,0:T(8,128)(2,1)S(1)}, u32[]{:S(2)}, u32[]{:S(2)}) %collective-permute-start.5) | collective-permute-done | bytes 196640 | tf_op jit(solution)/shard_map/ppermute | solution.py:21
  91.1 0.7 copy-done
  91.8 3.3 %collective-permute-start.9 = (bf16[128,1536]{1,0:T(8,128)(2,1)S(1)}, bf16[128,1536]{1,0:T(8,128)(2,1)S(1)}, u32[]{:S(2)}, u32[]{:S(2)}) collective-permute-start(bf16[128,1536]{1,0:T(8,128)(2,1)S(1)} %collective-permute-done.6.refs_8_), channel_id=1, source_target_pairs={{0,8},{8,0},{16,24},{24,16},{1,9},{9,1},{17,25},{25,17},{2,10},{10... | collective-permute-start | bytes 1179656 | tf_op jit(solution)/shard_map/ppermute | solution.py:21
  95.1 0.0 collective-permute-done.7.refs_6_
  95.1 1.9 %collective-permute-start.8 = (bf16[128,1536]{1,0:T(8,128)(2,1)S(1)}, bf16[128,1536]{1,0:T(8,128)(2,1)S(1)}, u32[]{:S(2)}, u32[]{:S(2)}) collective-permute-start(bf16[128,1536]{1,0:T(8,128)(2,1)S(1)} %collective-permute-done.7.refs_6_), channel_id=1, source_target_pairs={{0,8},{8,0},{16,24},{24,16},{1,9},{9,1},{17,25},{25,17},{2,10},{10... | collective-permute-start | bytes 1179656 | tf_op jit(solution)/shard_map/ppermute | solution.py:21
  97.1 2.4 %collective-permute-start.11 = (bf16[128,1536]{1,0:T(8,128)(2,1)S(1)}, bf16[128,1536]{1,0:T(8,128)(2,1)S(1)}, u32[]{:S(2)}, u32[]{:S(2)}) collective-permute-start(bf16[128,1536]{1,0:T(8,128)(2,1)S(1)} %collective-permute-done.10.refs_10_), channel_id=1, source_target_pairs={{0,8},{8,0},{16,24},{24,16},{1,9},{9,1},{17,25},{25,17},{2,10},{10... | collective-permute-start | bytes 1179656 | tf_op jit(solution)/shard_map/ppermute | solution.py:21
  99.5 0.0 collective-permute-done.9.refs_9_
  99.5 0.0 collective-permute-done.8.refs_7_
  99.5 1.3 collective-permute-done.11.refs_11_
  100.8 0.9 copy-done.1
  101.7 2.9 %shard_map.59 = (bf16[48,1536]{1,0:T(8,128)(2,1)S(1)}, bf16[48,1536]{1,0:T(8,128)(2,1)S(1)}, bf16[48,1536]{1,0:T(8,128)(2,1)S(1)}, bf16[48,1536]{1,0:T(8,128)(2,...) custom-call(bf16[384,256]{1,0:T(8,128)(2,1)S(1)} %bitcast.14, ...), custom_call_target="tpu_custom_call" | custom-call | flops 1207959552 | bytes 5111808 | tf_op jit(solution)/shard_map/pallas_call | solution.py:55
  104.6 0.6 copy-done.2
  105.3 2.0 %collective-permute-start.15 = (bf16[48,1536]{1,0:T(8,128)(2,1)}, bf16[48,1536]{1,0:T(8,128)(2,1)S(1)}, u32[]{:S(2)}, u32[]{:S(2)}) collective-permute-start(bf16[48,1536]{1,0:T(8,128)(2,1)} %get-tuple-element.39), channel_id=1, source_target_pairs={{0,64},{32,96},{64,128},{96,160},{128,192},{160,224},{192,256},{22... | collective-permute-start | bytes 442376 | tf_op jit(solution)/shard_map/ppermute | solution.py:138
  107.3 0.1 dynamic_slice.34
  107.4 9.4 %collective-permute-start.12 = (bf16[48,1536]{1,0:T(8,128)(2,1)}, bf16[48,1536]{1,0:T(8,128)(2,1)S(1)}, u32[]{:S(2)}, u32[]{:S(2)}) collective-permute-start(bf16[48,1536]{1,0:T(8,128)(2,1)} %copy-done.2), channel_id=1, source_target_pairs={{0,448},{32,480},{64,0},{96,32},{128,64},{160,96},{192,128},{224,1... | collective-permute-start | bytes 442376 | tf_op jit(solution)/shard_map/ppermute | solution.py:138
  116.8 2.2 %collective-permute-done.15 = bf16[48,1536]{1,0:T(8,128)(2,1)S(1)} collective-permute-done((bf16[48,1536]{1,0:T(8,128)(2,1)}, bf16[48,1536]{1,0:T(8,128)(2,1)S(1)}, u32[]{:S(2)}, u32[]{:S(2)}) %collective-permute-start.15) | collective-permute-done | bytes 147488 | tf_op jit(solution)/shard_map/ppermute | solution.py:138
  119.1 1.9 %collective-permute-start.16 = (bf16[48,1536]{1,0:T(8,128)(2,1)S(1)}, bf16[48,1536]{1,0:T(8,128)(2,1)S(1)}, u32[]{:S(2)}, u32[]{:S(2)}) collective-permute-start(bf16[48,1536]{1,0:T(8,128)(2,1)S(1)} %add_convert_fusion.2), channel_id=1, source_target_pairs={{0,64},{32,96},{64,128},{96,160},{128,192},{160,224},{192,256},{22... | collective-permute-start | bytes 442376 | tf_op jit(solution)/shard_map/ppermute | solution.py:138
  121.0 2.0 %collective-permute-done.12 = bf16[48,1536]{1,0:T(8,128)(2,1)S(1)} collective-permute-done((bf16[48,1536]{1,0:T(8,128)(2,1)}, bf16[48,1536]{1,0:T(8,128)(2,1)S(1)}, u32[]{:S(2)}, u32[]{:S(2)}) %collective-permute-start.12) | collective-permute-done | bytes 147488 | tf_op jit(solution)/shard_map/ppermute | solution.py:138
  123.0 6.3 %collective-permute-start.13 = (bf16[48,1536]{1,0:T(8,128)(2,1)S(1)}, bf16[48,1536]{1,0:T(8,128)(2,1)S(1)}, u32[]{:S(2)}, u32[]{:S(2)}) collective-permute-start(bf16[48,1536]{1,0:T(8,128)(2,1)S(1)} %add_convert_fusion.4), channel_id=1, source_target_pairs={{0,448},{32,480},{64,0},{96,32},{128,64},{160,96},{192,128},{224,1... | collective-permute-start | bytes 442376 | tf_op jit(solution)/shard_map/ppermute | solution.py:138
  129.3 0.0 collective-permute-done.16
  129.3 1.9 %collective-permute-start.17 = (bf16[48,1536]{1,0:T(8,128)(2,1)S(1)}, bf16[48,1536]{1,0:T(8,128)(2,1)S(1)}, u32[]{:S(2)}, u32[]{:S(2)}) collective-permute-start(bf16[48,1536]{1,0:T(8,128)(2,1)S(1)} %add_convert_fusion.1), channel_id=1, source_target_pairs={{0,64},{32,96},{64,128},{96,160},{128,192},{160,224},{192,256},{22... | collective-permute-start | bytes 442376 | tf_op jit(solution)/shard_map/ppermute | solution.py:138
  131.3 0.1 collective-permute-done.13
  131.4 6.0 %collective-permute-start.14 = (bf16[48,1536]{1,0:T(8,128)(2,1)S(1)}, bf16[48,1536]{1,0:T(8,128)(2,1)S(1)}, u32[]{:S(2)}, u32[]{:S(2)}) collective-permute-start(bf16[48,1536]{1,0:T(8,128)(2,1)S(1)} %add_convert_fusion.3), channel_id=1, source_target_pairs={{0,448},{32,480},{64,0},{96,32},{128,64},{160,96},{192,128},{224,1... | collective-permute-start | bytes 442376 | tf_op jit(solution)/shard_map/ppermute | solution.py:138
  137.4 0.0 collective-permute-done.17
  137.5 0.0 reduce-scatter.2.cloned.1.call-done
  137.5 1.9 %collective-permute-start.18 = (bf16[48,1536]{1,0:T(8,128)(2,1)S(1)}, bf16[48,1536]{1,0:T(8,128)(2,1)S(1)}, u32[]{:S(2)}, u32[]{:S(2)}) collective-permute-start(bf16[48,1536]{1,0:T(8,128)(2,1)S(1)} %convert_add_fusion.1), channel_id=1, source_target_pairs={{0,64},{32,96},{64,128},{96,160},{128,192},{160,224},{192,256},{22... | collective-permute-start | bytes 442376 | tf_op jit(solution)/shard_map/ppermute | solution.py:138
  139.4 0.0 copy-done.5
  139.4 1.2 multiply_reduce_fusion.1
  140.6 12.2 %all-reduce = (f32[32]{0:T(128)S(1)}, f32[32]{0:T(128)S(1)}) all-reduce(f32[32]{0:T(128)S(1)} %get-tuple-element.49, f32[32]{0:T(128)S(1)} %get-tuple-element.48), channel_id=1, replica_groups=mesh['dp'=32,'mx'=4,'my'=8] {'mx'}, use_global_device_ids=true, to_apply=%region_8.9 | all-reduce | flops 64 | bytes 512 | tf_op jit(solution)/shard_map/psum | solution.py:151
  152.8 1.8 %multiply_convert_fusion.1 = bf16[32,1536]{1,0:T(8,128)(2,1)} fusion(f32[256,1536]{1,0:T(8,128)} %get-tuple-element.54, s32[]{:T(128)S(6)} %select_n.77, f32[32,1536]{1,0:T(8,128)} %reduce-scatter.2.cloned.1.call-done, f32[32]{0:T(128)S(1)} %get-tuple-element.64, f32[32]{0:T(128)S(1)} %get-tuple-element.65, f32[1536]{0:T(1024)S(1)} %copy-done.5, ...), kind=kLoop, calls=%fused_computation.48 | loop fusion | flops 294912 | bytes 498052 | tf_op jit(solution)/shard_map/convert_element_type | solution.py:157
  154.6 0.0 collective-permute-done.14
  154.6 0.0 collective-permute-done.18
  154.6 0.7 fusion.23
  (14 shorter events, 0.2 us)
Async XLA Ops:
  7.2 130.3 %reduce-scatter.2.cloned.1.call-start = ((), (), s32[]{:S(2)}) async-start(), calls=%async_computation.1 | async-start | bytes 1769472 | tf_op jit(solution)/shard_map/reduce_scatter | solution.py:129
  35.2 5.9 %collective-permute-start = (bf16[128,1536]{1,0:T(8,128)(2,1)S(1)}, bf16[128,1536]{1,0:T(8,128)(2,1)S(1)}, u32[]{:S(2)}, u32[]{:S(2)}) collective-permute-start(bf16[128,1536]{1,0:T(8,128)(2,1)S(1)} %convolution_convert_fusion), channel_id=1, source_target_pairs={{0,8},{8,0},{16,24},{24,16},{1,9},{9,1},{17,25},{25,17},{2,10},{10... | collective-permute-start | bytes 1179656 | tf_op jit(solution)/shard_map/ppermute | solution.py:21
  41.1 14.1 %collective-permute-start.1 = (bf16[128,1536]{1,0:T(8,128)(2,1)S(1)}, bf16[128,1536]{1,0:T(8,128)(2,1)S(1)}, u32[]{:S(2)}, u32[]{:S(2)}) collective-permute-start(bf16[128,1536]{1,0:T(8,128)(2,1)S(1)} %fusion.15), channel_id=1, source_target_pairs={{0,16},{8,24},{16,0},{24,8},{1,17},{9,25},{17,1},{25,9},{2,18},{10... | collective-permute-start | bytes 1179656 | tf_op jit(solution)/shard_map/ppermute | solution.py:21
  43.5 11.8 %copy-start.3 = (bf16[256,1536]{1,0:T(8,128)(2,1)S(1)}, bf16[256,1536]{1,0:T(8,128)(2,1)}, u32[]{:S(2)}) copy-start(bf16[256,1536]{1,0:T(8,128)(2,1)} %param.7) | copy-start | bytes 2359300
  44.5 9.1 %collective-permute-start.3 = (bf16[384,256]{1,0:T(8,128)(2,1)S(1)}, bf16[384,256]{1,0:T(8,128)(2,1)S(1)}, u32[]{:S(2)}, u32[]{:S(2)}) collective-permute-start(bf16[384,256]{1,0:T(8,128)(2,1)S(1)} %bitcast.18), channel_id=1, source_target_pairs={{0,544},{32,512},{64,608},{96,576},{128,672},{160,640},{192,736},{... | collective-permute-start | bytes 589832 | tf_op jit(solution)/shard_map/ppermute | solution.py:21
  46.4 8.6 %collective-permute-start.2 = (bf16[384,256]{1,0:T(8,128)(2,1)S(1)}, bf16[384,256]{1,0:T(8,128)(2,1)S(1)}, u32[]{:S(2)}, u32[]{:S(2)}) collective-permute-start(bf16[384,256]{1,0:T(8,128)(2,1)S(1)} %bitcast.17), channel_id=1, source_target_pairs={{0,32},{32,0},{64,96},{96,64},{128,160},{160,128},{192,224},{224,1... | collective-permute-start | bytes 589832 | tf_op jit(solution)/shard_map/ppermute | solution.py:21
  55.2 13.2 %copy-start.4 = (bf16[1,8,1,48,256]{4,3,2,1,0:T(8,128)(2,1)S(1)}, bf16[1,8,1,48,256]{4,3,2,1,0:T(8,128)(2,1)}, u32[]{:S(2)}) copy-start(bf16[1,8,1,48,256]{4,3,2,1,0:T(8,128)(2,1)} %get-tuple-element.59) | copy-start | bytes 589828
  55.7 6.5 %collective-permute-start.4 = (bf16[128,1536]{1,0:T(8,128)(2,1)S(1)}, bf16[128,1536]{1,0:T(8,128)(2,1)S(1)}, u32[]{:S(2)}, u32[]{:S(2)}) collective-permute-start(bf16[128,1536]{1,0:T(8,128)(2,1)S(1)} %fusion.7.refs_4_), channel_id=1, source_target_pairs={{0,8},{8,0},{16,24},{24,16},{1,9},{9,1},{17,25},{25,17},{2,10},{10... | collective-permute-start | bytes 1179656 | tf_op jit(solution)/shard_map/ppermute | solution.py:21
  58.4 23.9 %collective-permute-start.6 = (bf16[128,1536]{1,0:T(8,128)(2,1)S(1)}, bf16[128,1536]{1,0:T(8,128)(2,1)S(1)}, u32[]{:S(2)}, u32[]{:S(2)}) collective-permute-start(bf16[128,1536]{1,0:T(8,128)(2,1)S(1)} %fusion.7.refs_4_), channel_id=1, source_target_pairs={{0,32},{32,0},{64,96},{96,64},{128,160},{160,128},{192,224},{224,1... | collective-permute-start | bytes 1179656 | tf_op jit(solution)/shard_map/ppermute | solution.py:21
  62.2 20.1 %collective-permute-start.10 = (bf16[128,1536]{1,0:T(8,128)(2,1)S(1)}, bf16[128,1536]{1,0:T(8,128)(2,1)S(1)}, u32[]{:S(2)}, u32[]{:S(2)}) collective-permute-start(bf16[128,1536]{1,0:T(8,128)(2,1)S(1)} %fusion.7.refs_4_), channel_id=1, source_target_pairs={{0,544},{32,512},{64,608},{96,576},{128,672},{160,640},{192,736},{... | collective-permute-start | bytes 1179656 | tf_op jit(solution)/shard_map/ppermute | solution.py:21
  66.5 28.6 %collective-permute-start.7 = (bf16[128,1536]{1,0:T(8,128)(2,1)S(1)}, bf16[128,1536]{1,0:T(8,128)(2,1)S(1)}, u32[]{:S(2)}, u32[]{:S(2)}) collective-permute-start(bf16[128,1536]{1,0:T(8,128)(2,1)S(1)} %fusion.7.refs_4_), channel_id=1, source_target_pairs={{0,512},{32,544},{64,576},{96,608},{128,640},{160,672},{192,704},{... | collective-permute-start | bytes 1179656 | tf_op jit(solution)/shard_map/ppermute | solution.py:21
  68.4 22.7 %collective-permute-start.5 = (bf16[384,256]{1,0:T(8,128)(2,1)S(1)}, bf16[384,256]{1,0:T(8,128)(2,1)S(1)}, u32[]{:S(2)}, u32[]{:S(2)}) collective-permute-start(bf16[384,256]{1,0:T(8,128)(2,1)S(1)} %bitcast.16), channel_id=1, source_target_pairs={{0,512},{32,544},{64,576},{96,608},{128,640},{160,672},{192,704},{... | collective-permute-start | bytes 589832 | tf_op jit(solution)/shard_map/ppermute | solution.py:21
  91.1 0.7 copy-start
  91.8 7.7 %collective-permute-start.9 = (bf16[128,1536]{1,0:T(8,128)(2,1)S(1)}, bf16[128,1536]{1,0:T(8,128)(2,1)S(1)}, u32[]{:S(2)}, u32[]{:S(2)}) collective-permute-start(bf16[128,1536]{1,0:T(8,128)(2,1)S(1)} %collective-permute-done.6.refs_8_), channel_id=1, source_target_pairs={{0,8},{8,0},{16,24},{24,16},{1,9},{9,1},{17,25},{25,17},{2,10},{10... | collective-permute-start | bytes 1179656 | tf_op jit(solution)/shard_map/ppermute | solution.py:21
  95.1 4.4 %collective-permute-start.8 = (bf16[128,1536]{1,0:T(8,128)(2,1)S(1)}, bf16[128,1536]{1,0:T(8,128)(2,1)S(1)}, u32[]{:S(2)}, u32[]{:S(2)}) collective-permute-start(bf16[128,1536]{1,0:T(8,128)(2,1)S(1)} %collective-permute-done.7.refs_6_), channel_id=1, source_target_pairs={{0,8},{8,0},{16,24},{24,16},{1,9},{9,1},{17,25},{25,17},{2,10},{10... | collective-permute-start | bytes 1179656 | tf_op jit(solution)/shard_map/ppermute | solution.py:21
  97.1 3.7 %collective-permute-start.11 = (bf16[128,1536]{1,0:T(8,128)(2,1)S(1)}, bf16[128,1536]{1,0:T(8,128)(2,1)S(1)}, u32[]{:S(2)}, u32[]{:S(2)}) collective-permute-start(bf16[128,1536]{1,0:T(8,128)(2,1)S(1)} %collective-permute-done.10.refs_10_), channel_id=1, source_target_pairs={{0,8},{8,0},{16,24},{24,16},{1,9},{9,1},{17,25},{25,17},{2,10},{10... | collective-permute-start | bytes 1179656 | tf_op jit(solution)/shard_map/ppermute | solution.py:21
  100.8 0.9 copy-start.1
  104.6 0.6 copy-start.2
  105.3 34.2 %copy-start.5 = (f32[1536]{0:T(1024)S(1)}, f32[1536]{0:T(1024)}, u32[]{:S(2)}) copy-start(f32[1536]{0:T(1024)} %param.5) | copy-start | bytes 18436
  105.3 13.8 %collective-permute-start.15 = (bf16[48,1536]{1,0:T(8,128)(2,1)}, bf16[48,1536]{1,0:T(8,128)(2,1)S(1)}, u32[]{:S(2)}, u32[]{:S(2)}) collective-permute-start(bf16[48,1536]{1,0:T(8,128)(2,1)} %get-tuple-element.39), channel_id=1, source_target_pairs={{0,64},{32,96},{64,128},{96,160},{128,192},{160,224},{192,256},{22... | collective-permute-start | bytes 442376 | tf_op jit(solution)/shard_map/ppermute | solution.py:138
  107.4 15.6 %collective-permute-start.12 = (bf16[48,1536]{1,0:T(8,128)(2,1)}, bf16[48,1536]{1,0:T(8,128)(2,1)S(1)}, u32[]{:S(2)}, u32[]{:S(2)}) collective-permute-start(bf16[48,1536]{1,0:T(8,128)(2,1)} %copy-done.2), channel_id=1, source_target_pairs={{0,448},{32,480},{64,0},{96,32},{128,64},{160,96},{192,128},{224,1... | collective-permute-start | bytes 442376 | tf_op jit(solution)/shard_map/ppermute | solution.py:138
  119.1 10.2 %collective-permute-start.16 = (bf16[48,1536]{1,0:T(8,128)(2,1)S(1)}, bf16[48,1536]{1,0:T(8,128)(2,1)S(1)}, u32[]{:S(2)}, u32[]{:S(2)}) collective-permute-start(bf16[48,1536]{1,0:T(8,128)(2,1)S(1)} %add_convert_fusion.2), channel_id=1, source_target_pairs={{0,64},{32,96},{64,128},{96,160},{128,192},{160,224},{192,256},{22... | collective-permute-start | bytes 442376 | tf_op jit(solution)/shard_map/ppermute | solution.py:138
  123.0 8.3 %collective-permute-start.13 = (bf16[48,1536]{1,0:T(8,128)(2,1)S(1)}, bf16[48,1536]{1,0:T(8,128)(2,1)S(1)}, u32[]{:S(2)}, u32[]{:S(2)}) collective-permute-start(bf16[48,1536]{1,0:T(8,128)(2,1)S(1)} %add_convert_fusion.4), channel_id=1, source_target_pairs={{0,448},{32,480},{64,0},{96,32},{128,64},{160,96},{192,128},{224,1... | collective-permute-start | bytes 442376 | tf_op jit(solution)/shard_map/ppermute | solution.py:138
  129.3 8.1 %collective-permute-start.17 = (bf16[48,1536]{1,0:T(8,128)(2,1)S(1)}, bf16[48,1536]{1,0:T(8,128)(2,1)S(1)}, u32[]{:S(2)}, u32[]{:S(2)}) collective-permute-start(bf16[48,1536]{1,0:T(8,128)(2,1)S(1)} %add_convert_fusion.1), channel_id=1, source_target_pairs={{0,64},{32,96},{64,128},{96,160},{128,192},{160,224},{192,256},{22... | collective-permute-start | bytes 442376 | tf_op jit(solution)/shard_map/ppermute | solution.py:138
  131.4 23.2 %collective-permute-start.14 = (bf16[48,1536]{1,0:T(8,128)(2,1)S(1)}, bf16[48,1536]{1,0:T(8,128)(2,1)S(1)}, u32[]{:S(2)}, u32[]{:S(2)}) collective-permute-start(bf16[48,1536]{1,0:T(8,128)(2,1)S(1)} %add_convert_fusion.3), channel_id=1, source_target_pairs={{0,448},{32,480},{64,0},{96,32},{128,64},{160,96},{192,128},{224,1... | collective-permute-start | bytes 442376 | tf_op jit(solution)/shard_map/ppermute | solution.py:138
  137.5 17.1 %collective-permute-start.18 = (bf16[48,1536]{1,0:T(8,128)(2,1)S(1)}, bf16[48,1536]{1,0:T(8,128)(2,1)S(1)}, u32[]{:S(2)}, u32[]{:S(2)}) collective-permute-start(bf16[48,1536]{1,0:T(8,128)(2,1)S(1)} %convert_add_fusion.1), channel_id=1, source_target_pairs={{0,64},{32,96},{64,128},{96,160},{128,192},{160,224},{192,256},{22... | collective-permute-start | bytes 442376 | tf_op jit(solution)/shard_map/ppermute | solution.py:138
Sparse Core Ops, SparseCore 0:
  82.4 42.9 reduce-scatter.1
